TPU v7x, 32 devices: a whole 2x2x4 slice. The times are simulated.
32 devices in a mesh: seq: 8 (over z, y), wshard: 4 (over x, core).
Axes of the slice: x: 2, y: 2, z: 4, core: 2. Of those that a mesh axis runs over, the one named last changes fastest.
Arguments:
- inputs: bfloat16 [4, 8192, 768], P('wshard', 'seq'), may hold values from -6 to 6
- gain_attn: bfloat16 [768], P('wshard'), may hold values from 0.5 to 1.5
- w_qkv: bfloat16 [768, 2304], P('wshard'), may hold values from -0.21875 to 0.21875
- w_out: bfloat16 [768, 768], P('wshard'), may hold values from -1.25 to 1.25
- gain_mlp: bfloat16 [768], P('wshard'), may hold values from 0.5 to 1.5
- w_in: bfloat16 [768, 2304], P('wshard'), may hold values from -0.21875 to 0.21875
- w_down: bfloat16 [1152, 768], P('wshard'), may hold values from -0.1875 to 0.1875
- bounds: int32 [4, 2], P('wshard'), may hold values from 1 to 8191, as said below
- grad_out: bfloat16 [4, 8192, 768], P('wshard', 'seq'), may hold values from -6 to 6
Outputs:
- output: bfloat16 [4, 8192, 768], P('wshard', 'seq')
- input_grad: bfloat16 [4, 8192, 768], P('wshard', 'seq')
- gain_attn_grad: float32 [768], P('wshard')
- w_qkv_grad: float32 [768, 2304], P('wshard')
- w_out_grad: float32 [768, 768], P('wshard')
- gain_mlp_grad: float32 [768], P('wshard')
- w_in_grad: float32 [768, 2304], P('wshard')
- w_down_grad: float32 [1152, 768], P('wshard')
Inputs may be any that keep to these rules, and one draw needn't show every extreme that they name: `bounds`: each sequence packs three documents: the second begins within its first 1024 tokens (column 0) and the third within its last 1024 tokens (column 1).
All inputs are finite; a program needn't handle non-finite values.
Results may differ from a plain program's by a relative error of at most 0.02.
Values may be sent and summed in bfloat16 or wider, within the bound.
A program may use at most 192 MiB of HBM per device.

v0:
```python
import math

import jax
import jax.numpy as jnp
from jax import lax
from jax.sharding import PartitionSpec as P

HD = 64
HALF = 64


rope_base = 10000.0


def extended_2(shard, sides, width):
    for axis, dim in sides:
        size, length = (lax.axis_size(axis), shard.shape[dim])
        up = [(i, (i + 1) % size) for i in range(size - 1)]
        down = [(j, i) for i, j in up]
        last = lax.slice_in_dim(shard, length - width, length, axis=dim)
        leading = lax.slice_in_dim(shard, 0, width, axis=dim)
        before = lax.ppermute(last, axis, up)
        after = lax.ppermute(leading, axis, down)
        shard = jnp.concatenate([before, shard, after], axis=dim)
    return shard


def from_behind(shard, axis, by):
    size = lax.axis_size(axis)
    pairs = [(i, i + by) for i in range(size) if 0 <= i + by < size]
    return lax.ppermute(shard, axis, pairs)


def layer_norm(stream, gain):
    centred = stream - jnp.mean(stream, axis=-1, keepdims=True)
    spread = jnp.mean(centred * centred, axis=-1, keepdims=True)
    return centred * lax.rsqrt(spread + 1e-05) * gain


def gated_act(lifted):
    hidden_width = lifted.shape[1] // 2
    return jax.nn.gelu(lifted[:, :hidden_width], approximate=False) * lifted[:, hidden_width:]


def rope_tables(positions, head_dim):
    frequency = rope_base ** (-(jnp.arange(head_dim // 2, dtype=jnp.float32) * 2.0) / head_dim)
    angles = positions[:, None] * frequency[None, :]
    return (jnp.cos(angles)[:, None, :], jnp.sin(angles)[:, None, :])


def rotate(tensor, cosine, sine_table, direction):
    half_dim = tensor.shape[-1] // 2
    upper_half = tensor[..., :half_dim]
    lower_half = tensor[..., half_dim:]
    turned = direction * sine_table
    return jnp.concatenate(
        [upper_half * cosine - lower_half * turned, lower_half * cosine + upper_half * turned],
        axis=-1,
    )


def key_mask(query_pos, key_pos, cut_first, cut_last, length):

    def segment(where_at):
        return (where_at >= cut_first).astype(jnp.int32) + (where_at >= cut_last).astype(jnp.int32)

    nearby = jnp.abs(query_pos[:, None] - key_pos[None, :]) <= HALF
    inside = (key_pos >= 0) & (key_pos < length)
    return nearby & inside[None, :] & (segment(query_pos)[:, None] == segment(key_pos)[None, :])


def local(inputs, gain_attn, w_qkv, w_out, gain_mlp, w_in, w_down, bounds, grad_out):
    tokens_dev = inputs.shape[1]
    model_width = inputs.shape[2]
    head_count = model_width // HD
    length = tokens_dev * lax.axis_size("seq")
    offset = lax.axis_index("seq") * tokens_dev
    cut_first = bounds[0, 0]
    cut_last = bounds[0, 1]
    scale_factor = 1.0 / math.sqrt(HD)
    block_rows = math.gcd(tokens_dev, 512)
    key_rows = block_rows + 2 * HALF
    blocks = tokens_dev // block_rows
    gathered = (
        lax.all_gather(gain_attn, "wshard", axis=0, tiled=True),
        lax.all_gather(w_qkv, "wshard", axis=0, tiled=True),
        lax.all_gather(w_out, "wshard", axis=0, tiled=True),
        lax.all_gather(gain_mlp, "wshard", axis=0, tiled=True),
        lax.all_gather(w_in, "wshard", axis=0, tiled=True),
        lax.all_gather(w_down, "wshard", axis=0, tiled=True),
    )
    gain_a = gathered[0].astype(jnp.float32)
    gain_m = gathered[3].astype(jnp.float32)
    stream = inputs[0].astype(jnp.float32)
    normed, norm_back_a = jax.vjp(layer_norm, stream, gain_a)
    normed_low = normed.astype(jnp.bfloat16)
    projected = jnp.dot(normed_low, gathered[1], preferred_element_type=jnp.float32)
    positions = (offset + jnp.arange(tokens_dev, dtype=jnp.int32)).astype(jnp.float32)
    cosine, sine_table = rope_tables(positions, HD)
    query = rotate(
        projected[:, :model_width].reshape(tokens_dev, head_count, HD), cosine, sine_table, 1.0
    ).astype(jnp.bfloat16)
    key_rot = rotate(
        projected[:, model_width : 2 * model_width].reshape(tokens_dev, head_count, HD),
        cosine,
        sine_table,
        1.0,
    )
    key_rot = key_rot.reshape(tokens_dev, model_width).astype(jnp.bfloat16)
    values = projected[:, 2 * model_width :].astype(jnp.bfloat16)
    extended = extended_2(jnp.concatenate([key_rot, values], axis=1), (("seq", 0),), HALF)
    key_ext = extended[:, :model_width].reshape(-1, head_count, HD)
    value_ext = extended[:, model_width:].reshape(-1, head_count, HD)
    query_pos_all = offset + jnp.arange(tokens_dev, dtype=jnp.int32)
    key_pos_all = offset - HALF + jnp.arange(tokens_dev + 2 * HALF, dtype=jnp.int32)

    def block_parts(number):
        rows = number * block_rows
        allowed = key_mask(
            query_pos_all[rows : rows + block_rows],
            key_pos_all[rows : rows + key_rows],
            cut_first,
            cut_last,
            length,
        )
        return (
            query[rows : rows + block_rows],
            key_ext[rows : rows + key_rows],
            value_ext[rows : rows + key_rows],
            allowed,
        )

    def block_scores(query_block, key_block, allowed):
        scores = (
            jnp.einsum("qhd,khd->hqk", query_block, key_block, preferred_element_type=jnp.float32)
            * scale_factor
        )
        return jnp.where(allowed[None], scores, -1e30)

    attended_parts = []
    lse_parts = []
    for number in range(blocks):
        query_block, key_block, value_block, allowed = block_parts(number)
        scores = block_scores(query_block, key_block, allowed)
        top_score = jnp.max(scores, axis=-1, keepdims=True)
        expo = jnp.exp(scores - top_score)
        row_total = jnp.sum(expo, axis=-1, keepdims=True)
        probs = (expo / row_total).astype(jnp.bfloat16)
        attended_parts.append(
            jnp.einsum("hqk,khd->qhd", probs, value_block, preferred_element_type=jnp.float32)
        )
        lse_parts.append(top_score + jnp.log(row_total))
    attended = (
        jnp.concatenate(attended_parts, axis=0)
        .reshape(tokens_dev, model_width)
        .astype(jnp.bfloat16)
    )
    middle = stream + jnp.dot(attended, gathered[2], preferred_element_type=jnp.float32)
    normed2, norm_back_m = jax.vjp(layer_norm, middle, gain_m)
    normed2_low = normed2.astype(jnp.bfloat16)
    lifted = jnp.dot(normed2_low, gathered[4], preferred_element_type=jnp.float32)
    hidden_f, gated_back = jax.vjp(gated_act, lifted)
    hidden = hidden_f.astype(jnp.bfloat16)
    result = middle + jnp.dot(hidden, gathered[5], preferred_element_type=jnp.float32)
    output = result.astype(jnp.bfloat16)[None]
    backward_weights = (
        lax.all_gather(gain_attn, "wshard", axis=0, tiled=True),
        lax.all_gather(w_qkv, "wshard", axis=0, tiled=True),
        lax.all_gather(w_out, "wshard", axis=0, tiled=True),
        lax.all_gather(gain_mlp, "wshard", axis=0, tiled=True),
        lax.all_gather(w_in, "wshard", axis=0, tiled=True),
        lax.all_gather(w_down, "wshard", axis=0, tiled=True),
    )
    weight_qkv_b = backward_weights[1]
    weight_out_b = backward_weights[2]
    weight_in_b = backward_weights[4]
    weight_down_b = backward_weights[5]
    upstream = grad_out[0].astype(jnp.float32)
    down_grad_low = grad_out[0]
    grad_w_down = jnp.einsum("tf,td->fd", hidden, down_grad_low, preferred_element_type=jnp.float32)
    grad_hidden = jnp.einsum(
        "td,fd->tf", down_grad_low, weight_down_b, preferred_element_type=jnp.float32
    )
    grad_lifted = gated_back(grad_hidden)[0].astype(jnp.bfloat16)
    grad_w_in = jnp.einsum(
        "td,tf->df", normed2_low, grad_lifted, preferred_element_type=jnp.float32
    )
    grad_normed2 = jnp.einsum(
        "tf,df->td", grad_lifted, weight_in_b, preferred_element_type=jnp.float32
    )
    grad_mid_norm, grad_gain_m = norm_back_m(grad_normed2)
    grad_middle = upstream + grad_mid_norm
    branch_grad_low = grad_middle.astype(jnp.bfloat16)
    grad_w_out = jnp.einsum(
        "td,te->de", attended, branch_grad_low, preferred_element_type=jnp.float32
    )
    grad_attended = jnp.einsum(
        "te,de->td", branch_grad_low, weight_out_b, preferred_element_type=jnp.float32
    )
    grad_attended = grad_attended.astype(jnp.bfloat16).reshape(tokens_dev, head_count, HD)
    kv_grad = jnp.zeros((tokens_dev + 2 * HALF, 2 * model_width), jnp.float32)
    query_grads = []
    for number in range(blocks):
        rows = number * block_rows
        query_block, key_block, value_block, allowed = block_parts(number)
        attended_grad_block = grad_attended[rows : rows + block_rows]
        scores = block_scores(query_block, key_block, allowed)
        probs = jnp.exp(scores - lse_parts[number])
        prob_grad = jnp.einsum(
            "qhd,khd->hqk", attended_grad_block, value_block, preferred_element_type=jnp.float32
        )
        centre = jnp.sum(probs * prob_grad, axis=-1, keepdims=True)
        score_grad = (probs * (prob_grad - centre)).astype(jnp.bfloat16)
        query_grads.append(
            jnp.einsum("hqk,khd->qhd", score_grad, key_block, preferred_element_type=jnp.float32)
            * scale_factor
        )
        key_part = (
            jnp.einsum("hqk,qhd->khd", score_grad, query_block, preferred_element_type=jnp.float32)
            * scale_factor
        )
        value_part = jnp.einsum(
            "hqk,qhd->khd",
            probs.astype(jnp.bfloat16),
            attended_grad_block,
            preferred_element_type=jnp.float32,
        )
        joined = jnp.concatenate(
            [key_part.reshape(key_rows, model_width), value_part.reshape(key_rows, model_width)],
            axis=1,
        )
        kv_grad = kv_grad.at[rows : rows + key_rows].add(joined)
    from_next = from_behind(kv_grad[:HALF].astype(jnp.bfloat16), "seq", -1).astype(jnp.float32)
    from_prev = from_behind(kv_grad[tokens_dev + HALF :].astype(jnp.bfloat16), "seq", 1).astype(
        jnp.float32
    )
    own_grad = kv_grad[HALF : HALF + tokens_dev]
    own_grad = own_grad.at[:HALF].add(from_prev)
    own_grad = own_grad.at[tokens_dev - HALF :].add(from_next)
    key_grad_low = own_grad[:, :model_width].astype(jnp.bfloat16)
    value_grad_low = own_grad[:, model_width:].astype(jnp.bfloat16)
    key_raw_grad = rotate(
        key_grad_low.astype(jnp.float32).reshape(tokens_dev, head_count, HD),
        cosine,
        sine_table,
        -1.0,
    )
    key_raw_grad = key_raw_grad.reshape(tokens_dev, model_width).astype(jnp.bfloat16)
    query_grad_low = jnp.concatenate(query_grads, axis=0).astype(jnp.bfloat16)
    query_raw_grad = rotate(query_grad_low.astype(jnp.float32), cosine, sine_table, -1.0)
    query_raw_grad = query_raw_grad.reshape(tokens_dev, model_width).astype(jnp.bfloat16)
    grad_projected = jnp.concatenate([query_raw_grad, key_raw_grad, value_grad_low], axis=1)
    grad_w_qkv = jnp.einsum(
        "td,te->de", normed_low, grad_projected, preferred_element_type=jnp.float32
    )
    grad_normed = jnp.einsum(
        "te,de->td", grad_projected, weight_qkv_b, preferred_element_type=jnp.float32
    )
    grad_stream_norm, grad_gain_a = norm_back_a(grad_normed)
    input_grad = (grad_middle + grad_stream_norm).astype(jnp.bfloat16)[None]
    terms = (grad_gain_a, grad_w_qkv, grad_w_out, grad_gain_m, grad_w_in, grad_w_down)
    shares = (
        lax.psum_scatter(
            terms[0].astype(jnp.bfloat16), "wshard", scatter_dimension=0, tiled=True
        ).astype(jnp.float32),
        lax.psum_scatter(
            terms[1].astype(jnp.bfloat16), "wshard", scatter_dimension=0, tiled=True
        ).astype(jnp.float32),
        lax.psum_scatter(
            terms[2].astype(jnp.bfloat16), "wshard", scatter_dimension=0, tiled=True
        ).astype(jnp.float32),
        lax.psum_scatter(
            terms[3].astype(jnp.bfloat16), "wshard", scatter_dimension=0, tiled=True
        ).astype(jnp.float32),
        lax.psum_scatter(
            terms[4].astype(jnp.bfloat16), "wshard", scatter_dimension=0, tiled=True
        ).astype(jnp.float32),
        lax.psum_scatter(
            terms[5].astype(jnp.bfloat16), "wshard", scatter_dimension=0, tiled=True
        ).astype(jnp.float32),
    )
    totals = lax.psum((shares[0], shares[1], shares[2], shares[3], shares[4], shares[5]), "seq")
    return (output, input_grad, totals[0], totals[1], totals[2], totals[3], totals[4], totals[5])


def solution(mesh):
    return jax.shard_map(
        local,
        mesh=mesh,
        in_specs=(
            P("wshard", "seq", None),
            P("wshard"),
            P("wshard", None),
            P("wshard", None),
            P("wshard"),
            P("wshard", None),
            P("wshard", None),
            P("wshard", None),
            P("wshard", "seq", None),
        ),
        out_specs=(
            P("wshard", "seq", None),
            P("wshard", "seq", None),
            P("wshard"),
            P("wshard", None),
            P("wshard", None),
            P("wshard"),
            P("wshard", None),
            P("wshard", None),
        ),
        check_vma=False,
    )
```

profile of v0, /device:TPU:0, one launch (start us, length us, event | category | flops | bytes accessed | tf_op | source)
XLA Modules:
  0.0 569.1 jit_solution(7392073452328503224)
XLA Ops:
  15.1 8.3 %all-reduce.9 = (bf16[768]{0:T(1024)(128)(2,1)S(1)}, bf16[768]{0:T(1024)(128)(2,1)S(1)}) all-reduce(bf16[768]{0:T(1024)(128)(2,1)S(1)} %dynamic-update-slice.12, bf16[768]{0:T(1024)(128)(2,1)S(1)} %dynamic-update-slice.13), channel_id=1, replica_groups=mesh['seq'=8,'wshard'=4] {'wshard'}, use_global_device_ids=true, to_apply=%add.3 | all-reduce | flops 1536 | bytes 6144
  32.3 10.9 %all-gather.5.cloned.1.call-done = bf16[768,2304]{1,0:T(8,128)(2,1)} async-done(((bf16[192,2304]{1,0:T(8,128)(2,1)}), bf16[768,2304]{1,0:T(8,128)(2,1)}) %all-gather.5.cloned.1.call-update) | async-done | bytes 3538960 | tf_op jit(solution)/shard_map/all_gather | solution.py:86
  43.1 6.2 %fusion.53 = f32[1024,2304]{1,0:T(8,128)S(1)} fusion(bf16[768,2304]{1,0:T(8,128)(2,1)} %all-gather.5.cloned.1.call-done, bf16[1,1024,768]{1,2,0:T(8,128)(2,1)S(1)} %copy.47, f32[768]{0:T(1024)S(1)} %convert_element_type.167, f32[1024]{0:T(1024)S(1)} %fusion.55, f32[1024]{0:T(1024)S(1)} %broadcast_multiply_fusion.2), kind=kOutput, calls=%fused_computation.128 | convolution fusion | flops 3627810816 | bytes 14560256 | tf_op jit(solution)/shard_map/dot_general | solution.py:97
  50.6 3.2 fusion.69
  53.8 3.5 copy.51
  57.3 3.6 copy.48
  60.9 3.9 subtract_convert_fusion.2
  70.1 3.5 collective-permute-start
  78.2 4.1 collective-permute-done.1
  82.3 3.4 pad_maximum_fusion.10
  94.7 4.5 fusion.75
  99.2 3.4 fusion.1
  102.6 2.7 copy-done
  105.4 5.1 fusion.48
  110.5 3.3 fusion.76
  113.8 3.4 fusion
  119.3 5.5 fusion.47
  126.2 3.3 fusion.77
  131.7 10.6 %fusion.66 = f32[1024,2304]{1,0:T(8,128)} fusion(bf16[768,2304]{1,0:T(8,128)(2,1)} %all-gather.9.cloned.1.call-done, f32[1024,768]{0,1:T(8,128)} %copy-done.14, f32[768]{0:T(1024)S(1)} %convert_element_type.182, f32[1024]{0:T(1024)S(1)} %fusion.56, f32[1024]{0:T(1024)S(1)} %broadcast_multiply_fusion.1), kind=kOutput, calls=%fused_computation.165 | convolution fusion | flops 3627024384 | bytes 16133120 | tf_op jit(solution)/shard_map/dot_general | solution.py:161
  142.2 14.9 %fusion.37 = (f32[1024,1152]{1,0:T(8,128)}, f32[1024,1152]{1,0:T(8,128)S(1)}, f32[1024,1152]{1,0:T(8,128)S(1)}) fusion(f32[1024,2304]{1,0:T(8,128)} %fusion.66, bf16[1152,768]{1,0:T(8,128)(2,1)} %all-gather.11.cloned.1.call-done, bf16[1,1024,768]{2,1,0:T(8,128)(2,1)S(1)} %copy-done.28), kind=kOutput, calls=%fused_computation.100 | convolution fusion | flops 1888616448 | bytes 22216704 | tf_op jit(solution)/shard_map/td,fd->tf/dot_general | solution.py:181
  157.1 3.5 multiply_add_fusion
  160.7 9.6 %multiply_reduce_fusion.2 = (bf16[768]{0:T(1024)(128)(2,1)}, f32[1024]{0:T(1024)S(1)}, f32[1024,768]{0,1:T(8,128)S(1)}) fusion(f32[1024,768]{0,1:T(8,128)S(1)} %copy-done.15, f32[1024]{0:T(1024)S(1)} %fusion.56, f32[1024]{0:T(1024)S(1)} %broadcast_multiply_fusion.1, f32[768]{0:T(1024)S(1)} %convert_element_type.182, ...), kind=kOutput, calls=%fused_computation.66 | convolution fusion | flops 3634100480 | bytes 19284480 | tf_op jit(solution)/shard_map/tf,df->td/dot_general | solution.py:188
  176.2 2.8 convolution_convert_fusion.3
  180.6 3.3 convolution_convert_fusion.2
  184.0 14.2 %multiply_reduce_fusion.1 = (f32[12,512]{1,0:T(8,128)S(1)}, f32[12,512,640]{2,1,0:T(8,128)}) fusion(f32[12,512,640]{2,1,0:T(8,128)} %copy-done.1, f32[12,512]{1,0:T(8,128)S(1)} %log_add_fusion.1, bf16[512,12,64]{0,2,1:T(8,128)(2,1)S(1)} %bitcast.137, bf16[640,12,64]{0,2,1:T(8,128)(2,1)} %bitcast.143), kind=kOutput, calls=%fused_computation.4 | convolution fusion | flops 515106816 | bytes 33275904 | tf_op jit(solution)/shard_map/qhd,khd->hqk/dot_general | solution.py:209
  200.0 7.6 %multiply_convert_fusion.1 = bf16[12,512,640]{2,1,0:T(8,128)(2,1)S(1)} fusion(f32[12,512,640]{2,1,0:T(8,128)} %get-tuple-element.154, f32[12,512,640]{2,1,0:T(8,128)S(1)} %bitcast.120, f32[12,512]{1,0:T(8,128)S(1)} %get-tuple-element.153, f32[12,512]{1,0:T(8,128)S(1)} %log_add_fusion.1), kind=kLoop, calls=%fused_computation.3 | loop fusion | flops 15728640 | bytes 39370752 | tf_op jit(solution)/shard_map/convert_element_type | solution.py:213
  207.6 3.1 copy-done.2
  210.7 2.7 convolution_multiply_fusion.1
  213.4 4.1 fusion.6
  217.6 9.5 %convolution_convert_fusion = bf16[768,2304]{1,0:T(8,128)(2,1)} fusion(f32[1024,1152]{1,0:T(8,128)} %copy-done.22, f32[1024,1152]{1,0:T(8,128)} %get-tuple-element.98, f32[1024,768]{0,1:T(8,128)S(1)} %copy-done.16, f32[768]{0:T(1024)S(1)} %convert_element_type.182, f32[1024]{0:T(1024)S(1)} %fusion.56, f32[1024]{0:T(1024)S(1)} %broadcast_multiply_fusion.1), kind=kOutput, calls=%fused_computation.26 | convolution fusion | flops 3633512448 | bytes 16133120 | tf_op jit(solution)/shard_map/td,tf->df/dot_general | solution.py:185
  227.2 14.3 %multiply_reduce_fusion = (f32[12,512]{1,0:T(8,128)S(1)}, f32[12,512,640]{2,1,0:T(8,128)}) fusion(f32[12,512,640]{2,1,0:T(8,128)} %copy-done, f32[12,512]{1,0:T(8,128)S(1)} %log_add_fusion, bf16[512,12,64]{0,2,1:T(8,128)(2,1)S(1)} %bitcast.135, bf16[640,12,64]{0,2,1:T(8,128)(2,1)} %bitcast.141), kind=kOutput, calls=%fused_computation.1 | convolution fusion | flops 515106816 | bytes 33275904 | tf_op jit(solution)/shard_map/qhd,khd->hqk/dot_general | solution.py:209
  243.1 8.3 %multiply_convert_fusion = bf16[12,512,640]{2,1,0:T(8,128)(2,1)S(1)} fusion(f32[12,512,640]{2,1,0:T(8,128)} %get-tuple-element.156, f32[12,512,640]{2,1,0:T(8,128)S(1)} %bitcast.118, f32[12,512]{1,0:T(8,128)S(1)} %get-tuple-element.155, f32[12,512]{1,0:T(8,128)S(1)} %log_add_fusion), kind=kLoop, calls=%fused_computation | loop fusion | flops 15728640 | bytes 39370752 | tf_op jit(solution)/shard_map/convert_element_type | solution.py:213
  251.4 3.1 copy-done.3
  257.1 4.1 fusion.4
  263.5 5.2 constant_dynamic-update-slice_fusion
  269.9 4.8 collective-permute-start.2
  279.9 4.4 slice.281
  287.9 5.0 scatter-add.16
  292.9 5.0 collective-permute-done.3
  299.3 4.6 scatter-add.19
  303.9 3.3 convert.67
  312.9 8.5 %convolution_convert_fusion.1 = bf16[768,2304]{1,0:T(8,128)(2,1)} fusion(bf16[1024,768]{0,1:T(8,128)(2,1)S(1)} %get-tuple-element.117, bf16[1024,768]{0,1:T(8,128)(2,1)S(1)} %bitcast.149, bf16[1024,768]{0,1:T(8,128)(2,1)S(1)} %bitcast.147, bf16[1,1024,768]{1,2,0:T(8,128)(2,1)S(1)} %copy-done.5, f32[768]{0:T(1024)S(1)} %copy-done.40, ...), kind=kOutput, calls=%fused_computation.27 | convolution fusion | flops 3643736064 | bytes 9841664 | tf_op jit(solution)/shard_map/td,te->de/dot_general | solution.py:253
  322.1 6.5 %fusion.38 = bf16[1,1024,768]{1,2,0:T(8,128)(2,1)} fusion(f32[1024,768]{0,1:T(8,128)} %copy-done.14, bf16[1024,1152]{1,0:T(8,128)(2,1)} %get-tuple-element.101, bf16[1152,768]{1,0:T(8,128)(2,1)} %all-gather.11.cloned.1.call-done), kind=kOutput, calls=%fused_computation.101 | convolution fusion | flops 1813512192 | bytes 8847360 | tf_op jit(solution)/shard_map/dot_general | solution.py:164
  328.7 2.9 copy.57
  331.6 7.0 %fusion.30 = (f32[1024]{0:T(1024)S(1)}, f32[1024,768]{0,1:T(8,128)S(1)}) fusion(bf16[1,1024,768]{1,2,0:T(8,128)(2,1)S(1)} %copy-done.5, f32[768]{0:T(1024)S(1)} %copy-done.40, f32[1024]{0:T(1024)S(1)} %copy-done.38, bf16[768,2304]{1,0:T(8,128)(2,1)} %all-gather.5.cloned.1.call-done, bf16[1024,768]{0,1:T(8,128)(2,1)} %copy-done.32, ...), kind=kOutput, calls=%fused_computation.64 | convolution fusion | flops 3641965568 | bytes 12987392 | tf_op jit(solution)/shard_map/te,de->td/dot_general | solution.py:256
  344.7 6.2 %all-reduce.8 = (bf16[768]{0:T(1024)(128)(2,1)S(1)}, bf16[768]{0:T(1024)(128)(2,1)S(1)}) all-reduce(bf16[768]{0:T(1024)(128)(2,1)S(1)} %get-tuple-element.82, bf16[768]{0:T(1024)(128)(2,1)S(1)} %copy-done.45), channel_id=2, replica_groups=mesh['seq'=8,'wshard'=4] {'wshard'}, use_global_device_ids=true, to_apply=%region_15.16.clone | all-reduce | flops 1536 | bytes 6144
  351.0 11.4 %reduce-scatter.5.cloned.1.call-done = bf16[192,2304]{1,0:T(8,128)(2,1)} async-done(((bf16[768,2304]{1,0:T(8,128)(2,1)}), bf16[192,2304]{1,0:T(8,128)(2,1)}) %reduce-scatter.5.cloned.1.call-update) | async-done | bytes 884752 | tf_op jit(solution)/shard_map/reduce_scatter | solution.py:266
  362.4 199.6 %all-reduce.11 = (f32[192]{0:T(256)}, f32[192,2304]{1,0:T(8,128)}, f32[192,768]{1,0:T(8,128)}, f32[192]{0:T(256)}, f32[192,2304]{1,0:T(8,128)}, /*index=5*/f32[288,768]{1,0:T(8,128)}) all-reduce(f32[192]{0:T(256)S(1)} %dynamic-slice_convert_fusion.1, ...), channel_id=1, replica_groups=mesh['seq'=8,'wshard'=4] {'seq'}, use_global_device_ids=true, to_apply=%region_16.17 | all-reduce | flops 1253760 | bytes 7523328 | tf_op jit(solution)/shard_map/psum | solution.py:282
  (207 shorter events, 80.7 us)
Async XLA Ops:
  7.2 18.9 %copy-start.26 = (bf16[1,1024,768]{2,1,0:T(8,128)(2,1)S(1)}, bf16[1,1024,768]{2,1,0:T(8,128)(2,1)}, u32[]{:S(2)}) copy-start(bf16[1,1024,768]{2,1,0:T(8,128)(2,1)} %param.17) | copy-start | bytes 4718596
  7.2 35.9 %all-gather.5.cloned.1.call-start = ((), (), s32[]{:S(2)}) async-start(), calls=%async_computation.4 | async-start | bytes 4423680 | tf_op jit(solution)/shard_map/all_gather | solution.py:86
  7.9 118.3 %all-gather.7.cloned.1.call-start = ((), (), s32[]{:S(2)}) async-start(), calls=%async_computation.5 | async-start | bytes 1474560 | tf_op jit(solution)/shard_map/all_gather | solution.py:87
  8.7 123.0 %all-gather.9.cloned.1.call-start = ((), (), s32[]{:S(2)}) async-start(), calls=%async_computation.6 | async-start | bytes 4423680 | tf_op jit(solution)/shard_map/all_gather | solution.py:89
  9.4 132.8 %all-gather.11.cloned.1.call-start = ((), (), s32[]{:S(2)}) async-start(), calls=%async_computation.7 | async-start | bytes 2211840 | tf_op jit(solution)/shard_map/all_gather | solution.py:90
  10.0 341.0 %reduce-scatter.7.cloned.1.call-start = ((), (), s32[]{:S(2)}) async-start(), calls=%async_computation.9 | async-start | bytes 1474560 | tf_op jit(solution)/shard_map/reduce_scatter | solution.py:269
  23.4 19.7 %copy-start.39 = (f32[768]{0:T(1024)}, f32[768]{0:T(1024)S(1)}, u32[]{:S(2)}) copy-start(f32[768]{0:T(1024)S(1)} %convert_element_type.167) | copy-start | bytes 9220
  26.8 99.4 %copy-start.4 = (bf16[1,1024,768]{1,2,0:T(8,128)(2,1)}, bf16[1,1024,768]{1,2,0:T(8,128)(2,1)S(1)}, u32[]{:S(2)}) copy-start(bf16[1,1024,768]{1,2,0:T(8,128)(2,1)S(1)} %copy.47) | copy-start | bytes 4718596
  27.1 22.2 %copy-start.37 = (f32[1024]{0:T(1024)}, f32[1024]{0:T(1024)S(1)}, u32[]{:S(2)}) copy-start(f32[1024]{0:T(1024)S(1)} %broadcast_multiply_fusion.2) | copy-start | bytes 12292
  27.6 4.1 copy-start.43
  28.8 20.5 %copy-start.41 = (f32[1024]{0:T(1024)}, f32[1024]{0:T(1024)S(1)}, u32[]{:S(2)}) copy-start(f32[1024]{0:T(1024)S(1)} %fusion.55) | copy-start | bytes 12292
  68.8 13.4 %copy-start.8 = (bf16[1024,768]{1,0:T(8,128)(2,1)S(1)}, bf16[1024,768]{1,0:T(8,128)(2,1)}, u32[]{:S(2)}) copy-start(bf16[1024,768]{1,0:T(8,128)(2,1)} %slice.344) | copy-start | bytes 4718596
  68.8 13.4 %copy-start.9 = (bf16[1024,768]{1,0:T(8,128)(2,1)S(1)}, bf16[1024,768]{1,0:T(8,128)(2,1)}, u32[]{:S(2)}) copy-start(bf16[1024,768]{1,0:T(8,128)(2,1)} %copy.49) | copy-start | bytes 4718596
  70.1 8.1 %collective-permute-start = (bf16[64,1536]{1,0:T(8,128)(2,1)S(1)}, bf16[64,1536]{1,0:T(8,128)(2,1)S(1)}, u32[]{:S(2)}, u32[]{:S(2)}) collective-permute-start(bf16[64,1536]{1,0:T(8,128)(2,1)S(1)} %get-tuple-element.120), channel_id=1, source_target_pairs={{0,4},{4,8},{8,12},{12,16},{16,20},{20,24},{24,28},{1,5},{5,9},{9,... | collective-permute-start | bytes 589832 | tf_op jit(solution)/shard_map/ppermute | solution.py:22
  73.6 8.7 %collective-permute-start.1 = (bf16[64,1536]{1,0:T(8,128)(2,1)S(1)}, bf16[64,1536]{1,0:T(8,128)(2,1)S(1)}, u32[]{:S(2)}, u32[]{:S(2)}) collective-permute-start(bf16[64,1536]{1,0:T(8,128)(2,1)S(1)} %get-tuple-element.121), channel_id=1, source_target_pairs={{4,0},{8,4},{12,8},{16,12},{20,16},{24,20},{28,24},{5,1},{9,5},{13... | collective-permute-start | bytes 589832 | tf_op jit(solution)/shard_map/ppermute | solution.py:23
  99.2 6.1 %copy-start = (f32[12,512,640]{2,1,0:T(8,128)}, f32[12,512,640]{2,1,0:T(8,128)S(1)}, u32[]{:S(2)}) copy-start(f32[12,512,640]{2,1,0:T(8,128)S(1)} %get-tuple-element.146) | copy-start | bytes 47185924
  99.2 6.1 %copy-start.23 = (bf16[640,768]{0,1:T(8,128)(2,1)S(1)}, bf16[640,768]{0,1:T(8,128)(2,1)}, u32[]{:S(2)}) copy-start(bf16[640,768]{0,1:T(8,128)(2,1)} %copy.53) | copy-start | bytes 2949124
  102.6 7.8 %copy-start.35 = (f32[12,512]{1,0:T(8,128)}, f32[12,512]{1,0:T(8,128)S(1)}, u32[]{:S(2)}) copy-start(f32[12,512]{1,0:T(8,128)S(1)} %fusion.1) | copy-start | bytes 73732
  105.4 5.1 copy-start.19
  113.7 5.6 copy-start.1
  113.7 5.6 copy-start.24
  131.6 10.6 %copy-start.28 = (bf16[1,1024,768]{2,1,0:T(8,128)(2,1)S(1)}, bf16[1,1024,768]{2,1,0:T(8,128)(2,1)}, u32[]{:S(2)}) copy-start(bf16[1,1024,768]{2,1,0:T(8,128)(2,1)} %param.25) | copy-start | bytes 4718596
  142.2 14.9 %copy-start.18 = (f32[1024,2304]{1,0:T(8,128)S(1)}, f32[1024,2304]{1,0:T(8,128)}, u32[]{:S(2)}) copy-start(f32[1024,2304]{1,0:T(8,128)} %fusion.66) | copy-start | bytes 28311556
  157.1 3.5 copy-start.15
  160.7 9.6 %copy-start.22 = (f32[1024,1152]{1,0:T(8,128)}, f32[1024,1152]{1,0:T(8,128)S(1)}, u32[]{:S(2)}) copy-start(f32[1024,1152]{1,0:T(8,128)S(1)} %get-tuple-element.100) | copy-start | bytes 14155780
  176.0 175.0 %reduce-scatter.11.cloned.1.call-start = ((), (), s32[]{:S(2)}) async-start(), calls=%async_computation.11 | async-start | bytes 2211840 | tf_op jit(solution)/shard_map/reduce_scatter | solution.py:278
  183.9 167.1 %reduce-scatter.9.cloned.1.call-start = ((), (), s32[]{:S(2)}) async-start(), calls=%async_computation.10 | async-start | bytes 4423680 | tf_op jit(solution)/shard_map/reduce_scatter | solution.py:275
  184.0 14.3 %slice-start.4 = ((s8[15728640]{0:T(1024)(128)(4,1)}), s8[4194304]{0:T(1024)(128)(4,1)S(1)}, s32[]{:S(2)}) async-start(s8[15728640]{0:T(1024)(128)(4,1)} %bitcast.119), calls=%async_computation.16 | async-start | bytes 8388608
  184.0 14.3 %slice-start.5 = ((s8[15728640]{0:T(1024)(128)(4,1)}), s8[4194304]{0:T(1024)(128)(4,1)S(1)}, s32[]{:S(2)}) async-start(s8[15728640]{0:T(1024)(128)(4,1)} %bitcast.119), calls=%async_computation.17 | async-start | bytes 8388608
  184.0 14.8 %slice-start.6 = ((s8[15728640]{0:T(1024)(128)(4,1)}), s8[4194304]{0:T(1024)(128)(4,1)S(1)}, s32[]{:S(2)}) async-start(s8[15728640]{0:T(1024)(128)(4,1)} %bitcast.119), calls=%async_computation.18 | async-start | bytes 8388608
  184.0 16.0 %slice-start.7 = ((s8[15728640]{0:T(1024)(128)(4,1)}), s8[3145728]{0:T(1024)(128)(4,1)S(1)}, s32[]{:S(2)}) async-start(s8[15728640]{0:T(1024)(128)(4,1)} %bitcast.119), calls=%async_computation.19 | async-start | bytes 6291456
  213.4 4.1 copy-start.16
  227.1 135.3 %reduce-scatter.5.cloned.1.call-start = ((), (), s32[]{:S(2)}) async-start(), calls=%async_computation.8 | async-start | bytes 4423680 | tf_op jit(solution)/shard_map/reduce_scatter | solution.py:266
  227.2 14.3 %slice-start = ((s8[15728640]{0:T(1024)(128)(4,1)}), s8[4194304]{0:T(1024)(128)(4,1)S(1)}, s32[]{:S(2)}) async-start(s8[15728640]{0:T(1024)(128)(4,1)} %bitcast.117), calls=%async_computation.12 | async-start | bytes 8388608
  227.2 14.3 %slice-start.1 = ((s8[15728640]{0:T(1024)(128)(4,1)}), s8[4194304]{0:T(1024)(128)(4,1)S(1)}, s32[]{:S(2)}) async-start(s8[15728640]{0:T(1024)(128)(4,1)} %bitcast.117), calls=%async_computation.13 | async-start | bytes 8388608
  227.2 14.3 %slice-start.2 = ((s8[15728640]{0:T(1024)(128)(4,1)}), s8[4194304]{0:T(1024)(128)(4,1)S(1)}, s32[]{:S(2)}) async-start(s8[15728640]{0:T(1024)(128)(4,1)} %bitcast.117), calls=%async_computation.14 | async-start | bytes 8388608
  227.2 15.9 %slice-start.3 = ((s8[15728640]{0:T(1024)(128)(4,1)}), s8[3145728]{0:T(1024)(128)(4,1)S(1)}, s32[]{:S(2)}) async-start(s8[15728640]{0:T(1024)(128)(4,1)} %bitcast.117), calls=%async_computation.15 | async-start | bytes 6291456
  257.1 4.1 copy-start.12
  261.3 13.4 %slice-start.10 = ((s8[7864320]{0:T(1024)(128)(4,1)}), s8[4194304]{0:T(1024)(128)(4,1)S(1)}, s32[]{:S(2)}) async-start(s8[7864320]{0:T(1024)(128)(4,1)} %bitcast.123), calls=%async_computation.22 | async-start | bytes 8388608
  261.3 15.9 %slice-start.8 = ((s8[7864320]{0:T(1024)(128)(4,1)}), s8[4194304]{0:T(1024)(128)(4,1)S(1)}, s32[]{:S(2)}) async-start(s8[7864320]{0:T(1024)(128)(4,1)} %bitcast.121), calls=%async_computation.20 | async-start | bytes 8388608
  263.5 11.2 %slice-start.11 = ((s8[7864320]{0:T(1024)(128)(4,1)}), s8[3670016]{0:T(1024)(128)(4,1)S(1)}, s32[]{:S(2)}) async-start(s8[7864320]{0:T(1024)(128)(4,1)} %bitcast.123), calls=%async_computation.23 | async-start | bytes 7340032
  263.5 11.2 %copy-start.21 = (bf16[640,768]{0,1:T(8,128)(2,1)S(1)}, bf16[640,768]{0,1:T(8,128)(2,1)}, u32[]{:S(2)}) copy-start(bf16[640,768]{0,1:T(8,128)(2,1)} %copy.54) | copy-start | bytes 2949124
  263.5 13.8 %slice-start.9 = ((s8[7864320]{0:T(1024)(128)(4,1)}), s8[3670016]{0:T(1024)(128)(4,1)S(1)}, s32[]{:S(2)}) async-start(s8[7864320]{0:T(1024)(128)(4,1)} %bitcast.121), calls=%async_computation.21 | async-start | bytes 7340032
  269.9 7.4 %copy-start.20 = (bf16[640,768]{0,1:T(8,128)(2,1)S(1)}, bf16[640,768]{0,1:T(8,128)(2,1)}, u32[]{:S(2)}) copy-start(bf16[640,768]{0,1:T(8,128)(2,1)} %copy.52) | copy-start | bytes 2949124
  269.9 17.8 %collective-permute-start.2 = (bf16[64,1536]{0,1:T(8,128)(2,1)S(1)}, bf16[64,1536]{0,1:T(8,128)(2,1)S(1)}, u32[]{:S(2)}, u32[]{:S(2)}) collective-permute-start(bf16[64,1536]{0,1:T(8,128)(2,1)S(1)} %slice.346), channel_id=1, source_target_pairs={{0,4},{4,8},{8,12},{12,16},{16,20},{20,24},{24,28},{1,5},{5,9},{9,... | collective-permute-start | bytes 589832 | tf_op jit(solution)/shard_map/ppermute | solution.py:31
  284.2 13.7 %collective-permute-start.3 = (bf16[64,1536]{0,1:T(8,128)(2,1)S(1)}, bf16[64,1536]{0,1:T(8,128)(2,1)S(1)}, u32[]{:S(2)}, u32[]{:S(2)}) collective-permute-start(bf16[64,1536]{0,1:T(8,128)(2,1)S(1)} %slice.345), channel_id=1, source_target_pairs={{4,0},{8,4},{12,8},{16,12},{20,16},{24,20},{28,24},{5,1},{9,5},{13... | collective-permute-start | bytes 589832 | tf_op jit(solution)/shard_map/ppermute | solution.py:31
  307.5 3.9 copy-start.32
  331.6 7.0 %copy-start.44 = (f32[1024]{0:T(1024)S(1)}, f32[1024]{0:T(1024)}, u32[]{:S(2)}) copy-start(f32[1024]{0:T(1024)} %copy-done.43) | copy-start | bytes 12292
  (22 other events, 46.7 us)
Sparse Core Ops, SparseCore 0:
  9.6 33.4 all-gather.4
  44.7 17.4 all-gather.6
  63.7 30.7 all-gather.8
  95.9 20.7 all-gather.10
  176.2 26.6 reduce-scatter.6
  206.0 29.4 reduce-scatter.10
  238.1 40.3 reduce-scatter.8
  321.6 40.7 reduce-scatter.4
where the time goes:
time: 578 us; the launch traced here: 569 us
  blocking collectives  214 us (37%)
  matrix products  150 us (26%)
  local copies, waits for them, and re-layouts  76 us (13%)
  other arithmetic  65.1 us (11%)
  waiting for transfers between devices  35.7 us (6%)
  between operations  16.6 us (3%)
  starting transfers between devices  11.4 us (2%)
    psum x1, blocking collectives, local(): lax.psum((shares[0], shares[1], shares[2], shares[3], shares[4], shares[5...  200 us
    unnamed x125, local copies, waits for them, and re-layouts  35.9 us
    dot_general x2, matrix products, local(): jnp.einsum('qhd,khd->hqk', attended_grad_block, value_block, preferred_el...  28.5 us
    convert_element_type x2, other arithmetic, local(): score_grad = (probs * (prob_grad - centre)).astype(jnp.bfloat16)  15.9 us
    dot_general x1, matrix products, local(): jnp.einsum('td,fd->tf', down_grad_low, weight_down_b, preferred_element_t...  14.9 us
    unnamed x2, blocking collectives  14.5 us
  transfers between devices with their start and end apart: 12, of which 5 were waited for; matrix products, arithmetic and copies ran while one was open for 41% of the time, Pallas kernels for 0%

commit v1 on v0

--- a/solution.py
+++ b/solution.py
@@ -29,6 +29,60 @@
     size = lax.axis_size(axis)
     pairs = [(i, i + by) for i in range(size) if 0 <= i + by < size]
     return lax.ppermute(shard, axis, pairs)
+
+
+def swap(shard, axis, bit):
+    return lax.ppermute(shard, axis, [(i, i ^ bit) for i in range(lax.axis_size(axis))])
+
+
+def bits_of(axis):
+    return [1 << b for b in range(lax.axis_size(axis).bit_length() - 1)]
+
+
+def gathered_small(shard, axis):
+    parts = shard[None]
+    for bit in bits_of(axis):
+        other = swap(parts, axis, bit)
+        upper = (lax.axis_index(axis) & bit) > 0
+        parts = jnp.concatenate(
+            [jnp.where(upper, other, parts), jnp.where(upper, parts, other)], axis=0
+        )
+    return parts.reshape((-1,) + shard.shape[1:])
+
+
+def reduced(term, owner_axis, sum_axis):
+    for bit in bits_of(owner_axis):
+        side = ((lax.axis_index(owner_axis) & bit) > 0).astype(jnp.int32)
+        pairs = term.reshape((term.shape[0] // 2, 2) + term.shape[1:])
+        kept = lax.dynamic_index_in_dim(pairs, side, 1, keepdims=False)
+        sent = lax.dynamic_index_in_dim(pairs, 1 - side, 1, keepdims=False)
+        term = kept + swap(sent, owner_axis, bit)
+    total = term[0]
+    halved = []
+    bits = bits_of(sum_axis)
+    for bit in bits:
+        rows = total.shape[0]
+        if bit != bits[-1] and rows % 32 == 0:
+            side = ((lax.axis_index(sum_axis) & bit) > 0).astype(jnp.int32)
+            kept = lax.dynamic_slice_in_dim(total, side * (rows // 2), rows // 2, 0)
+            sent = lax.dynamic_slice_in_dim(total, (1 - side) * (rows // 2), rows // 2, 0)
+            total = kept + swap(sent, sum_axis, bit)
+            halved.append(bit)
+        else:
+            total = total + swap(total, sum_axis, bit)
+    for bit in reversed(halved):
+        other = swap(total, sum_axis, bit)
+        upper = (lax.axis_index(sum_axis) & bit) > 0
+        total = jnp.concatenate(
+            [jnp.where(upper, other, total), jnp.where(upper, total, other)], axis=0
+        )
+    return total
+
+
+def total_of(grad):
+    owners = lax.axis_size("wshard")
+    term = grad.astype(jnp.bfloat16).reshape(owners, grad.shape[0] // owners, grad.shape[1])
+    return reduced(term, "wshard", "seq").astype(jnp.float32)
 
 
 def layer_norm(stream, gain):
@@ -82,10 +136,10 @@
     key_rows = block_rows + 2 * HALF
     blocks = tokens_dev // block_rows
     gathered = (
-        lax.all_gather(gain_attn, "wshard", axis=0, tiled=True),
+        gathered_small(gain_attn, "wshard"),
         lax.all_gather(w_qkv, "wshard", axis=0, tiled=True),
         lax.all_gather(w_out, "wshard", axis=0, tiled=True),
-        lax.all_gather(gain_mlp, "wshard", axis=0, tiled=True),
+        gathered_small(gain_mlp, "wshard"),
         lax.all_gather(w_in, "wshard", axis=0, tiled=True),
         lax.all_gather(w_down, "wshard", axis=0, tiled=True),
     )
@@ -163,14 +217,7 @@
     hidden = hidden_f.astype(jnp.bfloat16)
     result = middle + jnp.dot(hidden, gathered[5], preferred_element_type=jnp.float32)
     output = result.astype(jnp.bfloat16)[None]
-    backward_weights = (
-        lax.all_gather(gain_attn, "wshard", axis=0, tiled=True),
-        lax.all_gather(w_qkv, "wshard", axis=0, tiled=True),
-        lax.all_gather(w_out, "wshard", axis=0, tiled=True),
-        lax.all_gather(gain_mlp, "wshard", axis=0, tiled=True),
-        lax.all_gather(w_in, "wshard", axis=0, tiled=True),
-        lax.all_gather(w_down, "wshard", axis=0, tiled=True),
-    )
+    backward_weights = gathered
     weight_qkv_b = backward_weights[1]
     weight_out_b = backward_weights[2]
     weight_in_b = backward_weights[4]
@@ -258,29 +305,22 @@
     )
     grad_stream_norm, grad_gain_a = norm_back_a(grad_normed)
     input_grad = (grad_middle + grad_stream_norm).astype(jnp.bfloat16)[None]
-    terms = (grad_gain_a, grad_w_qkv, grad_w_out, grad_gain_m, grad_w_in, grad_w_down)
-    shares = (
-        lax.psum_scatter(
-            terms[0].astype(jnp.bfloat16), "wshard", scatter_dimension=0, tiled=True
-        ).astype(jnp.float32),
-        lax.psum_scatter(
-            terms[1].astype(jnp.bfloat16), "wshard", scatter_dimension=0, tiled=True
-        ).astype(jnp.float32),
-        lax.psum_scatter(
-            terms[2].astype(jnp.bfloat16), "wshard", scatter_dimension=0, tiled=True
-        ).astype(jnp.float32),
-        lax.psum_scatter(
-            terms[3].astype(jnp.bfloat16), "wshard", scatter_dimension=0, tiled=True
-        ).astype(jnp.float32),
-        lax.psum_scatter(
-            terms[4].astype(jnp.bfloat16), "wshard", scatter_dimension=0, tiled=True
-        ).astype(jnp.float32),
-        lax.psum_scatter(
-            terms[5].astype(jnp.bfloat16), "wshard", scatter_dimension=0, tiled=True
-        ).astype(jnp.float32),
-    )
-    totals = lax.psum((shares[0], shares[1], shares[2], shares[3], shares[4], shares[5]), "seq")
-    return (output, input_grad, totals[0], totals[1], totals[2], totals[3], totals[4], totals[5])
+    owners = lax.axis_size("wshard")
+    gains = reduced(
+        jnp.stack([grad_gain_a.reshape(owners, -1), grad_gain_m.reshape(owners, -1)], axis=1),
+        "wshard",
+        "seq",
+    )
+    return (
+        output,
+        input_grad,
+        gains[0],
+        total_of(grad_w_qkv),
+        total_of(grad_w_out),
+        gains[1],
+        total_of(grad_w_in),
+        total_of(grad_w_down),
+    )
 
 
 def solution(mesh):

time: 578 us -> 472 us (0.82)
  blocking collectives: 214 us -> 0 us
  waiting for transfers between devices: 35.7 us -> 125 us
  starting transfers between devices: 11.4 us -> 42.8 us
  matrix products: 150 us -> 126 us
  other arithmetic: 65.1 us -> 77.9 us
    psum x1 -> x0, blocking collectives: 200 us -> none  [local(): lax.psum((shares[0], shares[1], shares[2], shares[3], shares[4], shares[5...]
    ppermute x0 -> x36, waiting for transfers between devices: none -> 96.3 us  [swap(): lax.ppermute(shard, axis, [(i, i ^ bit) for i in range(lax.axis_size(axis...]
    ppermute x0 -> x36, starting transfers between devices: none -> 30.8 us  [swap(): lax.ppermute(shard, axis, [(i, i ^ bit) for i in range(lax.axis_size(axis...]
    unnamed x2 -> x0, blocking collectives: 14.5 us -> none
    reduce_scatter x4 -> x0, waiting for transfers between devices: 11.4 us -> none  [the longest x1 11.4 us: local(): lax.psum_scatter(terms[1].astype(jnp.bfloat16), 'wshard', scatter_dimensi...]
    unnamed x125 -> x154, local copies, waits for them, and re-layouts: 35.9 us -> 26.3 us
    dot_general x2, matrix products: 28.5 us -> 19.7 us  [local(): jnp.einsum('qhd,khd->hqk', attended_grad_block, value_block, preferred_el...]
    add x0 -> x24, other arithmetic: none -> 6.48 us  [the longest x9 4.8 us: reduced(): term = kept + swap(sent, owner_axis, bit)]
  transfers between devices with their start and end apart: 12 -> 44, of which waited for: 5 -> 25; matrix products, arithmetic and copies ran while one was open for 41% -> 34% of each run, Pallas kernels for 0% -> 0%
where the time goes in v1:
time: 472 us; the launch traced here: 463 us
  matrix products  126 us (27%)
  waiting for transfers between devices  125 us (26%)
  other arithmetic  77.9 us (17%)
  local copies, waits for them, and re-layouts  75.2 us (16%)
  starting transfers between devices  42.8 us (9%)
  between operations  15.5 us (3%)
    ppermute x36, waiting for transfers between devices, swap(): lax.ppermute(shard, axis, [(i, i ^ bit) for i in range(lax.axis_size(axis...  96.3 us
    ppermute x36, starting transfers between devices, swap(): lax.ppermute(shard, axis, [(i, i ^ bit) for i in range(lax.axis_size(axis...  30.8 us
    unnamed x154, local copies, waits for them, and re-layouts  26.3 us
    dot_general x2, matrix products, local(): jnp.einsum('qhd,khd->hqk', attended_grad_block, value_block, preferred_el...  19.7 us
    convert_element_type x2, other arithmetic, local(): score_grad = (probs * (prob_grad - centre)).astype(jnp.bfloat16)  19.5 us
    all_gather x1, waiting for transfers between devices, local(): lax.all_gather(w_qkv, 'wshard', axis=0, tiled=True)  15.4 us
    dot_general x1, matrix products, local(): jnp.einsum('td,fd->tf', down_grad_low, weight_down_b, preferred_element_t...  15.4 us
    dot_general x1, matrix products, local(): jnp.dot(normed2_low, gathered[4], preferred_element_type=jnp.float32)  10.5 us
  transfers between devices with their start and end apart: 44, of which 25 were waited for; matrix products, arithmetic and copies ran while one was open for 34% of the time, Pallas kernels for 0%

profile of v1, /device:TPU:0, one launch (start us, length us, event | category | flops | bytes accessed | tf_op | source)
XLA Modules:
  0.0 462.6 jit_solution(2200002174566815462)
XLA Ops:
  27.7 15.4 %all-gather.5.cloned.1.call-done = bf16[768,2304]{1,0:T(8,128)(2,1)} async-done(((bf16[192,2304]{1,0:T(8,128)(2,1)}), bf16[768,2304]{1,0:T(8,128)(2,1)}) %all-gather.5.cloned.1.call-update) | async-done | bytes 3538960 | tf_op jit(solution)/shard_map/all_gather | solution.py:140
  43.1 6.2 %fusion.53 = f32[1024,2304]{1,0:T(8,128)S(1)} fusion(bf16[768,2304]{1,0:T(8,128)(2,1)} %all-gather.5.cloned.1.call-done, bf16[1,1024,768]{1,2,0:T(8,128)(2,1)S(1)} %copy.35, f32[768]{0:T(1024)S(1)} %reshape.522, f32[1024]{0:T(1024)S(1)} %fusion.60, f32[1024]{0:T(1024)S(1)} %broadcast_multiply_fusion.2), kind=kOutput, calls=%fused_computation.154 | convolution fusion | flops 3627810816 | bytes 14560256 | tf_op jit(solution)/shard_map/dot_general | solution.py:151
  53.8 3.6 copy.39
  57.3 3.6 copy.36
  60.9 3.9 subtract_convert_fusion.2
  70.8 4.1 collective-permute-start.2
  79.0 4.7 %collective-permute-done.3 = bf16[64,1536]{1,0:T(8,128)(2,1)} collective-permute-done((bf16[64,1536]{1,0:T(8,128)(2,1)}, bf16[64,1536]{1,0:T(8,128)(2,1)}, u32[]{:S(2)}, u32[]{:S(2)}) %collective-permute-start.3) | collective-permute-done | bytes 196640 | tf_op jit(solution)/shard_map/ppermute | solution.py:23
  83.8 4.1 pad_maximum_fusion.10
  96.8 4.5 fusion.82
  101.4 3.4 fusion.1
  107.3 5.1 %fusion.48 = bf16[512,12,64]{0,2,1:T(8,128)(2,1)S(1)} fusion(bf16[640,12,64]{0,2,1:T(8,128)(2,1)S(1)} %bitcast.184, f32[12,512,640]{2,1,0:T(8,128)S(1)} %get-tuple-element.150, f32[12,512]{1,0:T(8,128)S(1)} %fusion.1, f32[12,512]{1,0:T(8,128)S(1)} %get-tuple-element.149), kind=kOutput, calls=%fused_computation.117 | convolution fusion | flops 515506176 | bytes 17547264 | tf_op jit(solution)/shard_map/hqk,khd->qhd/dot_general | solution.py:204
  115.7 3.4 fusion
  121.2 5.3 %fusion.47 = bf16[512,12,64]{0,2,1:T(8,128)(2,1)S(1)} fusion(bf16[640,12,64]{0,2,1:T(8,128)(2,1)S(1)} %bitcast.182, f32[12,512,640]{2,1,0:T(8,128)S(1)} %get-tuple-element.152, f32[12,512]{1,0:T(8,128)S(1)} %fusion, f32[12,512]{1,0:T(8,128)S(1)} %get-tuple-element.151), kind=kOutput, calls=%fused_computation.116 | convolution fusion | flops 515506176 | bytes 17547264 | tf_op jit(solution)/shard_map/hqk,khd->qhd/dot_general | solution.py:204
  126.8 3.3 fusion.84
  132.2 10.5 %fusion.73 = f32[1024,2304]{1,0:T(8,128)} fusion(bf16[768,2304]{1,0:T(8,128)(2,1)} %all-gather.9.cloned.1.call-done, f32[1024,768]{0,1:T(8,128)} %copy-done.13, f32[768]{0:T(1024)S(1)} %reshape.523, f32[1024]{0:T(1024)S(1)} %fusion.61, f32[1024]{0:T(1024)S(1)} %broadcast_multiply_fusion.1), kind=kOutput, calls=%fused_computation.239 | convolution fusion | flops 3627024384 | bytes 16133120 | tf_op jit(solution)/shard_map/dot_general | solution.py:215
  142.7 15.4 %fusion.37 = (f32[1024,1152]{1,0:T(8,128)}, f32[1024,1152]{1,0:T(8,128)S(1)}, f32[1024,1152]{1,0:T(8,128)S(1)}) fusion(f32[1024,2304]{1,0:T(8,128)} %fusion.73, bf16[1152,768]{1,0:T(8,128)(2,1)} %all-gather.11.cloned.1.call-done, bf16[1,1024,768]{2,1,0:T(8,128)(2,1)} %param.25), kind=kOutput, calls=%fused_computation.104 | convolution fusion | flops 1888616448 | bytes 22216704 | tf_op jit(solution)/shard_map/td,fd->tf/dot_general | solution.py:228
  158.2 3.8 multiply_add_fusion
  162.0 8.2 %convolution_convert_fusion = bf16[768,2304]{1,0:T(8,128)(2,1)} fusion(f32[1024,1152]{1,0:T(8,128)S(1)} %get-tuple-element.82, f32[1024,1152]{1,0:T(8,128)} %get-tuple-element.80, f32[1024,768]{0,1:T(8,128)S(1)} %copy-done.14, f32[768]{0:T(1024)S(1)} %reshape.523, f32[1024]{0:T(1024)S(1)} %fusion.61, f32[1024]{0:T(1024)S(1)} %broadcast_multiply_fusion.1), kind=kOutput, calls=%fused_computation.26 | convolution fusion | flops 3633512448 | bytes 16133120 | tf_op jit(solution)/shard_map/td,tf->df/dot_general | solution.py:232
  170.2 4.3 multiply_reduce_fusion.2
  183.7 4.2 fusion.4
  187.9 10.0 %multiply_reduce_fusion = (f32[12,512]{1,0:T(8,128)S(1)}, f32[12,512,640]{2,1,0:T(8,128)}) fusion(f32[12,512,640]{2,1,0:T(8,128)S(1)} %bitcast.164, f32[12,512]{1,0:T(8,128)S(1)} %log_add_fusion, bf16[512,12,64]{0,2,1:T(8,128)(2,1)S(1)} %bitcast.178, bf16[640,12,64]{0,2,1:T(8,128)(2,1)} %bitcast.183), kind=kOutput, calls=%fused_computation.1 | convolution fusion | flops 515106816 | bytes 33275904 | tf_op jit(solution)/shard_map/qhd,khd->hqk/dot_general | solution.py:256
  197.9 11.8 %multiply_convert_fusion = bf16[12,512,640]{2,1,0:T(8,128)(2,1)S(1)} fusion(f32[12,512,640]{2,1,0:T(8,128)} %get-tuple-element.160, f32[12,512,640]{2,1,0:T(8,128)} %copy-done.1, f32[12,512]{1,0:T(8,128)S(1)} %get-tuple-element.159, f32[12,512]{1,0:T(8,128)S(1)} %log_add_fusion), kind=kLoop, calls=%fused_computation | loop fusion | flops 15728640 | bytes 39370752 | tf_op jit(solution)/shard_map/convert_element_type | solution.py:260
  209.6 3.4 fusion.46
  215.8 4.2 fusion.6
  220.0 9.8 %multiply_reduce_fusion.1 = (f32[12,512]{1,0:T(8,128)S(1)}, f32[12,512,640]{2,1,0:T(8,128)}) fusion(f32[12,512,640]{2,1,0:T(8,128)S(1)} %bitcast.162, f32[12,512]{1,0:T(8,128)S(1)} %log_add_fusion.1, bf16[512,12,64]{0,2,1:T(8,128)(2,1)} %bitcast.175, bf16[640,12,64]{0,2,1:T(8,128)(2,1)} %bitcast.181), kind=kOutput, calls=%fused_computation.4 | convolution fusion | flops 515106816 | bytes 33275904 | tf_op jit(solution)/shard_map/qhd,khd->hqk/dot_general | solution.py:256
  229.7 7.8 %multiply_convert_fusion.1 = bf16[12,512,640]{2,1,0:T(8,128)(2,1)S(1)} fusion(f32[12,512,640]{2,1,0:T(8,128)} %get-tuple-element.158, f32[12,512,640]{2,1,0:T(8,128)S(1)} %bitcast.162, f32[12,512]{1,0:T(8,128)S(1)} %get-tuple-element.157, f32[12,512]{1,0:T(8,128)S(1)} %log_add_fusion.1), kind=kLoop, calls=%fused_computation.3 | loop fusion | flops 15728640 | bytes 39370752 | tf_op jit(solution)/shard_map/convert_element_type | solution.py:260
  237.5 3.4 fusion.45
  243.0 3.3 convolution_convert_fusion.2
  250.2 4.8 %collective-permute-start.6 = (bf16[64,1536]{0,1:T(8,128)(2,1)S(1)}, bf16[64,1536]{0,1:T(8,128)(2,1)}, u32[]{:S(2)}, u32[]{:S(2)}) collective-permute-start(bf16[64,1536]{0,1:T(8,128)(2,1)S(1)} %slice.356), channel_id=1, source_target_pairs={{0,4},{4,8},{8,12},{12,16},{16,20},{20,24},{24,28},{1,5},{5,9},{9,... | collective-permute-start | bytes 589832 | tf_op jit(solution)/shard_map/ppermute | solution.py:31
  256.4 3.5 fusion.38
  261.5 4.4 slice.289
  273.5 4.7 %scatter-add.16 = f32[1024,1536]{0,1:T(8,128)} dynamic-update-slice(f32[1024,1536]{0,1:T(8,128)} %slice.289, f32[64,1536]{0,1:T(8,128)S(1)} %slice_add_fusion.2, s32[]{:T(128)} %constant.254.clone.1, s32[]{:T(128)} %constant.254.clone.1) | dynamic-update-slice | bytes 786436 | tf_op jit(solution)/shard_map/scatter-add | solution.py:285
  278.2 4.1 collective-permute-done.7
  283.9 4.8 %scatter-add.19 = f32[1024,1536]{0,1:T(8,128)} dynamic-update-slice(f32[1024,1536]{0,1:T(8,128)} %scatter-add.16, f32[64,1536]{0,1:T(8,128)S(1)} %slice_add_fusion.1, s32[]{:T(128)} %constant.300.clone.1, s32[]{:T(128)} %constant.254.clone.1) | dynamic-update-slice | bytes 786436 | tf_op jit(solution)/shard_map/scatter-add | solution.py:286
  288.7 3.3 convert.69
  299.5 3.9 fusion.30
  310.0 6.5 %convolution_convert_fusion.1 = bf16[768,2304]{1,0:T(8,128)(2,1)S(1)} fusion(bf16[1024,768]{0,1:T(8,128)(2,1)} %copy-done.44, bf16[1024,768]{0,1:T(8,128)(2,1)} %bitcast.196, bf16[1024,768]{0,1:T(8,128)(2,1)} %bitcast.194, bf16[1,1024,768]{1,2,0:T(8,128)(2,1)S(1)} %copy-done.4, f32[768]{0:T(1024)S(1)} %copy-done.57, f32[1024]{0:T(1024)S(1)} %copy-done.55, ...), kind=kOutput, calls=%fused_computation.27 | convolution fusion | flops 3643736064 | bytes 9841664 | tf_op jit(solution)/shard_map/td,te->de/dot_general | solution.py:300
  345.1 3.4 collective-permute-done.24
  349.2 3.8 collective-permute-done.25
  355.2 3.4 collective-permute-done.26
  370.6 6.6 %collective-permute-done.38 = bf16[144,768]{1,0:T(8,128)(2,1)S(1)} collective-permute-done((bf16[144,768]{1,0:T(8,128)(2,1)S(1)}, bf16[144,768]{1,0:T(8,128)(2,1)S(1)}, u32[]{:S(2)}, u32[]{:S(2)}) %collective-permute-start.38) | collective-permute-done | bytes 221216 | tf_op jit(solution)/shard_map/ppermute | solution.py:35
  379.3 8.0 %collective-permute-done.28 = bf16[1,192,2304]{2,1,0:T(8,128)(2,1)S(1)} collective-permute-done((bf16[1,192,2304]{2,1,0:T(8,128)(2,1)S(1)}, bf16[1,192,2304]{2,1,0:T(8,128)(2,1)S(1)}, u32[]{:S(2)}, u32[]{:S(2)}) %collective-permute-start.28) | collective-permute-done | bytes 884768 | tf_op jit(solution)/shard_map/ppermute | solution.py:35
  388.1 15.0 %collective-permute-done.14 = bf16[1,192,2304]{2,1,0:T(8,128)(2,1)S(1)} collective-permute-done((bf16[1,192,2304]{2,1,0:T(8,128)(2,1)S(1)}, bf16[1,192,2304]{2,1,0:T(8,128)(2,1)S(1)}, u32[]{:S(2)}, u32[]{:S(2)}) %collective-permute-start.14) | collective-permute-done | bytes 884768 | tf_op jit(solution)/shard_map/ppermute | solution.py:35
  404.0 8.4 %collective-permute-done.15 = bf16[96,2304]{1,0:T(8,128)(2,1)S(1)} collective-permute-done((bf16[96,2304]{1,0:T(8,128)(2,1)S(1)}, bf16[96,2304]{1,0:T(8,128)(2,1)S(1)}, u32[]{:S(2)}, u32[]{:S(2)}) %collective-permute-start.15) | collective-permute-done | bytes 442400 | tf_op jit(solution)/shard_map/ppermute | solution.py:35
  413.6 6.3 %collective-permute-done.16 = bf16[48,2304]{1,0:T(8,128)(2,1)S(1)} collective-permute-done((bf16[48,2304]{1,0:T(8,128)(2,1)S(1)}, bf16[48,2304]{1,0:T(8,128)(2,1)S(1)}, u32[]{:S(2)}, u32[]{:S(2)}) %collective-permute-start.16) | collective-permute-done | bytes 221216 | tf_op jit(solution)/shard_map/ppermute | solution.py:35
  420.0 9.2 %collective-permute-done.31 = bf16[48,2304]{1,0:T(8,128)(2,1)S(1)} collective-permute-done((bf16[48,2304]{1,0:T(8,128)(2,1)S(1)}, bf16[48,2304]{1,0:T(8,128)(2,1)S(1)}, u32[]{:S(2)}, u32[]{:S(2)}) %collective-permute-start.31) | collective-permute-done | bytes 221216 | tf_op jit(solution)/shard_map/ppermute | solution.py:35
  432.5 4.9 %collective-permute-done.32 = bf16[48,2304]{1,0:T(8,128)(2,1)S(1)} collective-permute-done((bf16[48,2304]{1,0:T(8,128)(2,1)S(1)}, bf16[48,2304]{1,0:T(8,128)(2,1)S(1)}, u32[]{:S(2)}, u32[]{:S(2)}) %collective-permute-start.32) | collective-permute-done | bytes 221216 | tf_op jit(solution)/shard_map/ppermute | solution.py:35
  440.1 9.3 %collective-permute-done.33 = bf16[96,2304]{1,0:T(8,128)(2,1)S(1)} collective-permute-done((bf16[96,2304]{1,0:T(8,128)(2,1)S(1)}, bf16[96,2304]{1,0:T(8,128)(2,1)S(1)}, u32[]{:S(2)}, u32[]{:S(2)}) %collective-permute-start.33) | collective-permute-done | bytes 442400 | tf_op jit(solution)/shard_map/ppermute | solution.py:35
  (357 shorter events, 158.6 us)
Async XLA Ops:
  7.2 35.9 %all-gather.5.cloned.1.call-start = ((), (), s32[]{:S(2)}) async-start(), calls=%async_computation | async-start | bytes 4423680 | tf_op jit(solution)/shard_map/all_gather | solution.py:140
  7.9 118.8 %all-gather.7.cloned.1.call-start = ((), (), s32[]{:S(2)}) async-start(), calls=%async_computation.1 | async-start | bytes 1474560 | tf_op jit(solution)/shard_map/all_gather | solution.py:141
  8.7 123.5 %all-gather.9.cloned.1.call-start = ((), (), s32[]{:S(2)}) async-start(), calls=%async_computation.2 | async-start | bytes 4423680 | tf_op jit(solution)/shard_map/all_gather | solution.py:143
  9.4 133.3 %all-gather.11.cloned.1.call-start = ((), (), s32[]{:S(2)}) async-start(), calls=%async_computation.3 | async-start | bytes 2211840 | tf_op jit(solution)/shard_map/all_gather | solution.py:144
  10.1 12.8 %collective-permute-start.4 = (bf16[1,192]{1,0:T(2,128)(2,1)S(1)}, bf16[1,192]{1,0:T(2,128)(2,1)S(1)}, u32[]{:S(2)}, u32[]{:S(2)}) collective-permute-start(bf16[1,192]{1,0:T(2,128)(2,1)S(1)} %broadcast_in_dim.46), channel_id=1, source_target_pairs={{0,1},{1,0},{2,3},{3,2},{4,5},{5,4},{6,7},{7,6},{8,9},{9,8},{10,11... | collective-permute-start | bytes 1160 | tf_op jit(solution)/shard_map/ppermute | solution.py:35
  11.2 11.6 %collective-permute-start = (bf16[1,192]{1,0:T(2,128)(2,1)S(1)}, bf16[1,192]{1,0:T(2,128)(2,1)S(1)}, u32[]{:S(2)}, u32[]{:S(2)}) collective-permute-start(bf16[1,192]{1,0:T(2,128)(2,1)S(1)} %broadcast_in_dim.42), channel_id=1, source_target_pairs={{0,1},{1,0},{2,3},{3,2},{4,5},{5,4},{6,7},{7,6},{8,9},{9,8},{10,11... | collective-permute-start | bytes 1160 | tf_op jit(solution)/shard_map/ppermute | solution.py:35
  16.1 110.7 %copy-start.3 = (bf16[1,1024,768]{1,2,0:T(8,128)(2,1)}, bf16[1,1024,768]{1,2,0:T(8,128)(2,1)S(1)}, u32[]{:S(2)}) copy-start(bf16[1,1024,768]{1,2,0:T(8,128)(2,1)S(1)} %copy.35) | copy-start | bytes 4718596
  16.4 32.9 %copy-start.52 = (f32[1024]{0:T(1024)}, f32[1024]{0:T(1024)S(1)}, u32[]{:S(2)}) copy-start(f32[1024]{0:T(1024)S(1)} %broadcast_multiply_fusion.2) | copy-start | bytes 12292
  22.9 4.6 %collective-permute-start.1 = (bf16[2,192]{1,0:T(2,128)(2,1)S(1)}, bf16[2,192]{1,0:T(2,128)(2,1)S(1)}, u32[]{:S(2)}, u32[]{:S(2)}) collective-permute-start(bf16[2,192]{1,0:T(2,128)(2,1)S(1)} %pad_maximum_fusion.21), channel_id=1, source_target_pairs={{0,2},{1,3},{2,0},{3,1},{4,6},{5,7},{6,4},{7,5},{8,10},{9,11},{10,... | collective-permute-start | bytes 2312 | tf_op jit(solution)/shard_map/ppermute | solution.py:35
  26.0 50.6 %collective-permute-start.5 = (bf16[2,192]{1,0:T(2,128)(2,1)S(1)}, bf16[2,192]{1,0:T(2,128)(2,1)S(1)}, u32[]{:S(2)}, u32[]{:S(2)}) collective-permute-start(bf16[2,192]{1,0:T(2,128)(2,1)S(1)} %pad_maximum_fusion.22), channel_id=1, source_target_pairs={{0,2},{1,3},{2,0},{3,1},{4,6},{5,7},{6,4},{7,5},{8,10},{9,11},{10,... | collective-permute-start | bytes 2312 | tf_op jit(solution)/shard_map/ppermute | solution.py:35
  64.8 47.6 %copy-start.7 = (bf16[1024,12,32]{0,2,1:T(8,128)(2,1)}, bf16[1024,12,32]{0,2,1:T(8,128)(2,1)S(1)}, u32[]{:S(2)}) copy-start(bf16[1024,12,32]{0,2,1:T(8,128)(2,1)S(1)} %get-tuple-element.90) | copy-start | bytes 2359300
  64.8 47.6 %copy-start.9 = (bf16[1024,12,32]{0,2,1:T(8,128)(2,1)}, bf16[1024,12,32]{0,2,1:T(8,128)(2,1)S(1)}, u32[]{:S(2)}) copy-start(bf16[1024,12,32]{0,2,1:T(8,128)(2,1)S(1)} %get-tuple-element.91) | copy-start | bytes 2359300
  70.8 8.3 %collective-permute-start.2 = (bf16[64,1536]{1,0:T(8,128)(2,1)}, bf16[64,1536]{1,0:T(8,128)(2,1)}, u32[]{:S(2)}, u32[]{:S(2)}) collective-permute-start(bf16[64,1536]{1,0:T(8,128)(2,1)} %get-tuple-element.102), channel_id=1, source_target_pairs={{0,4},{4,8},{8,12},{12,16},{16,20},{20,24},{24,28},{1,5},{5,9},{9,... | collective-permute-start | bytes 589832 | tf_op jit(solution)/shard_map/ppermute | solution.py:22
  74.8 9.0 %collective-permute-start.3 = (bf16[64,1536]{1,0:T(8,128)(2,1)}, bf16[64,1536]{1,0:T(8,128)(2,1)}, u32[]{:S(2)}, u32[]{:S(2)}) collective-permute-start(bf16[64,1536]{1,0:T(8,128)(2,1)} %get-tuple-element.103), channel_id=1, source_target_pairs={{4,0},{8,4},{12,8},{16,12},{20,16},{24,20},{28,24},{5,1},{9,5},{13... | collective-permute-start | bytes 589832 | tf_op jit(solution)/shard_map/ppermute | solution.py:23
  250.2 21.8 %collective-permute-start.6 = (bf16[64,1536]{0,1:T(8,128)(2,1)S(1)}, bf16[64,1536]{0,1:T(8,128)(2,1)}, u32[]{:S(2)}, u32[]{:S(2)}) collective-permute-start(bf16[64,1536]{0,1:T(8,128)(2,1)S(1)} %slice.356), channel_id=1, source_target_pairs={{0,4},{4,8},{8,12},{12,16},{16,20},{20,24},{24,28},{1,5},{5,9},{9,... | collective-permute-start | bytes 589832 | tf_op jit(solution)/shard_map/ppermute | solution.py:31
  268.6 53.4 %collective-permute-start.20 = (bf16[2,192,768]{2,1,0:T(8,128)(2,1)}, bf16[2,192,768]{2,1,0:T(8,128)(2,1)}, u32[]{:S(2)}, u32[]{:S(2)}) collective-permute-start(bf16[2,192,768]{2,1,0:T(8,128)(2,1)} %dynamic-slice_bitcast_fusion.3), channel_id=1, source_target_pairs={{0,1},{1,0},{2,3},{3,2},{4,5},{5,4},{6,7},{7,6},{8,9},{9,8},{10,11... | collective-permute-start | bytes 1769480 | tf_op jit(solution)/shard_map/ppermute | solution.py:35
  268.6 13.7 %collective-permute-start.7 = (bf16[64,1536]{0,1:T(8,128)(2,1)}, bf16[64,1536]{0,1:T(8,128)(2,1)}, u32[]{:S(2)}, u32[]{:S(2)}) collective-permute-start(bf16[64,1536]{0,1:T(8,128)(2,1)} %slice.355), channel_id=1, source_target_pairs={{4,0},{8,4},{12,8},{16,12},{20,16},{24,20},{28,24},{5,1},{9,5},{13... | collective-permute-start | bytes 589832 | tf_op jit(solution)/shard_map/ppermute | solution.py:31
  306.5 2.7 collective-permute-start.8
  308.7 29.8 %collective-permute-start.34 = (bf16[2,288,768]{2,1,0:T(8,128)(2,1)}, bf16[2,288,768]{2,1,0:T(8,128)(2,1)}, u32[]{:S(2)}, u32[]{:S(2)}) collective-permute-start(bf16[2,288,768]{2,1,0:T(8,128)(2,1)} %dynamic-slice_bitcast_fusion.2), channel_id=1, source_target_pairs={{0,1},{1,0},{2,3},{3,2},{4,5},{5,4},{6,7},{7,6},{8,9},{9,8},{10,11... | collective-permute-start | bytes 2654216 | tf_op jit(solution)/shard_map/ppermute | solution.py:35
  309.2 53.6 %collective-permute-start.27 = (bf16[2,192,2304]{2,1,0:T(8,128)(2,1)}, bf16[2,192,2304]{2,1,0:T(8,128)(2,1)}, u32[]{:S(2)}, u32[]{:S(2)}) collective-permute-start(bf16[2,192,2304]{2,1,0:T(8,128)(2,1)} %dynamic-slice_bitcast_fusion), channel_id=1, source_target_pairs={{0,1},{1,0},{2,3},{3,2},{4,5},{5,4},{6,7},{7,6},{8,9},{9,8},{10,11... | collective-permute-start | bytes 5308424 | tf_op jit(solution)/shard_map/ppermute | solution.py:35
  309.3 7.2 %collective-permute-start.9 = (f32[1,2,192]{2,1,0:T(2,128)S(1)}, f32[1,2,192]{2,1,0:T(2,128)S(1)}, u32[]{:S(2)}, u32[]{:S(2)}) collective-permute-start(f32[1,2,192]{2,1,0:T(2,128)S(1)} %constant_dynamic-slice_fusion.9), channel_id=1, source_target_pairs={{0,2},{1,3},{2,0},{3,1},{4,6},{5,7},{6,4},{7,5},{8,10},{9,11},{10,... | collective-permute-start | bytes 4616 | tf_op jit(solution)/shard_map/ppermute | solution.py:35
  316.5 4.0 collective-permute-start.10
  320.6 6.9 %collective-permute-start.11 = (f32[2,192]{1,0:T(2,128)S(1)}, f32[2,192]{1,0:T(2,128)S(1)}, u32[]{:S(2)}, u32[]{:S(2)}) collective-permute-start(f32[2,192]{1,0:T(2,128)S(1)} %add.289), channel_id=1, source_target_pairs={{0,8},{4,12},{8,0},{12,4},{16,24},{20,28},{24,16},{28,20},{1,9},{5... | collective-permute-start | bytes 4616 | tf_op jit(solution)/shard_map/ppermute | solution.py:35
  323.2 8.0 %collective-permute-start.21 = (bf16[1,192,768]{2,1,0:T(8,128)(2,1)S(1)}, bf16[1,192,768]{2,1,0:T(8,128)(2,1)S(1)}, u32[]{:S(2)}, u32[]{:S(2)}) collective-permute-start(bf16[1,192,768]{2,1,0:T(8,128)(2,1)S(1)} %constant_dynamic-slice_fusion.6), channel_id=1, source_target_pairs={{0,2},{1,3},{2,0},{3,1},{4,6},{5,7},{6,4},{7,5},{8,10},{9,11},{10,... | collective-permute-start | bytes 884744 | tf_op jit(solution)/shard_map/ppermute | solution.py:35
  327.5 8.8 %collective-permute-start.12 = (f32[2,192]{1,0:T(2,128)S(1)}, f32[2,192]{1,0:T(2,128)S(1)}, u32[]{:S(2)}, u32[]{:S(2)}) collective-permute-start(f32[2,192]{1,0:T(2,128)S(1)} %add.290), channel_id=1, source_target_pairs={{0,16},{4,20},{8,24},{12,28},{16,0},{20,4},{24,8},{28,12},{1,17},{... | collective-permute-start | bytes 4616 | tf_op jit(solution)/shard_map/ppermute | solution.py:35
  331.6 5.3 %collective-permute-start.22 = (bf16[96,768]{1,0:T(8,128)(2,1)S(1)}, bf16[96,768]{1,0:T(8,128)(2,1)}, u32[]{:S(2)}, u32[]{:S(2)}) collective-permute-start(bf16[96,768]{1,0:T(8,128)(2,1)S(1)} %dynamic-slice_bitcast_fusion.7), channel_id=1, source_target_pairs={{0,4},{4,0},{8,12},{12,8},{16,20},{20,16},{24,28},{28,24},{1,5},{5... | collective-permute-start | bytes 442376 | tf_op jit(solution)/shard_map/ppermute | solution.py:35
  336.3 32.6 %collective-permute-start.13 = (bf16[2,192,2304]{2,1,0:T(8,128)(2,1)}, bf16[2,192,2304]{2,1,0:T(8,128)(2,1)S(1)}, u32[]{:S(2)}, u32[]{:S(2)}) collective-permute-start(bf16[2,192,2304]{2,1,0:T(8,128)(2,1)} %dynamic-slice_bitcast_fusion.1), channel_id=1, source_target_pairs={{0,1},{1,0},{2,3},{3,2},{4,5},{5,4},{6,7},{7,6},{8,9},{9,8},{10,11... | collective-permute-start | bytes 5308424 | tf_op jit(solution)/shard_map/ppermute | solution.py:35
  338.0 4.4 collective-permute-start.23
  342.4 6.1 %collective-permute-start.24 = (bf16[48,768]{1,0:T(8,128)(2,1)S(1)}, bf16[48,768]{1,0:T(8,128)(2,1)S(1)}, u32[]{:S(2)}, u32[]{:S(2)}) collective-permute-start(bf16[48,768]{1,0:T(8,128)(2,1)S(1)} %dynamic-slice_add_fusion.6), channel_id=1, source_target_pairs={{0,16},{4,20},{8,24},{12,28},{16,0},{20,4},{24,8},{28,12},{1,17},{... | collective-permute-start | bytes 221192 | tf_op jit(solution)/shard_map/ppermute | solution.py:35
  343.7 11.2 %collective-permute-start.35 = (bf16[1,288,768]{2,1,0:T(8,128)(2,1)S(1)}, bf16[1,288,768]{2,1,0:T(8,128)(2,1)S(1)}, u32[]{:S(2)}, u32[]{:S(2)}) collective-permute-start(bf16[1,288,768]{2,1,0:T(8,128)(2,1)S(1)} %constant_dynamic-slice_fusion.2), channel_id=1, source_target_pairs={{0,2},{1,3},{2,0},{3,1},{4,6},{5,7},{6,4},{7,5},{8,10},{9,11},{10,... | collective-permute-start | bytes 1327112 | tf_op jit(solution)/shard_map/ppermute | solution.py:35
  348.5 4.4 collective-permute-start.25
  353.0 5.6 %collective-permute-start.26 = (bf16[96,768]{1,0:T(8,128)(2,1)S(1)}, bf16[96,768]{1,0:T(8,128)(2,1)S(1)}, u32[]{:S(2)}, u32[]{:S(2)}) collective-permute-start(bf16[96,768]{1,0:T(8,128)(2,1)S(1)} %pad_maximum_fusion.18), channel_id=1, source_target_pairs={{0,4},{4,0},{8,12},{12,8},{16,20},{20,16},{24,28},{28,24},{1,5},{5... | collective-permute-start | bytes 442376 | tf_op jit(solution)/shard_map/ppermute | solution.py:35
  355.0 6.0 %collective-permute-start.36 = (bf16[144,768]{1,0:T(8,128)(2,1)S(1)}, bf16[144,768]{1,0:T(8,128)(2,1)S(1)}, u32[]{:S(2)}, u32[]{:S(2)}) collective-permute-start(bf16[144,768]{1,0:T(8,128)(2,1)S(1)} %dynamic-slice_bitcast_fusion.6), channel_id=1, source_target_pairs={{0,4},{4,0},{8,12},{12,8},{16,20},{20,16},{24,28},{28,24},{1,5},{5... | collective-permute-start | bytes 663560 | tf_op jit(solution)/shard_map/ppermute | solution.py:35
  361.1 6.0 %collective-permute-start.37 = (bf16[144,768]{1,0:T(8,128)(2,1)S(1)}, bf16[144,768]{1,0:T(8,128)(2,1)S(1)}, u32[]{:S(2)}, u32[]{:S(2)}) collective-permute-start(bf16[144,768]{1,0:T(8,128)(2,1)S(1)} %bitcast_add_fusion.6), channel_id=1, source_target_pairs={{0,8},{4,12},{8,0},{12,4},{16,24},{20,28},{24,16},{28,20},{1,9},{5... | collective-permute-start | bytes 663560 | tf_op jit(solution)/shard_map/ppermute | solution.py:35
  364.6 22.6 %collective-permute-start.28 = (bf16[1,192,2304]{2,1,0:T(8,128)(2,1)S(1)}, bf16[1,192,2304]{2,1,0:T(8,128)(2,1)S(1)}, u32[]{:S(2)}, u32[]{:S(2)}) collective-permute-start(bf16[1,192,2304]{2,1,0:T(8,128)(2,1)S(1)} %constant_dynamic-slice_fusion.4), channel_id=1, source_target_pairs={{0,2},{1,3},{2,0},{3,1},{4,6},{5,7},{6,4},{7,5},{8,10},{9,11},{10,... | collective-permute-start | bytes 2654216 | tf_op jit(solution)/shard_map/ppermute | solution.py:35
  367.1 10.1 %collective-permute-start.38 = (bf16[144,768]{1,0:T(8,128)(2,1)S(1)}, bf16[144,768]{1,0:T(8,128)(2,1)S(1)}, u32[]{:S(2)}, u32[]{:S(2)}) collective-permute-start(bf16[144,768]{1,0:T(8,128)(2,1)S(1)} %add.313), channel_id=1, source_target_pairs={{0,16},{4,20},{8,24},{12,28},{16,0},{20,4},{24,8},{28,12},{1,17},{... | collective-permute-start | bytes 663560 | tf_op jit(solution)/shard_map/ppermute | solution.py:35
  369.1 34.0 %collective-permute-start.14 = (bf16[1,192,2304]{2,1,0:T(8,128)(2,1)S(1)}, bf16[1,192,2304]{2,1,0:T(8,128)(2,1)S(1)}, u32[]{:S(2)}, u32[]{:S(2)}) collective-permute-start(bf16[1,192,2304]{2,1,0:T(8,128)(2,1)S(1)} %constant_dynamic-slice_fusion.8), channel_id=1, source_target_pairs={{0,2},{1,3},{2,0},{3,1},{4,6},{5,7},{6,4},{7,5},{8,10},{9,11},{10,... | collective-permute-start | bytes 2654216 | tf_op jit(solution)/shard_map/ppermute | solution.py:35
  377.3 52.1 %collective-permute-start.39 = (bf16[144,768]{1,0:T(8,128)(2,1)S(1)}, bf16[144,768]{1,0:T(8,128)(2,1)S(1)}, u32[]{:S(2)}, u32[]{:S(2)}) collective-permute-start(bf16[144,768]{1,0:T(8,128)(2,1)S(1)} %add.314), channel_id=1, source_target_pairs={{0,4},{4,0},{8,12},{12,8},{16,20},{20,16},{24,28},{28,24},{1,5},{5... | collective-permute-start | bytes 663560 | tf_op jit(solution)/shard_map/ppermute | solution.py:35
  387.4 16.0 %collective-permute-start.29 = (bf16[96,2304]{1,0:T(8,128)(2,1)S(1)}, bf16[96,2304]{1,0:T(8,128)(2,1)S(1)}, u32[]{:S(2)}, u32[]{:S(2)}) collective-permute-start(bf16[96,2304]{1,0:T(8,128)(2,1)S(1)} %dynamic-slice_bitcast_fusion.4), channel_id=1, source_target_pairs={{0,4},{4,0},{8,12},{12,8},{16,20},{20,16},{24,28},{28,24},{1,5},{5... | collective-permute-start | bytes 1327112 | tf_op jit(solution)/shard_map/ppermute | solution.py:35
  403.3 9.2 %collective-permute-start.15 = (bf16[96,2304]{1,0:T(8,128)(2,1)S(1)}, bf16[96,2304]{1,0:T(8,128)(2,1)S(1)}, u32[]{:S(2)}, u32[]{:S(2)}) collective-permute-start(bf16[96,2304]{1,0:T(8,128)(2,1)S(1)} %dynamic-slice_bitcast_fusion.5), channel_id=1, source_target_pairs={{0,4},{4,0},{8,12},{12,8},{16,20},{20,16},{24,28},{28,24},{1,5},{5... | collective-permute-start | bytes 1327112 | tf_op jit(solution)/shard_map/ppermute | solution.py:35
  403.5 9.6 %collective-permute-start.30 = (bf16[48,2304]{1,0:T(8,128)(2,1)S(1)}, bf16[48,2304]{1,0:T(8,128)(2,1)S(1)}, u32[]{:S(2)}, u32[]{:S(2)}) collective-permute-start(bf16[48,2304]{1,0:T(8,128)(2,1)S(1)} %constant_dynamic-slice_fusion.3), channel_id=1, source_target_pairs={{0,8},{4,12},{8,0},{12,4},{16,24},{20,28},{24,16},{28,20},{1,9},{5... | collective-permute-start | bytes 663560 | tf_op jit(solution)/shard_map/ppermute | solution.py:35
  412.6 7.3 %collective-permute-start.16 = (bf16[48,2304]{1,0:T(8,128)(2,1)S(1)}, bf16[48,2304]{1,0:T(8,128)(2,1)S(1)}, u32[]{:S(2)}, u32[]{:S(2)}) collective-permute-start(bf16[48,2304]{1,0:T(8,128)(2,1)S(1)} %constant_dynamic-slice_fusion.7), channel_id=1, source_target_pairs={{0,8},{4,12},{8,0},{12,4},{16,24},{20,28},{24,16},{28,20},{1,9},{5... | collective-permute-start | bytes 663560 | tf_op jit(solution)/shard_map/ppermute | solution.py:35
  413.1 16.0 %collective-permute-start.31 = (bf16[48,2304]{1,0:T(8,128)(2,1)S(1)}, bf16[48,2304]{1,0:T(8,128)(2,1)S(1)}, u32[]{:S(2)}, u32[]{:S(2)}) collective-permute-start(bf16[48,2304]{1,0:T(8,128)(2,1)S(1)} %dynamic-slice_add_fusion.4), channel_id=1, source_target_pairs={{0,16},{4,20},{8,24},{12,28},{16,0},{20,4},{24,8},{28,12},{1,17},{... | collective-permute-start | bytes 663560 | tf_op jit(solution)/shard_map/ppermute | solution.py:35
  419.9 11.9 %collective-permute-start.17 = (bf16[48,2304]{1,0:T(8,128)(2,1)S(1)}, bf16[48,2304]{1,0:T(8,128)(2,1)S(1)}, u32[]{:S(2)}, u32[]{:S(2)}) collective-permute-start(bf16[48,2304]{1,0:T(8,128)(2,1)S(1)} %dynamic-slice_add_fusion.5), channel_id=1, source_target_pairs={{0,16},{4,20},{8,24},{12,28},{16,0},{20,4},{24,8},{28,12},{1,17},{... | collective-permute-start | bytes 663560 | tf_op jit(solution)/shard_map/ppermute | solution.py:35
  429.2 8.1 %collective-permute-start.32 = (bf16[48,2304]{1,0:T(8,128)(2,1)S(1)}, bf16[48,2304]{1,0:T(8,128)(2,1)S(1)}, u32[]{:S(2)}, u32[]{:S(2)}) collective-permute-start(bf16[48,2304]{1,0:T(8,128)(2,1)S(1)} %add.308), channel_id=1, source_target_pairs={{0,8},{4,12},{8,0},{12,4},{16,24},{20,28},{24,16},{28,20},{1,9},{5... | collective-permute-start | bytes 663560 | tf_op jit(solution)/shard_map/ppermute | solution.py:35
  431.9 7.8 %collective-permute-start.18 = (bf16[48,2304]{1,0:T(8,128)(2,1)S(1)}, bf16[48,2304]{1,0:T(8,128)(2,1)S(1)}, u32[]{:S(2)}, u32[]{:S(2)}) collective-permute-start(bf16[48,2304]{1,0:T(8,128)(2,1)S(1)} %add.298), channel_id=1, source_target_pairs={{0,8},{4,12},{8,0},{12,4},{16,24},{20,28},{24,16},{28,20},{1,9},{5... | collective-permute-start | bytes 663560 | tf_op jit(solution)/shard_map/ppermute | solution.py:35
  437.4 12.0 %collective-permute-start.33 = (bf16[96,2304]{1,0:T(8,128)(2,1)S(1)}, bf16[96,2304]{1,0:T(8,128)(2,1)S(1)}, u32[]{:S(2)}, u32[]{:S(2)}) collective-permute-start(bf16[96,2304]{1,0:T(8,128)(2,1)S(1)} %pad_maximum_fusion.15), channel_id=1, source_target_pairs={{0,4},{4,0},{8,12},{12,8},{16,20},{20,16},{24,28},{28,24},{1,5},{5... | collective-permute-start | bytes 1327112 | tf_op jit(solution)/shard_map/ppermute | solution.py:35
  439.8 14.3 %collective-permute-start.19 = (bf16[96,2304]{1,0:T(8,128)(2,1)S(1)}, bf16[96,2304]{1,0:T(8,128)(2,1)S(1)}, u32[]{:S(2)}, u32[]{:S(2)}) collective-permute-start(bf16[96,2304]{1,0:T(8,128)(2,1)S(1)} %pad_maximum_fusion.14), channel_id=1, source_target_pairs={{0,4},{4,0},{8,12},{12,8},{16,20},{20,16},{24,28},{28,24},{1,5},{5... | collective-permute-start | bytes 1327112 | tf_op jit(solution)/shard_map/ppermute | solution.py:35
  (71 other events, 476.9 us)
Sparse Core Ops, SparseCore 0:
  9.6 33.4 all-gather.4
  44.7 17.4 all-gather.6
  63.7 30.7 all-gather.8
  95.9 20.7 all-gather.10

commit v2 on v1

v2 whole, which is shorter than its diff:
```python
import math

import jax
import jax.numpy as jnp
from jax import lax
from jax.experimental import pallas as pl
from jax.experimental.pallas import tpu as pltpu
from jax.sharding import PartitionSpec as P

HD = 64
HALF = 64


rope_base = 10000.0


def extended_2(shard, sides, width):
    for axis, dim in sides:
        size, length = (lax.axis_size(axis), shard.shape[dim])
        up = [(i, (i + 1) % size) for i in range(size - 1)]
        down = [(j, i) for i, j in up]
        last = lax.slice_in_dim(shard, length - width, length, axis=dim)
        leading = lax.slice_in_dim(shard, 0, width, axis=dim)
        before = lax.ppermute(last, axis, up)
        after = lax.ppermute(leading, axis, down)
        shard = jnp.concatenate([before, shard, after], axis=dim)
    return shard


def from_behind(shard, axis, by):
    size = lax.axis_size(axis)
    pairs = [(i, i + by) for i in range(size) if 0 <= i + by < size]
    return lax.ppermute(shard, axis, pairs)


def swap(shard, axis, bit):
    return lax.ppermute(shard, axis, [(i, i ^ bit) for i in range(lax.axis_size(axis))])


def bits_of(axis):
    return [1 << b for b in range(lax.axis_size(axis).bit_length() - 1)]


def gathered_small(shard, axis):
    parts = shard[None]
    for bit in bits_of(axis):
        other = swap(parts, axis, bit)
        upper = (lax.axis_index(axis) & bit) > 0
        parts = jnp.concatenate(
            [jnp.where(upper, other, parts), jnp.where(upper, parts, other)], axis=0
        )
    return parts.reshape((-1,) + shard.shape[1:])


def reduced(term, owner_axis, sum_axis):
    for bit in bits_of(owner_axis):
        side = ((lax.axis_index(owner_axis) & bit) > 0).astype(jnp.int32)
        pairs = term.reshape((term.shape[0] // 2, 2) + term.shape[1:])
        kept = lax.dynamic_index_in_dim(pairs, side, 1, keepdims=False)
        sent = lax.dynamic_index_in_dim(pairs, 1 - side, 1, keepdims=False)
        term = kept + swap(sent, owner_axis, bit)
    total = term[0]
    halved = []
    bits = bits_of(sum_axis)
    for bit in bits:
        rows = total.shape[0]
        if bit != bits[-1] and rows % 32 == 0:
            side = ((lax.axis_index(sum_axis) & bit) > 0).astype(jnp.int32)
            kept = lax.dynamic_slice_in_dim(total, side * (rows // 2), rows // 2, 0)
            sent = lax.dynamic_slice_in_dim(total, (1 - side) * (rows // 2), rows // 2, 0)
            total = kept + swap(sent, sum_axis, bit)
            halved.append(bit)
        else:
            total = total + swap(total, sum_axis, bit)
    for bit in reversed(halved):
        other = swap(total, sum_axis, bit)
        upper = (lax.axis_index(sum_axis) & bit) > 0
        total = jnp.concatenate(
            [jnp.where(upper, other, total), jnp.where(upper, total, other)], axis=0
        )
    return total


def total_of(grad):
    owners = lax.axis_size("wshard")
    term = grad.astype(jnp.bfloat16).reshape(owners, grad.shape[0] // owners, grad.shape[1])
    return reduced(term, "wshard", "seq").astype(jnp.float32)


def rope_tables(positions, head_dim):
    frequency = rope_base ** (-(jnp.arange(head_dim // 2, dtype=jnp.float32) * 2.0) / head_dim)
    angles = positions[:, None] * frequency[None, :]
    return (jnp.cos(angles)[:, None, :], jnp.sin(angles)[:, None, :])


ROWS = 256
QROWS = 128
LANES = 128
VMEM = 52 * 1024 * 1024
NT = (((1,), (1,)), ((), ()))
TN = (((0,), (0,)), ((), ()))


def mm(a, b, dims=(((1,), (0,)), ((), ()))):
    return lax.dot_general(a, b, dims, preferred_element_type=jnp.float32)


def standardised(stream):
    centred = stream - jnp.mean(stream, axis=-1, keepdims=True)
    scale = lax.rsqrt(jnp.mean(centred * centred, axis=-1, keepdims=True) + 1e-05)
    return centred * scale, scale


def norm_back(grad, unit, scale, gain):
    scaled = grad * gain
    first = jnp.mean(scaled, axis=-1, keepdims=True)
    second = jnp.mean(scaled * unit, axis=-1, keepdims=True)
    return scale * (scaled - first - unit * second)


def turn(chunk, cosine, sine_low, sine_high):
    ahead = pltpu.roll(chunk, LANES - HD // 2, 1)
    behind = pltpu.roll(chunk, HD // 2, 1)
    return chunk * cosine + ahead * sine_low + behind * sine_high


def qkv_kernel(x_ref, gain_ref, w_ref, cos_ref, low_ref, high_ref, normed_ref, q_ref, kv_ref):
    width = x_ref.shape[1]
    unit, _ = standardised(x_ref[...].astype(jnp.float32))
    normed = (unit * gain_ref[...]).astype(jnp.bfloat16)
    normed_ref[...] = normed
    cosine, low, high = cos_ref[...], low_ref[...], high_ref[...]
    for part in range(3):
        block = mm(normed, w_ref[:, part * width : (part + 1) * width])
        for c in range(0, width, LANES):
            chunk = block[:, c : c + LANES]
            if part < 2:
                chunk = turn(chunk, cosine, low, high)
            chunk = chunk.astype(jnp.bfloat16)
            if part == 0:
                q_ref[:, c : c + LANES] = chunk
            else:
                base = (part - 1) * width + c
                kv_ref[:, base : base + LANES] = chunk


def band_mask(meta_ref):
    start = meta_ref[2] + pl.program_id(0) * QROWS
    shape = (QROWS, QROWS + 2 * HALF)
    row = lax.broadcasted_iota(jnp.int32, shape, 0)
    col = lax.broadcasted_iota(jnp.int32, shape, 1)
    query_pos = start + row
    key_pos = start - HALF + col
    cut_first, cut_last = meta_ref[0], meta_ref[1]

    def segment(at):
        return (at >= cut_first).astype(jnp.int32) + (at >= cut_last).astype(jnp.int32)

    near = jnp.abs(query_pos - key_pos) <= HALF
    inside = (key_pos >= 0) & (key_pos < meta_ref[3])
    return near & inside & (segment(query_pos) == segment(key_pos))


def lower_lanes(rows):
    return lax.broadcasted_iota(jnp.int32, (rows, LANES), 1) < HD


def attend_kernel(meta_ref, q_ref, kv_ref, out_ref, lse_ref):
    width = q_ref.shape[1]
    allowed = band_mask(meta_ref)
    lower = lower_lanes(QROWS)
    rows = pl.ds(pl.multiple_of(pl.program_id(0) * QROWS, QROWS), QROWS + 2 * HALF)
    scale = 1.0 / math.sqrt(HD)
    lane = lax.broadcasted_iota(jnp.int32, (QROWS, LANES), 1)
    lses = jnp.zeros((QROWS, LANES), jnp.float32)
    for c in range(0, width, LANES):
        q = q_ref[:, c : c + LANES]
        k = kv_ref[rows, c : c + LANES]
        v = kv_ref[rows, width + c : width + c + LANES]
        outs = []
        for half in range(2):
            mine = lower if half == 0 else jnp.logical_not(lower)
            scores = mm(jnp.where(mine, q, jnp.zeros_like(q)), k, NT) * scale
            scores = jnp.where(allowed, scores, -1e30)
            top = jnp.max(scores, axis=-1, keepdims=True)
            expo = jnp.exp(scores - top)
            total = jnp.sum(expo, axis=-1, keepdims=True)
            probs = (expo * (1.0 / total)).astype(jnp.bfloat16)
            outs.append(mm(probs, v))
            lses = jnp.where(lane == c // HD + half, top + jnp.log(total), lses)
        out_ref[:, c : c + LANES] = jnp.where(lower, outs[0], outs[1]).astype(jnp.bfloat16)
    lse_ref[...] = lses


def attend_back_kernel(
    meta_ref, q_ref, go_ref, kv_ref, lse_ref, cos_ref, low_ref, high_ref, dq_ref, dkv_ref
):
    width = q_ref.shape[1]

    @pl.when(pl.program_id(0) == 0)
    def _():
        dkv_ref[...] = jnp.zeros_like(dkv_ref)

    allowed = band_mask(meta_ref)
    lower = lower_lanes(QROWS)
    rows = pl.ds(pl.multiple_of(pl.program_id(0) * QROWS, QROWS), QROWS + 2 * HALF)
    scale = 1.0 / math.sqrt(HD)
    for c in range(0, width, LANES):
        q = q_ref[:, c : c + LANES]
        go = go_ref[:, c : c + LANES]
        k = kv_ref[rows, c : c + LANES]
        v = kv_ref[rows, width + c : width + c + LANES]
        dqs = []
        dk = dv = None
        for half in range(2):
            mine = lower if half == 0 else jnp.logical_not(lower)
            q_half = jnp.where(mine, q, jnp.zeros_like(q))
            go_half = jnp.where(mine, go, jnp.zeros_like(go))
            head = c // HD + half
            scores = mm(q_half, k, NT) * scale
            scores = jnp.where(allowed, scores, -1e30)
            probs = jnp.exp(scores - lse_ref[:, head : head + 1])
            prob_grad = mm(go_half, v, NT)
            centre = jnp.sum(probs * prob_grad, axis=-1, keepdims=True)
            score_grad = (probs * (prob_grad - centre)).astype(jnp.bfloat16)
            dqs.append(mm(score_grad, k))
            dk_half = mm(score_grad, q_half, TN)
            dv_half = mm(probs.astype(jnp.bfloat16), go_half, TN)
            dk = dk_half if dk is None else dk + dk_half
            dv = dv_half if dv is None else dv + dv_half
        dq = (jnp.where(lower, dqs[0], dqs[1]) * scale).astype(jnp.bfloat16).astype(jnp.float32)
        dq_ref[:, c : c + LANES] = turn(
            dq, cos_ref[...], -low_ref[...], -high_ref[...]
        ).astype(jnp.bfloat16)
        dkv_ref[rows, c : c + LANES] += dk * scale
        dkv_ref[rows, width + c : width + c + LANES] += dv


def mlp_kernel(
    x_ref, att_ref, g_ref, gain_ref, wo_ref, wi_ref, wd_ref,
    out_ref, normed_ref, hidden_ref, gl_ref, gmid_ref, gm_ref, gatt_ref, ggain_ref,
):
    wide = wd_ref.shape[0]
    middle = x_ref[...].astype(jnp.float32) + mm(att_ref[...], wo_ref[...])
    unit, spread = standardised(middle)
    gain = gain_ref[...]
    normed = (unit * gain).astype(jnp.bfloat16)
    normed_ref[...] = normed
    active = mm(normed, wi_ref[:, :wide])
    gate = mm(normed, wi_ref[:, wide:])
    cdf = 0.5 * (1.0 + lax.erf(active * math.sqrt(0.5)))
    act = active * cdf
    hidden = (act * gate).astype(jnp.bfloat16)
    hidden_ref[...] = hidden
    out_ref[...] = (middle + mm(hidden, wd_ref[...])).astype(jnp.bfloat16)
    gd = g_ref[...]
    grad_hidden = mm(gd, wd_ref[...], NT)
    slope = cdf + active * (jnp.exp(-0.5 * active * active) * (1.0 / math.sqrt(2.0 * math.pi)))
    grad_active = (grad_hidden * gate * slope).astype(jnp.bfloat16)
    grad_gate = (grad_hidden * act).astype(jnp.bfloat16)
    gl_ref[:, :wide] = grad_active
    gl_ref[:, wide:] = grad_gate
    grad_normed = mm(grad_active, wi_ref[:, :wide], NT) + mm(grad_gate, wi_ref[:, wide:], NT)

    @pl.when(pl.program_id(0) == 0)
    def _():
        ggain_ref[...] = jnp.zeros_like(ggain_ref)

    ggain_ref[...] += jnp.sum(grad_normed * unit, axis=0, keepdims=True)
    grad_middle = gd.astype(jnp.float32) + norm_back(grad_normed, unit, spread, gain)
    gmid_ref[...] = grad_middle
    gm = grad_middle.astype(jnp.bfloat16)
    gm_ref[...] = gm
    gatt_ref[...] = mm(gm, wo_ref[...], NT).astype(jnp.bfloat16)


def last_kernel(
    x_ref, gain_ref, w_ref, dq_ref, dkv_ref, prev_ref, next_ref, cos_ref, low_ref, high_ref,
    gmid_ref, gp_ref, out_ref, ggain_ref,
):
    width = x_ref.shape[1]
    step = pl.program_id(0)
    start = pl.multiple_of(step * ROWS + HALF, HALF)
    first = (step == 0).astype(jnp.float32)
    last = (step == pl.num_programs(0) - 1).astype(jnp.float32)
    gp_ref[:, :width] = dq_ref[...]
    for c in range(0, 2 * width, LANES):
        own = dkv_ref[pl.ds(start, ROWS), c : c + LANES]
        top = own[:HALF] + prev_ref[:, c : c + LANES].astype(jnp.float32) * first
        low_end = own[ROWS - HALF :] + next_ref[:, c : c + LANES].astype(jnp.float32) * last
        chunk = jnp.concatenate([top, own[HALF : ROWS - HALF], low_end], axis=0)
        chunk = chunk.astype(jnp.bfloat16)
        if c < width:
            chunk = turn(
                chunk.astype(jnp.float32), cos_ref[...], -low_ref[...], -high_ref[...]
            ).astype(jnp.bfloat16)
        gp_ref[:, width + c : width + c + LANES] = chunk
    grad_normed = mm(gp_ref[...], w_ref[...], NT)
    unit, spread = standardised(x_ref[...].astype(jnp.float32))

    @pl.when(step == 0)
    def _():
        ggain_ref[...] = jnp.zeros_like(ggain_ref)

    ggain_ref[...] += jnp.sum(grad_normed * unit, axis=0, keepdims=True)
    out_ref[...] = (gmid_ref[...] + norm_back(grad_normed, unit, spread, gain_ref[...])).astype(
        jnp.bfloat16
    )


def run(body, steps, ins, outs, flops):
    def spec(array, rows):
        if rows == 0:
            return pl.BlockSpec(memory_space=pltpu.SMEM)
        if rows is None:
            return pl.BlockSpec(array.shape, lambda i: (0, 0))
        return pl.BlockSpec((rows, array.shape[1]), lambda i: (i, 0))

    moved = sum(a.size * a.dtype.itemsize for a, _ in ins + outs)
    return pl.pallas_call(
        body,
        grid=(steps,),
        in_specs=[spec(a, r) for a, r in ins],
        out_specs=[spec(a, r) for a, r in outs],
        out_shape=[a for a, _ in outs],
        compiler_params=pltpu.CompilerParams(
            vmem_limit_bytes=VMEM, dimension_semantics=("arbitrary",)
        ),
        cost_estimate=pl.CostEstimate(
            flops=int(flops), bytes_accessed=int(moved), transcendentals=0
        ),
    )(*[a for a, _ in ins])


def local(inputs, gain_attn, w_qkv, w_out, gain_mlp, w_in, w_down, bounds, grad_out):
    tokens = inputs.shape[1]
    width = inputs.shape[2]
    length = tokens * lax.axis_size("seq")
    offset = lax.axis_index("seq") * tokens
    shape = jax.ShapeDtypeStruct
    bf16, f32 = jnp.bfloat16, jnp.float32
    gains_all = gathered_small(jnp.stack([gain_attn, gain_mlp], axis=1), "wshard")
    gain_a = gains_all[:, 0].astype(f32)[None]
    gain_m = gains_all[:, 1].astype(f32)[None]
    weight_qkv = lax.all_gather(w_qkv, "wshard", axis=0, tiled=True)
    weight_out = lax.all_gather(w_out, "wshard", axis=0, tiled=True)
    weight_in = lax.all_gather(w_in, "wshard", axis=0, tiled=True)
    weight_down = lax.all_gather(w_down, "wshard", axis=0, tiled=True)
    wide = weight_down.shape[0]
    stream = inputs[0]
    upstream = grad_out[0]
    positions = (offset + jnp.arange(tokens, dtype=jnp.int32)).astype(f32)
    cosine, sine = rope_tables(positions, HD)
    cosine, sine = cosine[:, 0], sine[:, 0]
    none = jnp.zeros_like(sine)
    cos_t = jnp.concatenate([cosine] * 4, axis=1)
    low_t = jnp.concatenate([-sine, none] * 2, axis=1)
    high_t = jnp.concatenate([none, sine] * 2, axis=1)
    steps, qsteps = tokens // ROWS, tokens // QROWS
    normed, query, kv = run(
        qkv_kernel,
        steps,
        [(stream, ROWS), (gain_a, None), (weight_qkv, None)]
        + [(cos_t, ROWS), (low_t, ROWS), (high_t, ROWS)],
        [
            (shape((tokens, width), bf16), ROWS),
            (shape((tokens, width), bf16), ROWS),
            (shape((tokens, 2 * width), bf16), ROWS),
        ],
        6 * tokens * width * width,
    )
    kv_ext = extended_2(kv, (("seq", 0),), HALF)
    meta = jnp.stack([bounds[0, 0], bounds[0, 1], offset, jnp.int32(length)]).astype(jnp.int32)
    attended, lse = run(
        attend_kernel,
        qsteps,
        [(meta, 0), (query, QROWS), (kv_ext, None)],
        [(shape((tokens, width), bf16), QROWS), (shape((tokens, LANES), f32), QROWS)],
        16 * tokens * width * QROWS,
    )
    output, normed2, hidden, grad_lifted, grad_middle, grad_mid_low, grad_att, grad_gain_m = run(
        mlp_kernel,
        steps,
        [(stream, ROWS), (attended, ROWS), (upstream, ROWS), (gain_m, None)]
        + [(weight_out, None), (weight_in, None), (weight_down, None)],
        [
            (shape((tokens, width), bf16), ROWS),
            (shape((tokens, width), bf16), ROWS),
            (shape((tokens, wide), bf16), ROWS),
            (shape((tokens, 2 * wide), bf16), ROWS),
            (shape((tokens, width), f32), ROWS),
            (shape((tokens, width), bf16), ROWS),
            (shape((tokens, width), bf16), ROWS),
            (shape((1, width), f32), None),
        ],
        4 * tokens * width * (width + 3 * wide),
    )
    grad_w_down = mm(hidden, upstream, TN)
    grad_w_in = mm(normed2, grad_lifted, TN)
    grad_w_out = mm(attended, grad_mid_low, TN)
    query_grad, kv_grad = run(
        attend_back_kernel,
        qsteps,
        [(meta, 0), (query, QROWS), (grad_att, QROWS), (kv_ext, None), (lse, QROWS)]
        + [(cos_t, QROWS), (low_t, QROWS), (high_t, QROWS)],
        [
            (shape((tokens, width), bf16), QROWS),
            (shape((tokens + 2 * HALF, 2 * width), f32), None),
        ],
        40 * tokens * width * QROWS,
    )
    from_next = from_behind(kv_grad[:HALF].astype(bf16), "seq", -1)
    from_prev = from_behind(kv_grad[tokens + HALF :].astype(bf16), "seq", 1)
    grad_projected, input_grad, grad_gain_a = run(
        last_kernel,
        steps,
        [(stream, ROWS), (gain_a, None), (weight_qkv, None), (query_grad, ROWS), (kv_grad, None)]
        + [(from_prev, None), (from_next, None)]
        + [(cos_t, ROWS), (low_t, ROWS), (high_t, ROWS), (grad_middle, ROWS)],
        [
            (shape((tokens, 3 * width), bf16), ROWS),
            (shape((tokens, width), bf16), ROWS),
            (shape((1, width), f32), None),
        ],
        6 * tokens * width * width,
    )
    grad_w_qkv = mm(normed, grad_projected, TN)
    output, input_grad = output[None], input_grad[None]
    owners = lax.axis_size("wshard")
    gains = reduced(
        jnp.stack([grad_gain_a.reshape(owners, -1), grad_gain_m.reshape(owners, -1)], axis=1),
        "wshard",
        "seq",
    )
    return (
        output,
        input_grad,
        gains[0],
        total_of(grad_w_qkv),
        total_of(grad_w_out),
        gains[1],
        total_of(grad_w_in),
        total_of(grad_w_down),
    )


def solution(mesh):
    return jax.shard_map(
        local,
        mesh=mesh,
        in_specs=(
            P("wshard", "seq", None),
            P("wshard"),
            P("wshard", None),
            P("wshard", None),
            P("wshard"),
            P("wshard", None),
            P("wshard", None),
            P("wshard", None),
            P("wshard", "seq", None),
        ),
        out_specs=(
            P("wshard", "seq", None),
            P("wshard", "seq", None),
            P("wshard"),
            P("wshard", None),
            P("wshard", None),
            P("wshard"),
            P("wshard", None),
            P("wshard", None),
        ),
        check_vma=False,
    )
```

time: 472 us -> 359 us (0.76); the launches traced: 463 us -> 359 us
  matrix products: 126 us -> 18.2 us
  Pallas kernels: 0 us -> 96.9 us
  local copies, waits for them, and re-layouts: 75.2 us -> 10.6 us
  other arithmetic: 77.9 us -> 15.9 us
  waiting for transfers between devices: 125 us -> 161 us
    dot_general x24 -> x4, matrix products: 126 us -> 18.2 us  [mm(): return lax.dot_general(a, b, dims, preferred_element_type=jnp.float32)]
    pallas_call x0 -> x5, Pallas kernels: none -> 96.9 us  [run(): pl.pallas_call(body, grid=(steps,), in_specs=[spec(a, r) for a, r in ins]...]
    all_gather x4, waiting for transfers between devices: 15.5 us -> 58.7 us  [the longest x1 32.2 us: local(): weight_in = lax.all_gather(w_in, 'wshard', axis=0, tiled=True)]
    slice x14 -> x3, local copies, waits for them, and re-layouts: 28.5 us -> 1.7 us  [the longest x1 1.09 us: extended_2(): leading = lax.slice_in_dim(shard, 0, width, axis=dim)]
    convert_element_type x6 -> x2, other arithmetic: 22.3 us -> 0.01 us  [the longest x1 0.01 us: local(): gain_m = gains_all[:, 1].astype(f32)[None]]
    unnamed x154 -> x31, local copies, waits for them, and re-layouts: 26.3 us -> 6.4 us
    reduce_sum x7 -> x0, other arithmetic: 10 us -> none  [the longest x2 6.77 us: local(): row_total = jnp.sum(expo, axis=-1, keepdims=True)]
    scatter-add x2 -> x0, local copies, waits for them, and re-layouts: 9.57 us -> none  [the longest x1 4.84 us: local(): own_grad = own_grad.at[tokens_dev - HALF:].add(from_next)]
  transfers between devices with their start and end apart: 44 -> 42, of which waited for: 25 -> 30; matrix products, arithmetic and copies ran while one was open for 34% -> 10% of each run, Pallas kernels for 0% -> 20%
where the time goes in v2:
time: 359 us
  waiting for transfers between devices  161 us (45%)
  Pallas kernels  96.9 us (27%)
  starting transfers between devices  41.6 us (12%)
  matrix products  18.2 us (5%)
  other arithmetic  15.9 us (4%)
  between operations  14.5 us (4%)
  local copies, waits for them, and re-layouts  10.6 us (3%)
    pallas_call x5, Pallas kernels, run(): pl.pallas_call(body, grid=(steps,), in_specs=[spec(a, r) for a, r in ins]...  96.9 us
    ppermute x34, waiting for transfers between devices, swap(): lax.ppermute(shard, axis, [(i, i ^ bit) for i in range(lax.axis_size(axis...  90.9 us
    all_gather x1, waiting for transfers between devices, local(): weight_in = lax.all_gather(w_in, 'wshard', axis=0, tiled=True)  32.2 us
    ppermute x34, starting transfers between devices, swap(): lax.ppermute(shard, axis, [(i, i ^ bit) for i in range(lax.axis_size(axis...  31.7 us
    all_gather x1, waiting for transfers between devices, local(): weight_qkv = lax.all_gather(w_qkv, 'wshard', axis=0, tiled=True)  24.9 us
    dot_general x4, matrix products, mm(): return lax.dot_general(a, b, dims, preferred_element_type=jnp.float32)  18.2 us
  transfers between devices with their start and end apart: 42, of which 30 were waited for; matrix products, arithmetic and copies ran while one was open for 10% of the time, Pallas kernels for 20%

profile of v2, /device:TPU:0, one launch (start us, length us, event | category | flops | bytes accessed | tf_op | source)
XLA Modules:
  0.0 358.8 jit_solution(10586541063845812791)
XLA Ops:
  10.6 1.9 multiply_sine_fusion
  13.9 2.6 collective-permute-start.1
  16.5 1.6 collective-permute-done.1
  18.2 24.9 %all-gather.5.cloned.1.call-done.w_ref = bf16[768,2304]{1,0:T(8,128)(2,1)} async-done(((bf16[192,2304]{1,0:T(8,128)(2,1)}), bf16[768,2304]{1,0:T(8,128)(2,1)}) %all-gather.5.cloned.1.call-update) | async-done | bytes 3538960 | tf_op jit(solution)/shard_map/all_gather | solution.py:345
  43.1 8.8 %shard_map.152 = (bf16[1024,768]{1,0:T(8,128)(2,1)}, bf16[1024,768]{1,0:T(8,128)(2,1)}, bf16[1024,1536]{1,0:T(8,128)(2,1)}) custom-call(bf16[1024,768]{1,0:T(8,128)(2,1)} %bitcast.86, f32[1,768]{1,0:T(1,128)S(1)} %get-tuple-element.72.gain_ref, bf16[768,2304]{1,0:T(8,128)(2,1)} %all-gather.5.cloned.1.call-done.w_ref, ...), custom_call_target="tpu_custom_call" | custom-call | flops 3623878656 | bytes 12979200 | tf_op jit(solution)/shard_map/pallas_call | solution.py:320
  52.9 3.4 collective-permute-start.2
  61.0 2.1 constant_dynamic-update-slice_fusion.1
  63.1 4.0 %collective-permute-done.3 = bf16[64,1536]{1,0:T(8,128)(2,1)S(1)} collective-permute-done((bf16[64,1536]{1,0:T(8,128)(2,1)S(1)}, bf16[64,1536]{1,0:T(8,128)(2,1)S(1)}, u32[]{:S(2)}, u32[]{:S(2)}) %collective-permute-start.3) | collective-permute-done | bytes 196640 | tf_op jit(solution)/shard_map/ppermute | solution.py:25
  67.0 1.7 copy-done.5
  68.8 14.1 %shard_map.153 = (bf16[1024,768]{1,0:T(8,128)(2,1)}, f32[1024,128]{1,0:T(8,128)S(1)}) custom-call(s32[4]{0:T(128)S(1)} %pad_add_fusion.meta_ref, bf16[1024,768]{1,0:T(8,128)(2,1)} %get-tuple-element.26.q_ref, bf16[1152,1536]{1,0:T(8,128)(2,1)} %copy-done.5), custom_call_target="tpu_custom_call" | custom-call | flops 1610612736 | bytes 7208976 | tf_op jit(solution)/shard_map/pallas_call | solution.py:320
  82.9 1.6 all-gather.11.cloned.1.call-done.wd_ref
  84.5 32.2 %all-gather.9.cloned.1.call-done.wi_ref = bf16[768,2304]{1,0:T(8,128)(2,1)} async-done(((bf16[192,2304]{1,0:T(8,128)(2,1)}), bf16[768,2304]{1,0:T(8,128)(2,1)}) %all-gather.9.cloned.1.call-update) | async-done | bytes 3538960 | tf_op jit(solution)/shard_map/all_gather | solution.py:347
  118.0 25.6 %shard_map.154 = (bf16[1024,768]{1,0:T(8,128)(2,1)}, bf16[1024,768]{1,0:T(8,128)(2,1)}, bf16[1024,1152]{1,0:T(8,128)(2,1)}, bf16[1024,2304]{1,0:T(8,128)(2,1)}, ...) custom-call(bf16[1024,768]{1,0:T(8,128)(2,1)} %bitcast.87, ...), custom_call_target="tpu_custom_call" | custom-call | flops 13287555072 | bytes 27727872 | tf_op jit(solution)/shard_map/pallas_call | solution.py:320
  143.6 3.7 %convolution_convert_fusion.2 = bf16[1152,768]{1,0:T(8,128)(2,1)S(1)} fusion(bf16[1024,1152]{1,0:T(8,128)(2,1)} %get-tuple-element.43, bf16[1,1024,768]{2,1,0:T(8,128)(2,1)S(1)} %copy-done.7), kind=kOutput, calls=%fused_computation.2 | convolution fusion | flops 1812824064 | bytes 5701632 | tf_op jit(solution)/shard_map/dot_general | solution.py:105
  149.7 35.7 %shard_map.155 = (bf16[1024,768]{1,0:T(8,128)(2,1)}, f32[1152,1536]{1,0:T(8,128)}) custom-call(s32[4]{0:T(128)S(1)} %pad_add_fusion.meta_ref, bf16[1024,768]{1,0:T(8,128)(2,1)} %get-tuple-element.26.q_ref, bf16[1024,768]{1,0:T(8,128)(2,1)} %get-tuple-element.30.go_ref, bf16[1152,1536]{1,0:T(8,128)(2,1)} %copy-done.5, ...), custom_call_target="tpu_custom_call" | custom-call | flops 4026531840 | bytes 17432592 | tf_op jit(solution)/shard_map/pallas_call | solution.py:320
  185.5 3.4 convert.6
  188.9 3.4 collective-permute-start.4
  192.3 1.5 collective-permute-start.5
  194.0 3.4 convolution_convert_fusion.3
  197.3 3.7 %collective-permute-done.5.next_ref = bf16[64,1536]{1,0:T(8,128)(2,1)S(1)} collective-permute-done((bf16[64,1536]{1,0:T(8,128)(2,1)S(1)}, bf16[64,1536]{1,0:T(8,128)(2,1)S(1)}, u32[]{:S(2)}, u32[]{:S(2)}) %collective-permute-start.5) | collective-permute-done | bytes 196640 | tf_op jit(solution)/shard_map/ppermute | solution.py:33
  201.0 12.8 %shard_map.156 = (bf16[1024,2304]{1,0:T(8,128)(2,1)}, bf16[1024,768]{1,0:T(8,128)(2,1)}, f32[1,768]{1,0:T(1,128)S(1)}) custom-call(bf16[1024,768]{1,0:T(8,128)(2,1)} %bitcast.88, f32[1,768]{1,0:T(1,128)S(1)} %get-tuple-element.72.gain_ref, bf16[768,2304]{1,0:T(8,128)(2,1)} %all-gather.5.cloned.1.call-done.w_ref, bf16[1024,768]{1,0:T(8,128)(2,1)} %get-tuple-element.32.dq_ref, ...), custom_call_target="tpu_custom_call" | custom-call | flops 3623878656 | bytes 25171968 | tf_op jit(solution)/shard_map/pallas_call | solution.py:320
  215.8 6.7 %convolution_convert_fusion = bf16[768,2304]{1,0:T(8,128)(2,1)S(1)} fusion(bf16[1024,768]{1,0:T(8,128)(2,1)} %get-tuple-element.41, bf16[1024,2304]{1,0:T(8,128)(2,1)} %get-tuple-element.42), kind=kOutput, calls=%fused_computation | convolution fusion | flops 3625648128 | bytes 9830400 | tf_op jit(solution)/shard_map/dot_general | solution.py:105
  222.6 2.6 collective-permute-start.8
  226.8 2.9 collective-permute-start.9
  229.9 1.5 collective-permute-start.19
  231.4 4.4 %convolution_convert_fusion.1 = bf16[768,2304]{1,0:T(8,128)(2,1)S(1)} fusion(bf16[1024,768]{1,0:T(8,128)(2,1)S(1)} %copy-done.10, bf16[1024,2304]{1,0:T(8,128)(2,1)S(1)} %bitcast.96), kind=kOutput, calls=%fused_computation.1 | convolution fusion | flops 3625648128 | bytes 9830400 | tf_op jit(solution)/shard_map/dot_general | solution.py:105
  235.8 2.5 collective-permute-start.10
  238.7 1.7 collective-permute-done.10
  240.4 3.2 collective-permute-done.20
  245.5 2.6 collective-permute-done.21
  249.6 1.5 collective-permute-start.33
  251.1 3.1 collective-permute-done.22
  255.4 3.3 collective-permute-done.23
  258.9 2.1 collective-permute-start.34
  261.0 3.0 collective-permute-done.24
  267.6 6.8 %collective-permute-done.35 = bf16[144,768]{1,0:T(8,128)(2,1)S(1)} collective-permute-done((bf16[144,768]{1,0:T(8,128)(2,1)S(1)}, bf16[144,768]{1,0:T(8,128)(2,1)S(1)}, u32[]{:S(2)}, u32[]{:S(2)}) %collective-permute-start.35) | collective-permute-done | bytes 221216 | tf_op jit(solution)/shard_map/ppermute | solution.py:37
  275.6 7.1 %collective-permute-done.36 = bf16[144,768]{1,0:T(8,128)(2,1)S(1)} collective-permute-done((bf16[144,768]{1,0:T(8,128)(2,1)S(1)}, bf16[144,768]{1,0:T(8,128)(2,1)S(1)}, u32[]{:S(2)}, u32[]{:S(2)}) %collective-permute-start.36) | collective-permute-done | bytes 221216 | tf_op jit(solution)/shard_map/ppermute | solution.py:37
  283.7 6.2 %collective-permute-done.26 = bf16[1,192,2304]{2,1,0:T(8,128)(2,1)S(1)} collective-permute-done((bf16[1,192,2304]{2,1,0:T(8,128)(2,1)S(1)}, bf16[1,192,2304]{2,1,0:T(8,128)(2,1)S(1)}, u32[]{:S(2)}, u32[]{:S(2)}) %collective-permute-start.26) | collective-permute-done | bytes 884768 | tf_op jit(solution)/shard_map/ppermute | solution.py:37
  290.7 9.0 %collective-permute-done.12 = bf16[1,192,2304]{2,1,0:T(8,128)(2,1)S(1)} collective-permute-done((bf16[1,192,2304]{2,1,0:T(8,128)(2,1)S(1)}, bf16[1,192,2304]{2,1,0:T(8,128)(2,1)S(1)}, u32[]{:S(2)}, u32[]{:S(2)}) %collective-permute-start.12) | collective-permute-done | bytes 884768 | tf_op jit(solution)/shard_map/ppermute | solution.py:37
  301.2 1.7 collective-permute-done.27
  304.4 3.8 %collective-permute-done.13 = bf16[96,2304]{1,0:T(8,128)(2,1)S(1)} collective-permute-done((bf16[96,2304]{1,0:T(8,128)(2,1)S(1)}, bf16[96,2304]{1,0:T(8,128)(2,1)S(1)}, u32[]{:S(2)}, u32[]{:S(2)}) %collective-permute-start.13) | collective-permute-done | bytes 442400 | tf_op jit(solution)/shard_map/ppermute | solution.py:37
  308.4 1.8 collective-permute-start.14
  310.1 2.8 collective-permute-done.28
  313.1 2.6 collective-permute-done.14
  316.1 11.0 %collective-permute-done.29 = bf16[48,2304]{1,0:T(8,128)(2,1)S(1)} collective-permute-done((bf16[48,2304]{1,0:T(8,128)(2,1)S(1)}, bf16[48,2304]{1,0:T(8,128)(2,1)S(1)}, u32[]{:S(2)}, u32[]{:S(2)}) %collective-permute-start.29) | collective-permute-done | bytes 221216 | tf_op jit(solution)/shard_map/ppermute | solution.py:37
  330.5 4.2 %collective-permute-done.30 = bf16[48,2304]{1,0:T(8,128)(2,1)S(1)} collective-permute-done((bf16[48,2304]{1,0:T(8,128)(2,1)S(1)}, bf16[48,2304]{1,0:T(8,128)(2,1)S(1)}, u32[]{:S(2)}, u32[]{:S(2)}) %collective-permute-start.30) | collective-permute-done | bytes 221216 | tf_op jit(solution)/shard_map/ppermute | solution.py:37
  338.0 8.0 %collective-permute-done.31 = bf16[96,2304]{1,0:T(8,128)(2,1)S(1)} collective-permute-done((bf16[96,2304]{1,0:T(8,128)(2,1)S(1)}, bf16[96,2304]{1,0:T(8,128)(2,1)S(1)}, u32[]{:S(2)}, u32[]{:S(2)}) %collective-permute-start.31) | collective-permute-done | bytes 442400 | tf_op jit(solution)/shard_map/ppermute | solution.py:37
  347.5 3.3 collective-permute-done.17
  (164 shorter events, 42.8 us)
Async XLA Ops:
  7.2 35.9 %all-gather.5.cloned.1.call-start = ((), (), s32[]{:S(2)}) async-start(), calls=%async_computation | async-start | bytes 4423680 | tf_op jit(solution)/shard_map/all_gather | solution.py:345
  7.9 74.9 %all-gather.7.cloned.1.call-start = ((), (), s32[]{:S(2)}) async-start(), calls=%async_computation.1 | async-start | bytes 1474560 | tf_op jit(solution)/shard_map/all_gather | solution.py:346
  8.7 75.8 %all-gather.11.cloned.1.call-start = ((), (), s32[]{:S(2)}) async-start(), calls=%async_computation.3 | async-start | bytes 2211840 | tf_op jit(solution)/shard_map/all_gather | solution.py:348
  9.4 107.3 %all-gather.9.cloned.1.call-start = ((), (), s32[]{:S(2)}) async-start(), calls=%async_computation.2 | async-start | bytes 4423680 | tf_op jit(solution)/shard_map/all_gather | solution.py:347
  10.0 3.8 %collective-permute-start = (bf16[1,192,2]{1,2,0:T(2,128)(2,1)S(1)}, bf16[1,192,2]{1,2,0:T(2,128)(2,1)S(1)}, u32[]{:S(2)}, u32[]{:S(2)}) collective-permute-start(bf16[1,192,2]{1,2,0:T(2,128)(2,1)S(1)} %maximum_bitcast_fusion), channel_id=1, source_target_pairs={{0,1},{1,0},{2,3},{3,2},{4,5},{5,4},{6,7},{7,6},{8,9},{9,8},{10,11... | collective-permute-start | bytes 2312 | tf_op jit(solution)/shard_map/ppermute | solution.py:37
  13.8 38.0 %copy-start = (f32[1024,128]{1,0:T(8,128)}, f32[1024,128]{1,0:T(8,128)S(1)}, u32[]{:S(2)}) copy-start(f32[1024,128]{1,0:T(8,128)S(1)} %get-tuple-element.52.high_ref) | copy-start | bytes 1572868
  13.9 4.1 %collective-permute-start.1 = (bf16[2,192,2]{1,2,0:T(2,128)(2,1)S(1)}, bf16[2,192,2]{1,2,0:T(2,128)(2,1)S(1)}, u32[]{:S(2)}, u32[]{:S(2)}) collective-permute-start(bf16[2,192,2]{1,2,0:T(2,128)(2,1)S(1)} %pad_maximum_fusion.7), channel_id=1, source_target_pairs={{0,2},{1,3},{2,0},{3,1},{4,6},{5,7},{6,4},{7,5},{8,10},{9,11},{10,... | collective-permute-start | bytes 4616 | tf_op jit(solution)/shard_map/ppermute | solution.py:37
  43.1 13.3 %copy-start.6 = (s32[1,2]{1,0:T(1,128)S(1)}, s32[1,2]{1,0:T(1,128)}, u32[]{:S(2)}) copy-start(s32[1,2]{1,0:T(1,128)} %param.16) | copy-start | bytes 28
  52.9 8.0 %collective-permute-start.2 = (bf16[64,1536]{1,0:T(8,128)(2,1)S(1)}, bf16[64,1536]{1,0:T(8,128)(2,1)S(1)}, u32[]{:S(2)}, u32[]{:S(2)}) collective-permute-start(bf16[64,1536]{1,0:T(8,128)(2,1)S(1)} %get-tuple-element.47), channel_id=1, source_target_pairs={{0,4},{4,8},{8,12},{12,16},{16,20},{20,24},{24,28},{1,5},{5,9},{9,... | collective-permute-start | bytes 589832 | tf_op jit(solution)/shard_map/ppermute | solution.py:24
  58.3 8.7 %collective-permute-start.3 = (bf16[64,1536]{1,0:T(8,128)(2,1)S(1)}, bf16[64,1536]{1,0:T(8,128)(2,1)S(1)}, u32[]{:S(2)}, u32[]{:S(2)}) collective-permute-start(bf16[64,1536]{1,0:T(8,128)(2,1)S(1)} %get-tuple-element.46), channel_id=1, source_target_pairs={{4,0},{8,4},{12,8},{16,12},{20,16},{24,20},{28,24},{5,1},{9,5},{13... | collective-permute-start | bytes 589832 | tf_op jit(solution)/shard_map/ppermute | solution.py:25
  118.0 25.6 %copy-start.7 = (bf16[1,1024,768]{2,1,0:T(8,128)(2,1)S(1)}, bf16[1,1024,768]{2,1,0:T(8,128)(2,1)}, u32[]{:S(2)}) copy-start(bf16[1,1024,768]{2,1,0:T(8,128)(2,1)} %param.17) | copy-start | bytes 4718596
  149.5 94.8 %collective-permute-start.32 = (bf16[2,288,768]{2,1,0:T(8,128)(2,1)}, bf16[2,288,768]{2,1,0:T(8,128)(2,1)}, u32[]{:S(2)}, u32[]{:S(2)}) collective-permute-start(bf16[2,288,768]{2,1,0:T(8,128)(2,1)} %dynamic-slice_bitcast_fusion.2), channel_id=1, source_target_pairs={{0,1},{1,0},{2,3},{3,2},{4,5},{5,4},{6,7},{7,6},{8,9},{9,8},{10,11... | collective-permute-start | bytes 2654216 | tf_op jit(solution)/shard_map/ppermute | solution.py:37
  188.9 8.4 %collective-permute-start.4 = (bf16[64,1536]{1,0:T(8,128)(2,1)S(1)}, bf16[64,1536]{1,0:T(8,128)(2,1)S(1)}, u32[]{:S(2)}, u32[]{:S(2)}) collective-permute-start(bf16[64,1536]{1,0:T(8,128)(2,1)S(1)} %get-tuple-element.45), channel_id=1, source_target_pairs={{0,4},{4,8},{8,12},{12,16},{16,20},{20,24},{24,28},{1,5},{5,9},{9,... | collective-permute-start | bytes 589832 | tf_op jit(solution)/shard_map/ppermute | solution.py:33
  192.3 8.7 %collective-permute-start.5 = (bf16[64,1536]{1,0:T(8,128)(2,1)S(1)}, bf16[64,1536]{1,0:T(8,128)(2,1)S(1)}, u32[]{:S(2)}, u32[]{:S(2)}) collective-permute-start(bf16[64,1536]{1,0:T(8,128)(2,1)S(1)} %get-tuple-element.44), channel_id=1, source_target_pairs={{4,0},{8,4},{12,8},{16,12},{20,16},{24,20},{28,24},{5,1},{9,5},{13... | collective-permute-start | bytes 589832 | tf_op jit(solution)/shard_map/ppermute | solution.py:33
  193.9 7.1 %copy-start.1 = (f32[1024,128]{1,0:T(8,128)S(1)}, f32[1024,128]{1,0:T(8,128)}, u32[]{:S(2)}) copy-start(f32[1024,128]{1,0:T(8,128)} %copy-done) | copy-start | bytes 1572868
  214.0 1.2 collective-permute-start.6
  214.0 17.4 %slice-start = ((s8[4718592]{0:T(1024)(128)(4,1)}), s8[4194304]{0:T(1024)(128)(4,1)S(1)}, s32[]{:S(2)}) async-start(s8[4718592]{0:T(1024)(128)(4,1)} %bitcast.95), calls=%async_computation.4 | async-start | bytes 8388608
  214.1 15.6 %collective-permute-start.18 = (bf16[2,192,768]{2,1,0:T(8,128)(2,1)S(1)}, bf16[2,192,768]{2,1,0:T(8,128)(2,1)S(1)}, u32[]{:S(2)}, u32[]{:S(2)}) collective-permute-start(bf16[2,192,768]{2,1,0:T(8,128)(2,1)S(1)} %dynamic-slice_bitcast_fusion.3), channel_id=1, source_target_pairs={{0,1},{1,0},{2,3},{3,2},{4,5},{5,4},{6,7},{7,6},{8,9},{9,8},{10,11... | collective-permute-start | bytes 1769480 | tf_op jit(solution)/shard_map/ppermute | solution.py:37
  215.2 7.4 %collective-permute-start.7 = (f32[1,2,192]{2,0,1:T(1,128)S(1)}, f32[1,2,192]{2,0,1:T(1,128)S(1)}, u32[]{:S(2)}, u32[]{:S(2)}) collective-permute-start(f32[1,2,192]{2,0,1:T(1,128)S(1)} %constant_dynamic-slice_fusion.7), channel_id=1, source_target_pairs={{0,2},{1,3},{2,0},{3,1},{4,6},{5,7},{6,4},{7,5},{8,10},{9,11},{10,... | collective-permute-start | bytes 4616 | tf_op jit(solution)/shard_map/ppermute | solution.py:37
  215.8 15.6 %slice-start.1 = ((s8[4718592]{0:T(1024)(128)(4,1)}), s8[524288]{0:T(1024)(128)(4,1)S(1)}, s32[]{:S(2)}) async-start(s8[4718592]{0:T(1024)(128)(4,1)} %bitcast.95), calls=%async_computation.5 | async-start | bytes 1048576
  222.6 4.2 %collective-permute-start.8 = (f32[2,192]{1,0:T(2,128)S(1)}, f32[2,192]{1,0:T(2,128)S(1)}, u32[]{:S(2)}, u32[]{:S(2)}) collective-permute-start(f32[2,192]{1,0:T(2,128)S(1)} %bitcast.92), channel_id=1, source_target_pairs={{0,4},{4,0},{8,12},{12,8},{16,20},{20,16},{24,28},{28,24},{1,5},{5... | collective-permute-start | bytes 4616 | tf_op jit(solution)/shard_map/ppermute | solution.py:37
  225.4 41.5 %collective-permute-start.25 = (bf16[2,192,2304]{2,1,0:T(8,128)(2,1)S(1)}, bf16[2,192,2304]{2,1,0:T(8,128)(2,1)S(1)}, u32[]{:S(2)}, u32[]{:S(2)}) collective-permute-start(bf16[2,192,2304]{2,1,0:T(8,128)(2,1)S(1)} %dynamic-slice_bitcast_fusion), channel_id=1, source_target_pairs={{0,1},{1,0},{2,3},{3,2},{4,5},{5,4},{6,7},{7,6},{8,9},{9,8},{10,11... | collective-permute-start | bytes 5308424 | tf_op jit(solution)/shard_map/ppermute | solution.py:37
  226.8 9.0 %collective-permute-start.9 = (f32[2,192]{1,0:T(2,128)S(1)}, f32[2,192]{1,0:T(2,128)S(1)}, u32[]{:S(2)}, u32[]{:S(2)}) collective-permute-start(f32[2,192]{1,0:T(2,128)S(1)} %fusion.5), channel_id=1, source_target_pairs={{0,8},{4,12},{8,0},{12,4},{16,24},{20,28},{24,16},{28,20},{1,9},{5... | collective-permute-start | bytes 4616 | tf_op jit(solution)/shard_map/ppermute | solution.py:37
  229.9 8.4 %collective-permute-start.19 = (bf16[1,192,768]{2,1,0:T(8,128)(2,1)S(1)}, bf16[1,192,768]{2,1,0:T(8,128)(2,1)S(1)}, u32[]{:S(2)}, u32[]{:S(2)}) collective-permute-start(bf16[1,192,768]{2,1,0:T(8,128)(2,1)S(1)} %constant_dynamic-slice_fusion.4), channel_id=1, source_target_pairs={{0,2},{1,3},{2,0},{3,1},{4,6},{5,7},{6,4},{7,5},{8,10},{9,11},{10,... | collective-permute-start | bytes 884744 | tf_op jit(solution)/shard_map/ppermute | solution.py:37
  235.8 4.5 %collective-permute-start.10 = (f32[2,192]{1,0:T(2,128)S(1)}, f32[2,192]{1,0:T(2,128)S(1)}, u32[]{:S(2)}, u32[]{:S(2)}) collective-permute-start(f32[2,192]{1,0:T(2,128)S(1)} %add.152), channel_id=1, source_target_pairs={{0,16},{4,20},{8,24},{12,28},{16,0},{20,4},{24,8},{28,12},{1,17},{... | collective-permute-start | bytes 4616 | tf_op jit(solution)/shard_map/ppermute | solution.py:37
  238.4 5.2 %collective-permute-start.20 = (bf16[96,768]{1,0:T(8,128)(2,1)S(1)}, bf16[96,768]{1,0:T(8,128)(2,1)S(1)}, u32[]{:S(2)}, u32[]{:S(2)}) collective-permute-start(bf16[96,768]{1,0:T(8,128)(2,1)S(1)} %dynamic-slice_bitcast_fusion.7), channel_id=1, source_target_pairs={{0,4},{4,0},{8,12},{12,8},{16,20},{20,16},{24,28},{28,24},{1,5},{5... | collective-permute-start | bytes 442376 | tf_op jit(solution)/shard_map/ppermute | solution.py:37
  238.6 35.9 %collective-permute-start.11 = (bf16[2,192,2304]{2,1,0:T(8,128)(2,1)S(1)}, bf16[2,192,2304]{2,1,0:T(8,128)(2,1)S(1)}, u32[]{:S(2)}, u32[]{:S(2)}) collective-permute-start(bf16[2,192,2304]{2,1,0:T(8,128)(2,1)S(1)} %dynamic-slice_bitcast_fusion.1), channel_id=1, source_target_pairs={{0,1},{1,0},{2,3},{3,2},{4,5},{5,4},{6,7},{7,6},{8,9},{9,8},{10,11... | collective-permute-start | bytes 5308424 | tf_op jit(solution)/shard_map/ppermute | solution.py:37
  243.6 4.5 %collective-permute-start.21 = (bf16[48,768]{1,0:T(8,128)(2,1)S(1)}, bf16[48,768]{1,0:T(8,128)(2,1)S(1)}, u32[]{:S(2)}, u32[]{:S(2)}) collective-permute-start(bf16[48,768]{1,0:T(8,128)(2,1)S(1)} %constant_dynamic-slice_fusion.3), channel_id=1, source_target_pairs={{0,8},{4,12},{8,0},{12,4},{16,24},{20,28},{24,16},{28,20},{1,9},{5... | collective-permute-start | bytes 221192 | tf_op jit(solution)/shard_map/ppermute | solution.py:37
  248.1 6.1 %collective-permute-start.22 = (bf16[48,768]{1,0:T(8,128)(2,1)S(1)}, bf16[48,768]{1,0:T(8,128)(2,1)S(1)}, u32[]{:S(2)}, u32[]{:S(2)}) collective-permute-start(bf16[48,768]{1,0:T(8,128)(2,1)S(1)} %dynamic-slice_add_fusion.6), channel_id=1, source_target_pairs={{0,16},{4,20},{8,24},{12,28},{16,0},{20,4},{24,8},{28,12},{1,17},{... | collective-permute-start | bytes 221192 | tf_op jit(solution)/shard_map/ppermute | solution.py:37
  249.6 9.2 %collective-permute-start.33 = (bf16[1,288,768]{2,1,0:T(8,128)(2,1)S(1)}, bf16[1,288,768]{2,1,0:T(8,128)(2,1)S(1)}, u32[]{:S(2)}, u32[]{:S(2)}) collective-permute-start(bf16[1,288,768]{2,1,0:T(8,128)(2,1)S(1)} %constant_dynamic-slice_fusion), channel_id=1, source_target_pairs={{0,2},{1,3},{2,0},{3,1},{4,6},{5,7},{6,4},{7,5},{8,10},{9,11},{10,... | collective-permute-start | bytes 1327112 | tf_op jit(solution)/shard_map/ppermute | solution.py:37
  254.3 4.4 %collective-permute-start.23 = (bf16[48,768]{1,0:T(8,128)(2,1)S(1)}, bf16[48,768]{1,0:T(8,128)(2,1)S(1)}, u32[]{:S(2)}, u32[]{:S(2)}) collective-permute-start(bf16[48,768]{1,0:T(8,128)(2,1)S(1)} %add.165), channel_id=1, source_target_pairs={{0,8},{4,12},{8,0},{12,4},{16,24},{20,28},{24,16},{28,20},{1,9},{5... | collective-permute-start | bytes 221192 | tf_op jit(solution)/shard_map/ppermute | solution.py:37
  258.7 5.2 %collective-permute-start.24 = (bf16[96,768]{1,0:T(8,128)(2,1)S(1)}, bf16[96,768]{1,0:T(8,128)(2,1)S(1)}, u32[]{:S(2)}, u32[]{:S(2)}) collective-permute-start(bf16[96,768]{1,0:T(8,128)(2,1)S(1)} %pad_maximum_fusion.5), channel_id=1, source_target_pairs={{0,4},{4,0},{8,12},{12,8},{16,20},{20,16},{24,28},{28,24},{1,5},{5... | collective-permute-start | bytes 442376 | tf_op jit(solution)/shard_map/ppermute | solution.py:37
  258.9 7.4 %collective-permute-start.34 = (bf16[144,768]{1,0:T(8,128)(2,1)S(1)}, bf16[144,768]{1,0:T(8,128)(2,1)S(1)}, u32[]{:S(2)}, u32[]{:S(2)}) collective-permute-start(bf16[144,768]{1,0:T(8,128)(2,1)S(1)} %dynamic-slice_bitcast_fusion.6), channel_id=1, source_target_pairs={{0,4},{4,0},{8,12},{12,8},{16,20},{20,16},{24,28},{28,24},{1,5},{5... | collective-permute-start | bytes 663560 | tf_op jit(solution)/shard_map/ppermute | solution.py:37
  266.4 8.0 %collective-permute-start.35 = (bf16[144,768]{1,0:T(8,128)(2,1)S(1)}, bf16[144,768]{1,0:T(8,128)(2,1)S(1)}, u32[]{:S(2)}, u32[]{:S(2)}) collective-permute-start(bf16[144,768]{1,0:T(8,128)(2,1)S(1)} %bitcast_add_fusion.6), channel_id=1, source_target_pairs={{0,8},{4,12},{8,0},{12,4},{16,24},{20,28},{24,16},{28,20},{1,9},{5... | collective-permute-start | bytes 663560 | tf_op jit(solution)/shard_map/ppermute | solution.py:37
  267.2 22.6 %collective-permute-start.26 = (bf16[1,192,2304]{2,1,0:T(8,128)(2,1)S(1)}, bf16[1,192,2304]{2,1,0:T(8,128)(2,1)S(1)}, u32[]{:S(2)}, u32[]{:S(2)}) collective-permute-start(bf16[1,192,2304]{2,1,0:T(8,128)(2,1)S(1)} %constant_dynamic-slice_fusion.2), channel_id=1, source_target_pairs={{0,2},{1,3},{2,0},{3,1},{4,6},{5,7},{6,4},{7,5},{8,10},{9,11},{10,... | collective-permute-start | bytes 2654216 | tf_op jit(solution)/shard_map/ppermute | solution.py:37
  274.4 8.2 %collective-permute-start.36 = (bf16[144,768]{1,0:T(8,128)(2,1)S(1)}, bf16[144,768]{1,0:T(8,128)(2,1)S(1)}, u32[]{:S(2)}, u32[]{:S(2)}) collective-permute-start(bf16[144,768]{1,0:T(8,128)(2,1)S(1)} %add.175), channel_id=1, source_target_pairs={{0,16},{4,20},{8,24},{12,28},{16,0},{20,4},{24,8},{28,12},{1,17},{... | collective-permute-start | bytes 663560 | tf_op jit(solution)/shard_map/ppermute | solution.py:37
  274.8 24.9 %collective-permute-start.12 = (bf16[1,192,2304]{2,1,0:T(8,128)(2,1)S(1)}, bf16[1,192,2304]{2,1,0:T(8,128)(2,1)S(1)}, u32[]{:S(2)}, u32[]{:S(2)}) collective-permute-start(bf16[1,192,2304]{2,1,0:T(8,128)(2,1)S(1)} %constant_dynamic-slice_fusion.6), channel_id=1, source_target_pairs={{0,2},{1,3},{2,0},{3,1},{4,6},{5,7},{6,4},{7,5},{8,10},{9,11},{10,... | collective-permute-start | bytes 2654216 | tf_op jit(solution)/shard_map/ppermute | solution.py:37
  282.7 44.6 %collective-permute-start.37 = (bf16[144,768]{1,0:T(8,128)(2,1)S(1)}, bf16[144,768]{1,0:T(8,128)(2,1)S(1)}, u32[]{:S(2)}, u32[]{:S(2)}) collective-permute-start(bf16[144,768]{1,0:T(8,128)(2,1)S(1)} %add.176), channel_id=1, source_target_pairs={{0,4},{4,0},{8,12},{12,8},{16,20},{20,16},{24,28},{28,24},{1,5},{5... | collective-permute-start | bytes 663560 | tf_op jit(solution)/shard_map/ppermute | solution.py:37
  290.0 12.9 %collective-permute-start.27 = (bf16[96,2304]{1,0:T(8,128)(2,1)S(1)}, bf16[96,2304]{1,0:T(8,128)(2,1)S(1)}, u32[]{:S(2)}, u32[]{:S(2)}) collective-permute-start(bf16[96,2304]{1,0:T(8,128)(2,1)S(1)} %dynamic-slice_bitcast_fusion.4), channel_id=1, source_target_pairs={{0,4},{4,0},{8,12},{12,8},{16,20},{20,16},{24,28},{28,24},{1,5},{5... | collective-permute-start | bytes 1327112 | tf_op jit(solution)/shard_map/ppermute | solution.py:37
  299.8 8.4 %collective-permute-start.13 = (bf16[96,2304]{1,0:T(8,128)(2,1)S(1)}, bf16[96,2304]{1,0:T(8,128)(2,1)S(1)}, u32[]{:S(2)}, u32[]{:S(2)}) collective-permute-start(bf16[96,2304]{1,0:T(8,128)(2,1)S(1)} %dynamic-slice_bitcast_fusion.5), channel_id=1, source_target_pairs={{0,4},{4,0},{8,12},{12,8},{16,20},{20,16},{24,28},{28,24},{1,5},{5... | collective-permute-start | bytes 1327112 | tf_op jit(solution)/shard_map/ppermute | solution.py:37
  303.1 9.9 %collective-permute-start.28 = (bf16[48,2304]{1,0:T(8,128)(2,1)S(1)}, bf16[48,2304]{1,0:T(8,128)(2,1)S(1)}, u32[]{:S(2)}, u32[]{:S(2)}) collective-permute-start(bf16[48,2304]{1,0:T(8,128)(2,1)S(1)} %constant_dynamic-slice_fusion.1), channel_id=1, source_target_pairs={{0,8},{4,12},{8,0},{12,4},{16,24},{20,28},{24,16},{28,20},{1,9},{5... | collective-permute-start | bytes 663560 | tf_op jit(solution)/shard_map/ppermute | solution.py:37
  308.4 7.4 %collective-permute-start.14 = (bf16[48,2304]{1,0:T(8,128)(2,1)S(1)}, bf16[48,2304]{1,0:T(8,128)(2,1)S(1)}, u32[]{:S(2)}, u32[]{:S(2)}) collective-permute-start(bf16[48,2304]{1,0:T(8,128)(2,1)S(1)} %constant_dynamic-slice_fusion.5), channel_id=1, source_target_pairs={{0,8},{4,12},{8,0},{12,4},{16,24},{20,28},{24,16},{28,20},{1,9},{5... | collective-permute-start | bytes 663560 | tf_op jit(solution)/shard_map/ppermute | solution.py:37
  313.0 14.2 %collective-permute-start.29 = (bf16[48,2304]{1,0:T(8,128)(2,1)S(1)}, bf16[48,2304]{1,0:T(8,128)(2,1)S(1)}, u32[]{:S(2)}, u32[]{:S(2)}) collective-permute-start(bf16[48,2304]{1,0:T(8,128)(2,1)S(1)} %dynamic-slice_add_fusion.4), channel_id=1, source_target_pairs={{0,16},{4,20},{8,24},{12,28},{16,0},{20,4},{24,8},{28,12},{1,17},{... | collective-permute-start | bytes 663560 | tf_op jit(solution)/shard_map/ppermute | solution.py:37
  315.8 13.8 %collective-permute-start.15 = (bf16[48,2304]{1,0:T(8,128)(2,1)S(1)}, bf16[48,2304]{1,0:T(8,128)(2,1)S(1)}, u32[]{:S(2)}, u32[]{:S(2)}) collective-permute-start(bf16[48,2304]{1,0:T(8,128)(2,1)S(1)} %dynamic-slice_add_fusion.5), channel_id=1, source_target_pairs={{0,16},{4,20},{8,24},{12,28},{16,0},{20,4},{24,8},{28,12},{1,17},{... | collective-permute-start | bytes 663560 | tf_op jit(solution)/shard_map/ppermute | solution.py:37
  327.2 7.4 %collective-permute-start.30 = (bf16[48,2304]{1,0:T(8,128)(2,1)S(1)}, bf16[48,2304]{1,0:T(8,128)(2,1)S(1)}, u32[]{:S(2)}, u32[]{:S(2)}) collective-permute-start(bf16[48,2304]{1,0:T(8,128)(2,1)S(1)} %add.170), channel_id=1, source_target_pairs={{0,8},{4,12},{8,0},{12,4},{16,24},{20,28},{24,16},{28,20},{1,9},{5... | collective-permute-start | bytes 663560 | tf_op jit(solution)/shard_map/ppermute | solution.py:37
  329.6 7.4 %collective-permute-start.16 = (bf16[48,2304]{1,0:T(8,128)(2,1)S(1)}, bf16[48,2304]{1,0:T(8,128)(2,1)S(1)}, u32[]{:S(2)}, u32[]{:S(2)}) collective-permute-start(bf16[48,2304]{1,0:T(8,128)(2,1)S(1)} %add.160), channel_id=1, source_target_pairs={{0,8},{4,12},{8,0},{12,4},{16,24},{20,28},{24,16},{28,20},{1,9},{5... | collective-permute-start | bytes 663560 | tf_op jit(solution)/shard_map/ppermute | solution.py:37
  334.7 11.3 %collective-permute-start.31 = (bf16[96,2304]{1,0:T(8,128)(2,1)S(1)}, bf16[96,2304]{1,0:T(8,128)(2,1)S(1)}, u32[]{:S(2)}, u32[]{:S(2)}) collective-permute-start(bf16[96,2304]{1,0:T(8,128)(2,1)S(1)} %pad_maximum_fusion.4), channel_id=1, source_target_pairs={{0,4},{4,0},{8,12},{12,8},{16,20},{20,16},{24,28},{28,24},{1,5},{5... | collective-permute-start | bytes 1327112 | tf_op jit(solution)/shard_map/ppermute | solution.py:37
  337.1 13.7 %collective-permute-start.17 = (bf16[96,2304]{1,0:T(8,128)(2,1)S(1)}, bf16[96,2304]{1,0:T(8,128)(2,1)S(1)}, u32[]{:S(2)}, u32[]{:S(2)}) collective-permute-start(bf16[96,2304]{1,0:T(8,128)(2,1)S(1)} %pad_maximum_fusion.3), channel_id=1, source_target_pairs={{0,4},{4,0},{8,12},{12,8},{16,20},{20,16},{24,28},{28,24},{1,5},{5... | collective-permute-start | bytes 1327112 | tf_op jit(solution)/shard_map/ppermute | solution.py:37
  (7 other events, 21.7 us)
Sparse Core Ops, SparseCore 0:
  9.6 33.4 all-gather.4
  44.6 17.4 all-gather.6
  63.7 20.7 all-gather.10
  85.9 30.7 all-gather.8

commit v3 on v2

--- a/solution.py
+++ b/solution.py
@@ -1,3 +1,4 @@
+import functools
 import math
 
 import jax
@@ -41,49 +42,62 @@
     return [1 << b for b in range(lax.axis_size(axis).bit_length() - 1)]
 
 
-def gathered_small(shard, axis):
+def gathered_by_swaps(shard, axis):
+    size, me = lax.axis_size(axis), lax.axis_index(axis)
     parts = shard[None]
-    for bit in bits_of(axis):
+    for bit in reversed(bits_of(axis)):
         other = swap(parts, axis, bit)
+        upper = (me & bit) > 0
+        parts = jnp.stack(
+            [jnp.where(upper, other, parts), jnp.where(upper, parts, other)], axis=1
+        ).reshape((-1,) + shard.shape)
+    return parts.reshape((size * shard.shape[0],) + shard.shape[1:])
+
+
+def owner_step(term, axis, bit):
+    side = ((lax.axis_index(axis) & bit) > 0).astype(jnp.int32)
+    pairs = term.reshape((term.shape[0] // 2, 2) + term.shape[1:])
+    kept = lax.dynamic_index_in_dim(pairs, side, 1, keepdims=False)
+    sent = lax.dynamic_index_in_dim(pairs, 1 - side, 1, keepdims=False)
+    return kept + swap(sent, axis, bit)
+
+
+def sum_step(total, axis, bit, halved):
+    rows = total.shape[0]
+    if bit == bits_of(axis)[-1] or rows % 32:
+        return total + swap(total, axis, bit), halved
+    side = ((lax.axis_index(axis) & bit) > 0).astype(jnp.int32)
+    kept = lax.dynamic_slice_in_dim(total, side * (rows // 2), rows // 2, 0)
+    sent = lax.dynamic_slice_in_dim(total, (1 - side) * (rows // 2), rows // 2, 0)
+    return kept + swap(sent, axis, bit), halved + [bit]
+
+
+def summed(total, axis, done=0, halved=()):
+    halved = list(halved)
+    for bit in bits_of(axis)[done:]:
+        total, halved = sum_step(total, axis, bit, halved)
+    for bit in reversed(halved):
+        other = swap(total, axis, bit)
         upper = (lax.axis_index(axis) & bit) > 0
-        parts = jnp.concatenate(
-            [jnp.where(upper, other, parts), jnp.where(upper, parts, other)], axis=0
-        )
-    return parts.reshape((-1,) + shard.shape[1:])
-
-
-def reduced(term, owner_axis, sum_axis):
-    for bit in bits_of(owner_axis):
-        side = ((lax.axis_index(owner_axis) & bit) > 0).astype(jnp.int32)
-        pairs = term.reshape((term.shape[0] // 2, 2) + term.shape[1:])
-        kept = lax.dynamic_index_in_dim(pairs, side, 1, keepdims=False)
-        sent = lax.dynamic_index_in_dim(pairs, 1 - side, 1, keepdims=False)
-        term = kept + swap(sent, owner_axis, bit)
-    total = term[0]
-    halved = []
-    bits = bits_of(sum_axis)
-    for bit in bits:
-        rows = total.shape[0]
-        if bit != bits[-1] and rows % 32 == 0:
-            side = ((lax.axis_index(sum_axis) & bit) > 0).astype(jnp.int32)
-            kept = lax.dynamic_slice_in_dim(total, side * (rows // 2), rows // 2, 0)
-            sent = lax.dynamic_slice_in_dim(total, (1 - side) * (rows // 2), rows // 2, 0)
-            total = kept + swap(sent, sum_axis, bit)
-            halved.append(bit)
-        else:
-            total = total + swap(total, sum_axis, bit)
-    for bit in reversed(halved):
-        other = swap(total, sum_axis, bit)
-        upper = (lax.axis_index(sum_axis) & bit) > 0
         total = jnp.concatenate(
             [jnp.where(upper, other, total), jnp.where(upper, total, other)], axis=0
         )
     return total
 
 
-def total_of(grad):
+def reduced(term, owner_axis, sum_axis):
+    while term.shape[0] > 1:
+        bit = lax.axis_size(owner_axis) // term.shape[0]
+        term = owner_step(term, owner_axis, bit)
+    return summed(term[0], sum_axis)
+
+
+def term_of(grad):
     owners = lax.axis_size("wshard")
-    term = grad.astype(jnp.bfloat16).reshape(owners, grad.shape[0] // owners, grad.shape[1])
+    return grad.astype(jnp.bfloat16).reshape(owners, grad.shape[0] // owners, grad.shape[1])
+
+
+def total_of(term):
     return reduced(term, "wshard", "seq").astype(jnp.float32)
 
 
@@ -193,13 +207,15 @@
 
 
 def attend_back_kernel(
-    meta_ref, q_ref, go_ref, kv_ref, lse_ref, cos_ref, low_ref, high_ref, dq_ref, dkv_ref
+    group, meta_ref, q_ref, go_ref, k_ref, v_ref, lse_ref, cos_ref, low_ref, high_ref,
+    dq_ref, dk_ref, dv_ref,
 ):
     width = q_ref.shape[1]
 
     @pl.when(pl.program_id(0) == 0)
     def _():
-        dkv_ref[...] = jnp.zeros_like(dkv_ref)
+        dk_ref[...] = jnp.zeros_like(dk_ref)
+        dv_ref[...] = jnp.zeros_like(dv_ref)
 
     allowed = band_mask(meta_ref)
     lower = lower_lanes(QROWS)
@@ -208,15 +224,15 @@
     for c in range(0, width, LANES):
         q = q_ref[:, c : c + LANES]
         go = go_ref[:, c : c + LANES]
-        k = kv_ref[rows, c : c + LANES]
-        v = kv_ref[rows, width + c : width + c + LANES]
+        k = k_ref[rows, c : c + LANES]
+        v = v_ref[rows, c : c + LANES]
         dqs = []
         dk = dv = None
         for half in range(2):
             mine = lower if half == 0 else jnp.logical_not(lower)
             q_half = jnp.where(mine, q, jnp.zeros_like(q))
             go_half = jnp.where(mine, go, jnp.zeros_like(go))
-            head = c // HD + half
+            head = (group * width + c) // HD + half
             scores = mm(q_half, k, NT) * scale
             scores = jnp.where(allowed, scores, -1e30)
             probs = jnp.exp(scores - lse_ref[:, head : head + 1])
@@ -232,8 +248,8 @@
         dq_ref[:, c : c + LANES] = turn(
             dq, cos_ref[...], -low_ref[...], -high_ref[...]
         ).astype(jnp.bfloat16)
-        dkv_ref[rows, c : c + LANES] += dk * scale
-        dkv_ref[rows, width + c : width + c + LANES] += dv
+        dk_ref[rows, c : c + LANES] += dk * scale
+        dv_ref[rows, c : c + LANES] += dv
 
 
 def mlp_kernel(
@@ -275,17 +291,20 @@
 
 
 def last_kernel(
-    x_ref, gain_ref, w_ref, dq_ref, dkv_ref, prev_ref, next_ref, cos_ref, low_ref, high_ref,
-    gmid_ref, gp_ref, out_ref, ggain_ref,
+    x_ref, gain_ref, w_ref, dq0_ref, dq1_ref, dk0_ref, dk1_ref, dv0_ref, dv1_ref, prev_ref,
+    next_ref, cos_ref, low_ref, high_ref, gmid_ref, gp_ref, out_ref, ggain_ref,
 ):
     width = x_ref.shape[1]
     step = pl.program_id(0)
     start = pl.multiple_of(step * ROWS + HALF, HALF)
     first = (step == 0).astype(jnp.float32)
     last = (step == pl.num_programs(0) - 1).astype(jnp.float32)
-    gp_ref[:, :width] = dq_ref[...]
+    part = width // 2
+    gp_ref[:, :part] = dq0_ref[...]
+    gp_ref[:, part:width] = dq1_ref[...]
+    pieces = (dk0_ref, dk1_ref, dv0_ref, dv1_ref)
     for c in range(0, 2 * width, LANES):
-        own = dkv_ref[pl.ds(start, ROWS), c : c + LANES]
+        own = pieces[c // part][pl.ds(start, ROWS), c % part : c % part + LANES]
         top = own[:HALF] + prev_ref[:, c : c + LANES].astype(jnp.float32) * first
         low_end = own[ROWS - HALF :] + next_ref[:, c : c + LANES].astype(jnp.float32) * last
         chunk = jnp.concatenate([top, own[HALF : ROWS - HALF], low_end], axis=0)
@@ -310,6 +329,11 @@
 
 def run(body, steps, ins, outs, flops):
     def spec(array, rows):
+        if isinstance(rows, tuple):
+            rows, cols, place = rows
+            if rows is None:
+                return pl.BlockSpec((array.shape[0], cols), lambda i: (0, place))
+            return pl.BlockSpec((rows, cols), lambda i: (i, place))
         if rows == 0:
             return pl.BlockSpec(memory_space=pltpu.SMEM)
         if rows is None:
@@ -339,12 +363,13 @@
     offset = lax.axis_index("seq") * tokens
     shape = jax.ShapeDtypeStruct
     bf16, f32 = jnp.bfloat16, jnp.float32
-    gains_all = gathered_small(jnp.stack([gain_attn, gain_mlp], axis=1), "wshard")
+    gains_all = gathered_by_swaps(jnp.stack([gain_attn, gain_mlp], axis=1), "wshard")
     gain_a = gains_all[:, 0].astype(f32)[None]
     gain_m = gains_all[:, 1].astype(f32)[None]
     weight_qkv = lax.all_gather(w_qkv, "wshard", axis=0, tiled=True)
     weight_out = lax.all_gather(w_out, "wshard", axis=0, tiled=True)
-    weight_in = lax.all_gather(w_in, "wshard", axis=0, tiled=True)
+    weight_qkv, w_in = lax.optimization_barrier((weight_qkv, w_in))
+    weight_in = gathered_by_swaps(w_in, "wshard")
     weight_down = lax.all_gather(w_down, "wshard", axis=0, tiled=True)
     wide = weight_down.shape[0]
     stream = inputs[0]
@@ -367,7 +392,7 @@
             (shape((tokens, width), bf16), ROWS),
             (shape((tokens, 2 * width), bf16), ROWS),
         ],
-        6 * tokens * width * width,
+        18 * tokens * width * width,
     )
     kv_ext = extended_2(kv, (("seq", 0),), HALF)
     meta = jnp.stack([bounds[0, 0], bounds[0, 1], offset, jnp.int32(length)]).astype(jnp.int32)
@@ -376,7 +401,7 @@
         qsteps,
         [(meta, 0), (query, QROWS), (kv_ext, None)],
         [(shape((tokens, width), bf16), QROWS), (shape((tokens, LANES), f32), QROWS)],
-        16 * tokens * width * QROWS,
+        150 * tokens * width * QROWS,
     )
     output, normed2, hidden, grad_lifted, grad_middle, grad_mid_low, grad_att, grad_gain_m = run(
         mlp_kernel,
@@ -395,26 +420,48 @@
         ],
         4 * tokens * width * (width + 3 * wide),
     )
-    grad_w_down = mm(hidden, upstream, TN)
-    grad_w_in = mm(normed2, grad_lifted, TN)
-    grad_w_out = mm(attended, grad_mid_low, TN)
-    query_grad, kv_grad = run(
-        attend_back_kernel,
-        qsteps,
-        [(meta, 0), (query, QROWS), (grad_att, QROWS), (kv_ext, None), (lse, QROWS)]
-        + [(cos_t, QROWS), (low_t, QROWS), (high_t, QROWS)],
-        [
-            (shape((tokens, width), bf16), QROWS),
-            (shape((tokens + 2 * HALF, 2 * width), f32), None),
-        ],
-        40 * tokens * width * QROWS,
-    )
-    from_next = from_behind(kv_grad[:HALF].astype(bf16), "seq", -1)
-    from_prev = from_behind(kv_grad[tokens + HALF :].astype(bf16), "seq", 1)
+    terms = [
+        term_of(mm(normed2, grad_lifted, TN)),
+        term_of(mm(hidden, upstream, TN)),
+        term_of(mm(attended, grad_mid_low, TN)),
+    ]
+    grad_att, *terms = lax.optimization_barrier((grad_att, *terms))
+    part = width // 2
+    query_grads, key_grads, value_grads = [], [], []
+    for group in range(2):
+        dq, dk, dv = run(
+            functools.partial(attend_back_kernel, group),
+            qsteps,
+            [(meta, 0), (query, (QROWS, part, group)), (grad_att, (QROWS, part, group))]
+            + [(kv_ext, (None, part, group)), (kv_ext, (None, part, 2 + group)), (lse, QROWS)]
+            + [(cos_t, QROWS), (low_t, QROWS), (high_t, QROWS)],
+            [(shape((tokens, part), bf16), QROWS)]
+            + [(shape((tokens + 2 * HALF, part), f32), None)] * 2,
+            200 * tokens * width * QROWS,
+        )
+        query_grads.append(dq)
+        key_grads.append(dk)
+        value_grads.append(dv)
+        if group == 0:
+            terms = [owner_step(term, "wshard", 1) for term in terms]
+            dq, grad_att, *terms = lax.optimization_barrier((dq, grad_att, *terms))
+            query_grads[0] = dq
+    pieces = key_grads + value_grads
+    from_next = from_behind(
+        jnp.concatenate([piece[:HALF] for piece in pieces], axis=1).astype(bf16), "seq", -1
+    )
+    from_prev = from_behind(
+        jnp.concatenate([piece[tokens + HALF :] for piece in pieces], axis=1).astype(bf16), "seq", 1
+    )
+    terms = [owner_step(term, "wshard", 2)[0] for term in terms]
+    from_next, from_prev, *terms = lax.optimization_barrier((from_next, from_prev, *terms))
+    begun = [sum_step(term, "seq", 1, []) for term in terms]
     grad_projected, input_grad, grad_gain_a = run(
         last_kernel,
         steps,
-        [(stream, ROWS), (gain_a, None), (weight_qkv, None), (query_grad, ROWS), (kv_grad, None)]
+        [(stream, ROWS), (gain_a, None), (weight_qkv, None), (query_grads[0], ROWS)]
+        + [(query_grads[1], ROWS)]
+        + [(piece, None) for piece in pieces]
         + [(from_prev, None), (from_next, None)]
         + [(cos_t, ROWS), (low_t, ROWS), (high_t, ROWS), (grad_middle, ROWS)],
         [
@@ -422,8 +469,14 @@
             (shape((tokens, width), bf16), ROWS),
             (shape((1, width), f32), None),
         ],
-        6 * tokens * width * width,
-    )
+        18 * tokens * width * width,
+    )
+    grad_projected, *terms = lax.optimization_barrier(
+        (grad_projected, *[total for total, _ in begun])
+    )
+    sums = [
+        summed(term, "seq", 1, halved).astype(f32) for term, (_, halved) in zip(terms, begun)
+    ]
     grad_w_qkv = mm(normed, grad_projected, TN)
     output, input_grad = output[None], input_grad[None]
     owners = lax.axis_size("wshard")
@@ -436,11 +489,11 @@
         output,
         input_grad,
         gains[0],
-        total_of(grad_w_qkv),
-        total_of(grad_w_out),
+        total_of(term_of(grad_w_qkv)),
+        sums[2],
         gains[1],
-        total_of(grad_w_in),
-        total_of(grad_w_down),
+        sums[0],
+        sums[1],
     )
 
 

time: 359 us -> 327 us (0.911)
  waiting for transfers between devices: 161 us -> 102 us
  starting transfers between devices: 41.6 us -> 50.8 us
  other arithmetic: 15.9 us -> 24.4 us
  local copies, waits for them, and re-layouts: 10.6 us -> 17.5 us
    all_gather x1 -> x0, waiting for transfers between devices: 32.2 us -> none  [local(): weight_in = lax.all_gather(w_in, 'wshard', axis=0, tiled=True)]
    ppermute x34 -> x36, waiting for transfers between devices: 90.9 us -> 73.9 us  [swap(): lax.ppermute(shard, axis, [(i, i ^ bit) for i in range(lax.axis_size(axis...]
    ppermute x34 -> x36, starting transfers between devices: 31.7 us -> 40.8 us  [swap(): lax.ppermute(shard, axis, [(i, i ^ bit) for i in range(lax.axis_size(axis...]
    add x25 -> x22, other arithmetic: 2.79 us -> 8.15 us  [the longest x7 4.42 us: owner_step(): return kept + swap(sent, axis, bit)]
    ppermute x1, waiting for transfers between devices: 3.95 us -> 0.01 us  [extended_2(): after = lax.ppermute(leading, axis, down)]
    ppermute x2, waiting for transfers between devices: 3.68 us -> 0.01 us  [from_behind(): return lax.ppermute(shard, axis, pairs)]
    pallas_call x5 -> x6, Pallas kernels: 96.9 us -> 100 us  [run(): pl.pallas_call(body, grid=(steps,), in_specs=[spec(a, r) for a, r in ins]...]
  transfers between devices with their start and end apart: 42 -> 43, of which waited for: 30 -> 20; matrix products, arithmetic and copies ran while one was open for 10% -> 10% of each run, Pallas kernels for 20% -> 23%
where the time goes in v3:
time: 327 us; the launch traced here: 326 us
  waiting for transfers between devices  102 us (31%)
  Pallas kernels  100 us (31%)
  starting transfers between devices  50.8 us (16%)
  other arithmetic  24.4 us (7%)
  matrix products  17.6 us (5%)
  local copies, waits for them, and re-layouts  17.5 us (5%)
  between operations  14.5 us (4%)
    pallas_call x6, Pallas kernels, run(): pl.pallas_call(body, grid=(steps,), in_specs=[spec(a, r) for a, r in ins]...  100 us
    ppermute x36, waiting for transfers between devices, swap(): lax.ppermute(shard, axis, [(i, i ^ bit) for i in range(lax.axis_size(axis...  73.9 us
    ppermute x36, starting transfers between devices, swap(): lax.ppermute(shard, axis, [(i, i ^ bit) for i in range(lax.axis_size(axis...  40.8 us
    all_gather x1, waiting for transfers between devices, local(): weight_qkv = lax.all_gather(w_qkv, 'wshard', axis=0, tiled=True)  25.2 us
    dot_general x4, matrix products, mm(): return lax.dot_general(a, b, dims, preferred_element_type=jnp.float32)  17.6 us
  transfers between devices with their start and end apart: 43, of which 20 were waited for; matrix products, arithmetic and copies ran while one was open for 10% of the time, Pallas kernels for 23%

profile of v3, /device:TPU:0, one launch (start us, length us, event | category | flops | bytes accessed | tf_op | source)
XLA Modules:
  0.0 326.5 jit_solution(15650393850678918384)
XLA Ops:
  10.0 3.0 collective-permute-start
  13.1 1.9 multiply_sine_fusion
  17.8 25.2 %all-gather.4.cloned.1.call-done.w_ref = bf16[768,2304]{1,0:T(8,128)(2,1)} async-done(((bf16[192,2304]{1,0:T(8,128)(2,1)}), bf16[768,2304]{1,0:T(8,128)(2,1)}) %all-gather.4.cloned.1.call-update) | async-done | bytes 3538960 | tf_op jit(solution)/shard_map/all_gather | solution.py:369
  43.4 8.8 %shard_map.152 = (bf16[1024,768]{1,0:T(8,128)(2,1)}, bf16[1024,768]{1,0:T(8,128)(2,1)}, bf16[1024,1536]{1,0:T(8,128)(2,1)}) custom-call(bf16[1024,768]{1,0:T(8,128)(2,1)} %bitcast.136, f32[1,768]{1,0:T(1,128)S(1)} %get-tuple-element.130.gain_ref, bf16[768,2304]{1,0:T(8,128)(2,1)} %all-gather.4.cloned.1.call-done.w_ref, ...), custom_call_target="tpu_custom_call" | custom-call | flops 10871635968 | bytes 12979200 | tf_op jit(solution)/shard_map/pallas_call | solution.py:344
  53.2 3.6 %collective-permute-start.2 = (bf16[64,1536]{1,0:T(8,128)(2,1)S(1)}, bf16[64,1536]{1,0:T(8,128)(2,1)S(1)}, u32[]{:S(2)}, u32[]{:S(2)}) collective-permute-start(bf16[64,1536]{1,0:T(8,128)(2,1)S(1)} %get-tuple-element.95), channel_id=1, source_target_pairs={{0,4},{4,8},{8,12},{12,16},{16,20},{20,24},{24,28},{1,5},{5,9},{9,... | collective-permute-start | bytes 589832 | tf_op jit(solution)/shard_map/ppermute | solution.py:25
  61.2 10.0 %collective-permute-done.4 = bf16[1,192,2304]{2,1,0:T(8,128)(2,1)S(1)} collective-permute-done((bf16[1,192,2304]{2,1,0:T(8,128)(2,1)S(1)}, bf16[1,192,2304]{2,1,0:T(8,128)(2,1)S(1)}, u32[]{:S(2)}, u32[]{:S(2)}) %collective-permute-start.4) | collective-permute-done | bytes 884768 | tf_op jit(solution)/shard_map/ppermute | solution.py:38
  71.6 1.6 copy-done.3
  73.4 1.8 copy-done.9
  75.3 14.1 %shard_map.153 = (bf16[1024,768]{1,0:T(8,128)(2,1)}, f32[1024,128]{1,0:T(8,128)S(1)}) custom-call(s32[4]{0:T(128)S(1)} %pad_add_fusion.meta_ref, bf16[1024,768]{1,0:T(8,128)(2,1)} %get-tuple-element.51.q_ref, bf16[1152,1536]{1,0:T(8,128)(2,1)} %copy-done.9), custom_call_target="tpu_custom_call" | custom-call | flops 15099494400 | bytes 7208976 | tf_op jit(solution)/shard_map/pallas_call | solution.py:344
  89.9 2.0 copy.25
  93.2 25.6 %shard_map.154 = (bf16[1024,768]{1,0:T(8,128)(2,1)}, bf16[1024,768]{1,0:T(8,128)(2,1)}, bf16[1024,1152]{1,0:T(8,128)(2,1)}, bf16[1024,2304]{1,0:T(8,128)(2,1)}, ...) custom-call(bf16[1024,768]{1,0:T(8,128)(2,1)} %bitcast.137, ...), custom_call_target="tpu_custom_call" | custom-call | flops 13287555072 | bytes 27727872 | tf_op jit(solution)/shard_map/pallas_call | solution.py:344
  118.8 3.0 convolution_convert_fusion.3
  121.8 3.9 %convolution_convert_fusion.2 = bf16[1152,768]{1,0:T(8,128)(2,1)S(1)} fusion(bf16[1024,1152]{1,0:T(8,128)(2,1)} %get-tuple-element.59, bf16[1,1024,768]{2,1,0:T(8,128)(2,1)S(1)} %copy-done.11), kind=kOutput, calls=%fused_computation.3 | convolution fusion | flops 1812824064 | bytes 5701632 | tf_op jit(solution)/shard_map/dot_general | solution.py:119
  125.7 4.3 %convolution_convert_fusion.1 = bf16[768,2304]{1,0:T(8,128)(2,1)S(1)} fusion(bf16[1024,768]{1,0:T(8,128)(2,1)S(1)} %copy-done.14, bf16[1024,2304]{1,0:T(8,128)(2,1)S(1)} %bitcast.142), kind=kOutput, calls=%fused_computation.1 | convolution fusion | flops 3625648128 | bytes 9830400 | tf_op jit(solution)/shard_map/dot_general | solution.py:119
  132.2 19.4 %shard_map.155 = (bf16[1024,384]{1,0:T(8,128)(2,1)}, f32[1152,384]{1,0:T(8,128)}, f32[1152,384]{1,0:T(8,128)}) custom-call(s32[4]{0:T(128)S(1)} %pad_add_fusion.meta_ref, bf16[1024,768]{1,0:T(8,128)(2,1)} %get-tuple-element.51.q_ref, bf16[1024,768]{1,0:T(8,128)(2,1)} %get-tuple-element.68.go_ref, bf16[1152,1536]{1,0:T(8,128)(2,1)} %copy-done.9, ...), custom_call_target="tpu_custom_call" | custom-call | flops 20132659200 | bytes 16646160 | tf_op jit(solution)/shard_map/pallas_call | solution.py:344
  151.6 2.6 convert.26
  158.1 2.0 collective-permute-start.12
  160.3 19.4 %shard_map.156 = (bf16[1024,384]{1,0:T(8,128)(2,1)}, f32[1152,384]{1,0:T(8,128)}, f32[1152,384]{1,0:T(8,128)}) custom-call(s32[4]{0:T(128)S(1)} %pad_add_fusion.meta_ref, bf16[1024,768]{1,0:T(8,128)(2,1)} %get-tuple-element.51.q_ref, bf16[1024,768]{1,0:T(8,128)(2,1)} %get-tuple-element.68.go_ref, bf16[1152,1536]{1,0:T(8,128)(2,1)} %copy-done.9, ...), custom_call_target="tpu_custom_call" | custom-call | flops 20132659200 | bytes 16646160 | tf_op jit(solution)/shard_map/pallas_call | solution.py:344
  179.7 1.7 convert.27
  183.6 3.7 %collective-permute-start.10 = (bf16[64,1536]{1,0:T(8,128)(2,1)S(1)}, bf16[64,1536]{1,0:T(8,128)(2,1)S(1)}, u32[]{:S(2)}, u32[]{:S(2)}) collective-permute-start(bf16[64,1536]{1,0:T(8,128)(2,1)S(1)} %pad_maximum_fusion.7), channel_id=1, source_target_pairs={{0,4},{4,8},{8,12},{12,16},{16,20},{20,24},{24,28},{1,5},{5,9},{9,... | collective-permute-start | bytes 589832 | tf_op jit(solution)/shard_map/ppermute | solution.py:34
  188.7 7.1 %collective-permute-done.11 = bf16[1,192,2304]{2,1,0:T(8,128)(2,1)S(1)} collective-permute-done((bf16[1,192,2304]{2,1,0:T(8,128)(2,1)S(1)}, bf16[1,192,2304]{2,1,0:T(8,128)(2,1)S(1)}, u32[]{:S(2)}, u32[]{:S(2)}) %collective-permute-start.11) | collective-permute-done | bytes 884768 | tf_op jit(solution)/shard_map/ppermute | solution.py:38
  196.0 2.0 collective-permute-start.21
  198.2 2.0 collective-permute-start.19
  200.2 12.9 %shard_map.157 = (bf16[1024,2304]{1,0:T(8,128)(2,1)}, bf16[1024,768]{1,0:T(8,128)(2,1)}, f32[1,768]{1,0:T(1,128)S(1)}) custom-call(bf16[1024,768]{1,0:T(8,128)(2,1)} %bitcast.138, f32[1,768]{1,0:T(1,128)S(1)} %get-tuple-element.130.gain_ref, bf16[768,2304]{1,0:T(8,128)(2,1)} %all-gather.4.cloned.1.call-done.w_ref, ...), custom_call_target="tpu_custom_call" | custom-call | flops 10871635968 | bytes 25171968 | tf_op jit(solution)/shard_map/pallas_call | solution.py:344
  216.6 6.4 %convolution_convert_fusion = bf16[768,2304]{1,0:T(8,128)(2,1)S(1)} fusion(bf16[1024,768]{1,0:T(8,128)(2,1)S(1)} %copy-done.13, bf16[1024,2304]{1,0:T(8,128)(2,1)} %get-tuple-element.88), kind=kOutput, calls=%fused_computation | convolution fusion | flops 3625648128 | bytes 9830400 | tf_op jit(solution)/shard_map/dot_general | solution.py:119
  225.1 2.9 collective-permute-done.14
  228.6 3.1 collective-permute-done.15
  234.7 2.0 collective-permute-start.29
  236.7 1.8 collective-permute-start.17
  238.5 1.8 collective-permute-done.17
  240.3 2.7 collective-permute-start.18
  243.0 1.8 collective-permute-done.18
  245.8 2.8 collective-permute-start.30
  248.5 1.7 bitcast_add_fusion.1
  250.3 1.7 collective-permute-start.23
  256.3 5.1 %collective-permute-done.37 = bf16[144,768]{1,0:T(8,128)(2,1)S(1)} collective-permute-done((bf16[144,768]{1,0:T(8,128)(2,1)S(1)}, bf16[144,768]{1,0:T(8,128)(2,1)S(1)}, u32[]{:S(2)}, u32[]{:S(2)}) %collective-permute-start.37) | collective-permute-done | bytes 221216 | tf_op jit(solution)/shard_map/ppermute | solution.py:38
  262.2 1.8 collective-permute-start.32
  264.0 3.5 %collective-permute-done.23 = bf16[1,192,2304]{2,1,0:T(8,128)(2,1)S(1)} collective-permute-done((bf16[1,192,2304]{2,1,0:T(8,128)(2,1)S(1)}, bf16[1,192,2304]{2,1,0:T(8,128)(2,1)S(1)}, u32[]{:S(2)}, u32[]{:S(2)}) %collective-permute-start.23) | collective-permute-done | bytes 884768 | tf_op jit(solution)/shard_map/ppermute | solution.py:38
  267.7 1.8 collective-permute-start.24
  271.0 3.7 %collective-permute-done.38 = bf16[144,768]{1,0:T(8,128)(2,1)S(1)} collective-permute-done((bf16[144,768]{1,0:T(8,128)(2,1)S(1)}, bf16[144,768]{1,0:T(8,128)(2,1)S(1)}, u32[]{:S(2)}, u32[]{:S(2)}) %collective-permute-start.38) | collective-permute-done | bytes 221216 | tf_op jit(solution)/shard_map/ppermute | solution.py:38
  274.8 4.7 %collective-permute-start.39 = (bf16[144,768]{1,0:T(8,128)(2,1)S(1)}, bf16[144,768]{1,0:T(8,128)(2,1)S(1)}, u32[]{:S(2)}, u32[]{:S(2)}) collective-permute-start(bf16[144,768]{1,0:T(8,128)(2,1)S(1)} %add.176), channel_id=1, source_target_pairs={{0,4},{4,0},{8,12},{12,8},{16,20},{20,16},{24,28},{28,24},{1,5},{5... | collective-permute-start | bytes 663560 | tf_op jit(solution)/shard_map/ppermute | solution.py:38
  280.5 2.1 collective-permute-start.25
  282.5 5.9 %collective-permute-done.35 = bf16[48,2304]{1,0:T(8,128)(2,1)S(1)} collective-permute-done((bf16[48,2304]{1,0:T(8,128)(2,1)S(1)}, bf16[48,2304]{1,0:T(8,128)(2,1)S(1)}, u32[]{:S(2)}, u32[]{:S(2)}) %collective-permute-start.35) | collective-permute-done | bytes 221216 | tf_op jit(solution)/shard_map/ppermute | solution.py:38
  288.5 2.3 collective-permute-done.25
  291.2 1.6 collective-permute-start.36
  292.7 8.7 %collective-permute-done.26 = bf16[48,2304]{1,0:T(8,128)(2,1)S(1)} collective-permute-done((bf16[48,2304]{1,0:T(8,128)(2,1)S(1)}, bf16[48,2304]{1,0:T(8,128)(2,1)S(1)}, u32[]{:S(2)}, u32[]{:S(2)}) %collective-permute-start.26) | collective-permute-done | bytes 221216 | tf_op jit(solution)/shard_map/ppermute | solution.py:38
  302.6 5.4 %collective-permute-done.27 = bf16[48,2304]{1,0:T(8,128)(2,1)S(1)} collective-permute-done((bf16[48,2304]{1,0:T(8,128)(2,1)S(1)}, bf16[48,2304]{1,0:T(8,128)(2,1)S(1)}, u32[]{:S(2)}, u32[]{:S(2)}) %collective-permute-start.27) | collective-permute-done | bytes 221216 | tf_op jit(solution)/shard_map/ppermute | solution.py:38
  309.7 8.8 %collective-permute-done.28 = bf16[96,2304]{1,0:T(8,128)(2,1)S(1)} collective-permute-done((bf16[96,2304]{1,0:T(8,128)(2,1)S(1)}, bf16[96,2304]{1,0:T(8,128)(2,1)S(1)}, u32[]{:S(2)}, u32[]{:S(2)}) %collective-permute-start.28) | collective-permute-done | bytes 442400 | tf_op jit(solution)/shard_map/ppermute | solution.py:38
  (186 shorter events, 46.3 us)
Async XLA Ops:
  7.2 35.9 %all-gather.4.cloned.1.call-start = ((), (), s32[]{:S(2)}) async-start(), calls=%async_computation | async-start | bytes 4423680 | tf_op jit(solution)/shard_map/all_gather | solution.py:369
  7.9 84.0 %all-gather.6.cloned.1.call-start = ((), (), s32[]{:S(2)}) async-start(), calls=%async_computation.1 | async-start | bytes 1474560 | tf_op jit(solution)/shard_map/all_gather | solution.py:370
  8.7 83.2 %all-gather.8.cloned.1.call-start = ((), (), s32[]{:S(2)}) async-start(), calls=%async_computation.2 | async-start | bytes 2211840 | tf_op jit(solution)/shard_map/all_gather | solution.py:373
  10.0 6.4 %collective-permute-start = (bf16[1,192,2]{1,2,0:T(2,128)(2,1)S(1)}, bf16[1,192,2]{1,2,0:T(2,128)(2,1)S(1)}, u32[]{:S(2)}, u32[]{:S(2)}) collective-permute-start(bf16[1,192,2]{1,2,0:T(2,128)(2,1)S(1)} %maximum_bitcast_fusion.2), channel_id=1, source_target_pairs={{0,2},{1,3},{2,0},{3,1},{4,6},{5,7},{6,4},{7,5},{8,10},{9,11},{10,... | collective-permute-start | bytes 2312 | tf_op jit(solution)/shard_map/ppermute | solution.py:38
  15.0 28.0 %copy-start.8 = (bf16[192,2304]{1,0:T(8,128)(2,1)S(1)}, bf16[192,2304]{1,0:T(8,128)(2,1)}, u32[]{:S(2)}) copy-start(bf16[192,2304]{1,0:T(8,128)(2,1)} %param.14) | copy-start | bytes 2654212
  15.9 36.2 %copy-start = (f32[1024,128]{1,0:T(8,128)}, f32[1024,128]{1,0:T(8,128)S(1)}, u32[]{:S(2)}) copy-start(f32[1024,128]{1,0:T(8,128)S(1)} %get-tuple-element.110.high_ref) | copy-start | bytes 1572868
  16.5 1.2 collective-permute-start.1
  43.1 28.1 %collective-permute-start.4 = (bf16[1,192,2304]{2,1,0:T(8,128)(2,1)S(1)}, bf16[1,192,2304]{2,1,0:T(8,128)(2,1)S(1)}, u32[]{:S(2)}, u32[]{:S(2)}) collective-permute-start(bf16[1,192,2304]{2,1,0:T(8,128)(2,1)S(1)} %bitcast.130), channel_id=1, source_target_pairs={{0,2},{1,3},{2,0},{3,1},{4,6},{5,7},{6,4},{7,5},{8,10},{9,11},{10,... | collective-permute-start | bytes 2654216 | tf_op jit(solution)/shard_map/ppermute | solution.py:38
  43.4 13.5 %copy-start.10 = (s32[1,2]{1,0:T(1,128)S(1)}, s32[1,2]{1,0:T(1,128)}, u32[]{:S(2)}) copy-start(s32[1,2]{1,0:T(1,128)} %param.16) | copy-start | bytes 28
  53.2 7.9 %collective-permute-start.2 = (bf16[64,1536]{1,0:T(8,128)(2,1)S(1)}, bf16[64,1536]{1,0:T(8,128)(2,1)S(1)}, u32[]{:S(2)}, u32[]{:S(2)}) collective-permute-start(bf16[64,1536]{1,0:T(8,128)(2,1)S(1)} %get-tuple-element.95), channel_id=1, source_target_pairs={{0,4},{4,8},{8,12},{12,16},{16,20},{20,24},{24,28},{1,5},{5,9},{9,... | collective-permute-start | bytes 589832 | tf_op jit(solution)/shard_map/ppermute | solution.py:25
  58.8 14.6 %collective-permute-start.3 = (bf16[64,1536]{1,0:T(8,128)(2,1)S(1)}, bf16[64,1536]{1,0:T(8,128)(2,1)S(1)}, u32[]{:S(2)}, u32[]{:S(2)}) collective-permute-start(bf16[64,1536]{1,0:T(8,128)(2,1)S(1)} %get-tuple-element.94), channel_id=1, source_target_pairs={{4,0},{8,4},{12,8},{16,12},{20,16},{24,20},{28,24},{5,1},{9,5},{13... | collective-permute-start | bytes 589832 | tf_op jit(solution)/shard_map/ppermute | solution.py:26
  71.5 17.8 %collective-permute-start.5 = (bf16[2,192,2304]{2,1,0:T(8,128)(2,1)S(1)}, bf16[2,192,2304]{2,1,0:T(8,128)(2,1)S(1)}, u32[]{:S(2)}, u32[]{:S(2)}) collective-permute-start(bf16[2,192,2304]{2,1,0:T(8,128)(2,1)S(1)} %maximum_bitcast_fusion), channel_id=1, source_target_pairs={{0,1},{1,0},{2,3},{3,2},{4,5},{5,4},{6,7},{7,6},{8,9},{9,8},{10,11... | collective-permute-start | bytes 5308424 | tf_op jit(solution)/shard_map/ppermute | solution.py:38
  93.2 25.6 %copy-start.12 = (bf16[1024,768]{1,0:T(8,128)(2,1)S(1)}, bf16[1024,768]{1,0:T(8,128)(2,1)}, u32[]{:S(2)}) copy-start(bf16[1024,768]{1,0:T(8,128)(2,1)} %get-tuple-element.53.att_ref) | copy-start | bytes 4718596
  130.1 25.1 %collective-permute-start.8 = (bf16[2,192,768]{2,1,0:T(8,128)(2,1)S(1)}, bf16[2,192,768]{2,1,0:T(8,128)(2,1)}, u32[]{:S(2)}, u32[]{:S(2)}) collective-permute-start(bf16[2,192,768]{2,1,0:T(8,128)(2,1)S(1)} %dynamic-slice_bitcast_fusion.3), channel_id=1, source_target_pairs={{0,1},{1,0},{2,3},{3,2},{4,5},{5,4},{6,7},{7,6},{8,9},{9,8},{10,11... | collective-permute-start | bytes 1769480 | tf_op jit(solution)/shard_map/ppermute | solution.py:38
  130.3 26.1 %collective-permute-start.7 = (bf16[2,288,768]{2,1,0:T(8,128)(2,1)S(1)}, bf16[2,288,768]{2,1,0:T(8,128)(2,1)}, u32[]{:S(2)}, u32[]{:S(2)}) collective-permute-start(bf16[2,288,768]{2,1,0:T(8,128)(2,1)S(1)} %dynamic-slice_bitcast_fusion.2), channel_id=1, source_target_pairs={{0,1},{1,0},{2,3},{3,2},{4,5},{5,4},{6,7},{7,6},{8,9},{9,8},{10,11... | collective-permute-start | bytes 2654216 | tf_op jit(solution)/shard_map/ppermute | solution.py:38
  132.1 25.5 %collective-permute-start.6 = (bf16[2,192,2304]{2,1,0:T(8,128)(2,1)}, bf16[2,192,2304]{2,1,0:T(8,128)(2,1)S(1)}, u32[]{:S(2)}, u32[]{:S(2)}) collective-permute-start(bf16[2,192,2304]{2,1,0:T(8,128)(2,1)} %dynamic-slice_bitcast_fusion.1), channel_id=1, source_target_pairs={{0,1},{1,0},{2,3},{3,2},{4,5},{5,4},{6,7},{7,6},{8,9},{9,8},{10,11... | collective-permute-start | bytes 5308424 | tf_op jit(solution)/shard_map/ppermute | solution.py:38
  157.9 30.6 %collective-permute-start.13 = (bf16[1,192,768]{2,1,0:T(8,128)(2,1)S(1)}, bf16[1,192,768]{2,1,0:T(8,128)(2,1)S(1)}, u32[]{:S(2)}, u32[]{:S(2)}) collective-permute-start(bf16[1,192,768]{2,1,0:T(8,128)(2,1)S(1)} %constant_dynamic-slice_fusion.11), channel_id=1, source_target_pairs={{0,2},{1,3},{2,0},{3,1},{4,6},{5,7},{6,4},{7,5},{8,10},{9,11},{10,... | collective-permute-start | bytes 884744 | tf_op jit(solution)/shard_map/ppermute | solution.py:38
  158.1 30.5 %collective-permute-start.12 = (bf16[1,288,768]{2,1,0:T(8,128)(2,1)S(1)}, bf16[1,288,768]{2,1,0:T(8,128)(2,1)S(1)}, u32[]{:S(2)}, u32[]{:S(2)}) collective-permute-start(bf16[1,288,768]{2,1,0:T(8,128)(2,1)S(1)} %constant_dynamic-slice_fusion.12), channel_id=1, source_target_pairs={{0,2},{1,3},{2,0},{3,1},{4,6},{5,7},{6,4},{7,5},{8,10},{9,11},{10,... | collective-permute-start | bytes 1327112 | tf_op jit(solution)/shard_map/ppermute | solution.py:38
  160.2 35.6 %collective-permute-start.11 = (bf16[1,192,2304]{2,1,0:T(8,128)(2,1)S(1)}, bf16[1,192,2304]{2,1,0:T(8,128)(2,1)S(1)}, u32[]{:S(2)}, u32[]{:S(2)}) collective-permute-start(bf16[1,192,2304]{2,1,0:T(8,128)(2,1)S(1)} %constant_dynamic-slice_fusion.13), channel_id=1, source_target_pairs={{0,2},{1,3},{2,0},{3,1},{4,6},{5,7},{6,4},{7,5},{8,10},{9,11},{10,... | collective-permute-start | bytes 2654216 | tf_op jit(solution)/shard_map/ppermute | solution.py:38
  183.6 12.3 %collective-permute-start.10 = (bf16[64,1536]{1,0:T(8,128)(2,1)S(1)}, bf16[64,1536]{1,0:T(8,128)(2,1)S(1)}, u32[]{:S(2)}, u32[]{:S(2)}) collective-permute-start(bf16[64,1536]{1,0:T(8,128)(2,1)S(1)} %pad_maximum_fusion.7), channel_id=1, source_target_pairs={{0,4},{4,8},{8,12},{12,16},{16,20},{20,24},{24,28},{1,5},{5,9},{9,... | collective-permute-start | bytes 589832 | tf_op jit(solution)/shard_map/ppermute | solution.py:34
  187.3 8.7 %collective-permute-start.9 = (bf16[64,1536]{1,0:T(8,128)(2,1)S(1)}, bf16[64,1536]{1,0:T(8,128)(2,1)S(1)}, u32[]{:S(2)}, u32[]{:S(2)}) collective-permute-start(bf16[64,1536]{1,0:T(8,128)(2,1)S(1)} %pad_maximum_fusion.6), channel_id=1, source_target_pairs={{4,0},{8,4},{12,8},{16,12},{20,16},{24,20},{28,24},{5,1},{9,5},{13... | collective-permute-start | bytes 589832 | tf_op jit(solution)/shard_map/ppermute | solution.py:34
  188.7 11.5 %copy-start.1 = (f32[1024,128]{1,0:T(8,128)S(1)}, f32[1024,128]{1,0:T(8,128)}, u32[]{:S(2)}) copy-start(f32[1024,128]{1,0:T(8,128)} %copy-done) | copy-start | bytes 1572868
  196.0 17.1 %collective-permute-start.21 = (bf16[96,768]{1,0:T(8,128)(2,1)S(1)}, bf16[96,768]{1,0:T(8,128)(2,1)S(1)}, u32[]{:S(2)}, u32[]{:S(2)}) collective-permute-start(bf16[96,768]{1,0:T(8,128)(2,1)S(1)} %constant_dynamic-slice_fusion.4), channel_id=1, source_target_pairs={{0,4},{4,0},{8,12},{12,8},{16,20},{20,16},{24,28},{28,24},{1,5},{5... | collective-permute-start | bytes 442376 | tf_op jit(solution)/shard_map/ppermute | solution.py:38
  198.0 15.8 %collective-permute-start.20 = (bf16[144,768]{1,0:T(8,128)(2,1)S(1)}, bf16[144,768]{1,0:T(8,128)(2,1)S(1)}, u32[]{:S(2)}, u32[]{:S(2)}) collective-permute-start(bf16[144,768]{1,0:T(8,128)(2,1)S(1)} %constant_dynamic-slice_fusion.5), channel_id=1, source_target_pairs={{0,4},{4,0},{8,12},{12,8},{16,20},{20,16},{24,28},{28,24},{1,5},{5... | collective-permute-start | bytes 663560 | tf_op jit(solution)/shard_map/ppermute | solution.py:38
  198.2 17.5 %collective-permute-start.19 = (bf16[96,2304]{1,0:T(8,128)(2,1)S(1)}, bf16[96,2304]{1,0:T(8,128)(2,1)S(1)}, u32[]{:S(2)}, u32[]{:S(2)}) collective-permute-start(bf16[96,2304]{1,0:T(8,128)(2,1)S(1)} %constant_dynamic-slice_fusion.6), channel_id=1, source_target_pairs={{0,4},{4,0},{8,12},{12,8},{16,20},{20,16},{24,28},{28,24},{1,5},{5... | collective-permute-start | bytes 1327112 | tf_op jit(solution)/shard_map/ppermute | solution.py:38
  224.3 24.2 %collective-permute-start.22 = (bf16[2,192,2304]{2,1,0:T(8,128)(2,1)}, bf16[2,192,2304]{2,1,0:T(8,128)(2,1)}, u32[]{:S(2)}, u32[]{:S(2)}) collective-permute-start(bf16[2,192,2304]{2,1,0:T(8,128)(2,1)} %dynamic-slice_bitcast_fusion), channel_id=1, source_target_pairs={{0,1},{1,0},{2,3},{3,2},{4,5},{5,4},{6,7},{7,6},{8,9},{9,8},{10,11... | collective-permute-start | bytes 5308424 | tf_op jit(solution)/shard_map/ppermute | solution.py:38
  224.6 3.5 %collective-permute-start.14 = (f32[2,2,192]{2,0,1:T(2,128)S(1)}, f32[2,2,192]{2,0,1:T(2,128)S(1)}, u32[]{:S(2)}, u32[]{:S(2)}) collective-permute-start(f32[2,2,192]{2,0,1:T(2,128)S(1)} %bitcast.131), channel_id=1, source_target_pairs={{0,1},{1,0},{2,3},{3,2},{4,5},{5,4},{6,7},{7,6},{8,9},{9,8},{10,11... | collective-permute-start | bytes 9224 | tf_op jit(solution)/shard_map/ppermute | solution.py:38
  228.0 3.7 %collective-permute-start.15 = (f32[1,2,192]{2,0,1:T(1,128)S(1)}, f32[1,2,192]{2,0,1:T(1,128)S(1)}, u32[]{:S(2)}, u32[]{:S(2)}) collective-permute-start(f32[1,2,192]{2,0,1:T(1,128)S(1)} %constant_dynamic-slice_fusion.7), channel_id=1, source_target_pairs={{0,2},{1,3},{2,0},{3,1},{4,6},{5,7},{6,4},{7,5},{8,10},{9,11},{10,... | collective-permute-start | bytes 4616 | tf_op jit(solution)/shard_map/ppermute | solution.py:38
  231.7 5.0 %collective-permute-start.16 = (f32[2,192]{1,0:T(2,128)S(1)}, f32[2,192]{1,0:T(2,128)S(1)}, u32[]{:S(2)}, u32[]{:S(2)}) collective-permute-start(f32[2,192]{1,0:T(2,128)S(1)} %bitcast.132), channel_id=1, source_target_pairs={{0,4},{4,0},{8,12},{12,8},{16,20},{20,16},{24,28},{28,24},{1,5},{5... | collective-permute-start | bytes 4616 | tf_op jit(solution)/shard_map/ppermute | solution.py:38
  234.7 10.1 %collective-permute-start.29 = (bf16[48,768]{1,0:T(8,128)(2,1)}, bf16[48,768]{1,0:T(8,128)(2,1)}, u32[]{:S(2)}, u32[]{:S(2)}) collective-permute-start(bf16[48,768]{1,0:T(8,128)(2,1)} %constant_dynamic-slice_fusion.1), channel_id=1, source_target_pairs={{0,8},{4,12},{8,0},{12,4},{16,24},{20,28},{24,16},{28,20},{1,9},{5... | collective-permute-start | bytes 221192 | tf_op jit(solution)/shard_map/ppermute | solution.py:38
  236.7 3.6 %collective-permute-start.17 = (f32[2,192]{1,0:T(2,128)S(1)}, f32[2,192]{1,0:T(2,128)S(1)}, u32[]{:S(2)}, u32[]{:S(2)}) collective-permute-start(f32[2,192]{1,0:T(2,128)S(1)} %fusion.9), channel_id=1, source_target_pairs={{0,8},{4,12},{8,0},{12,4},{16,24},{20,28},{24,16},{28,20},{1,9},{5... | collective-permute-start | bytes 4616 | tf_op jit(solution)/shard_map/ppermute | solution.py:38
  240.3 4.5 %collective-permute-start.18 = (f32[2,192]{1,0:T(2,128)S(1)}, f32[2,192]{1,0:T(2,128)S(1)}, u32[]{:S(2)}, u32[]{:S(2)}) collective-permute-start(f32[2,192]{1,0:T(2,128)S(1)} %add.158), channel_id=1, source_target_pairs={{0,16},{4,20},{8,24},{12,28},{16,0},{20,4},{24,8},{28,12},{1,17},{... | collective-permute-start | bytes 4616 | tf_op jit(solution)/shard_map/ppermute | solution.py:38
  245.8 8.3 %collective-permute-start.30 = (bf16[48,768]{1,0:T(8,128)(2,1)S(1)}, bf16[48,768]{1,0:T(8,128)(2,1)S(1)}, u32[]{:S(2)}, u32[]{:S(2)}) collective-permute-start(bf16[48,768]{1,0:T(8,128)(2,1)S(1)} %dynamic-slice_add_fusion.6), channel_id=1, source_target_pairs={{0,16},{4,20},{8,24},{12,28},{16,0},{20,4},{24,8},{28,12},{1,17},{... | collective-permute-start | bytes 221192 | tf_op jit(solution)/shard_map/ppermute | solution.py:38
  250.3 17.2 %collective-permute-start.23 = (bf16[1,192,2304]{2,1,0:T(8,128)(2,1)S(1)}, bf16[1,192,2304]{2,1,0:T(8,128)(2,1)S(1)}, u32[]{:S(2)}, u32[]{:S(2)}) collective-permute-start(bf16[1,192,2304]{2,1,0:T(8,128)(2,1)S(1)} %constant_dynamic-slice_fusion.3), channel_id=1, source_target_pairs={{0,2},{1,3},{2,0},{3,1},{4,6},{5,7},{6,4},{7,5},{8,10},{9,11},{10,... | collective-permute-start | bytes 2654216 | tf_op jit(solution)/shard_map/ppermute | solution.py:38
  252.6 8.8 %collective-permute-start.37 = (bf16[144,768]{1,0:T(8,128)(2,1)S(1)}, bf16[144,768]{1,0:T(8,128)(2,1)S(1)}, u32[]{:S(2)}, u32[]{:S(2)}) collective-permute-start(bf16[144,768]{1,0:T(8,128)(2,1)S(1)} %copy-done.7), channel_id=1, source_target_pairs={{0,8},{4,12},{8,0},{12,4},{16,24},{20,28},{24,16},{28,20},{1,9},{5... | collective-permute-start | bytes 663560 | tf_op jit(solution)/shard_map/ppermute | solution.py:38
  254.1 8.0 %collective-permute-start.31 = (bf16[48,768]{1,0:T(8,128)(2,1)S(1)}, bf16[48,768]{1,0:T(8,128)(2,1)S(1)}, u32[]{:S(2)}, u32[]{:S(2)}) collective-permute-start(bf16[48,768]{1,0:T(8,128)(2,1)S(1)} %add.172), channel_id=1, source_target_pairs={{0,8},{4,12},{8,0},{12,4},{16,24},{20,28},{24,16},{28,20},{1,9},{5... | collective-permute-start | bytes 221192 | tf_op jit(solution)/shard_map/ppermute | solution.py:38
  254.7 14.8 %collective-permute-start.33 = (bf16[48,2304]{1,0:T(8,128)(2,1)S(1)}, bf16[48,2304]{1,0:T(8,128)(2,1)S(1)}, u32[]{:S(2)}, u32[]{:S(2)}) collective-permute-start(bf16[48,2304]{1,0:T(8,128)(2,1)S(1)} %constant_dynamic-slice_fusion), channel_id=1, source_target_pairs={{0,8},{4,12},{8,0},{12,4},{16,24},{20,28},{24,16},{28,20},{1,9},{5... | collective-permute-start | bytes 663560 | tf_op jit(solution)/shard_map/ppermute | solution.py:38
  261.4 13.3 %collective-permute-start.38 = (bf16[144,768]{1,0:T(8,128)(2,1)S(1)}, bf16[144,768]{1,0:T(8,128)(2,1)S(1)}, u32[]{:S(2)}, u32[]{:S(2)}) collective-permute-start(bf16[144,768]{1,0:T(8,128)(2,1)S(1)} %add.175), channel_id=1, source_target_pairs={{0,16},{4,20},{8,24},{12,28},{16,0},{20,4},{24,8},{28,12},{1,17},{... | collective-permute-start | bytes 663560 | tf_op jit(solution)/shard_map/ppermute | solution.py:38
  262.2 7.9 %collective-permute-start.32 = (bf16[96,768]{1,0:T(8,128)(2,1)S(1)}, bf16[96,768]{1,0:T(8,128)(2,1)S(1)}, u32[]{:S(2)}, u32[]{:S(2)}) collective-permute-start(bf16[96,768]{1,0:T(8,128)(2,1)S(1)} %pad_maximum_fusion.8), channel_id=1, source_target_pairs={{0,4},{4,0},{8,12},{12,8},{16,20},{20,16},{24,28},{28,24},{1,5},{5... | collective-permute-start | bytes 442376 | tf_op jit(solution)/shard_map/ppermute | solution.py:38
  267.7 12.6 %collective-permute-start.24 = (bf16[96,2304]{1,0:T(8,128)(2,1)S(1)}, bf16[96,2304]{1,0:T(8,128)(2,1)S(1)}, u32[]{:S(2)}, u32[]{:S(2)}) collective-permute-start(bf16[96,2304]{1,0:T(8,128)(2,1)S(1)} %dynamic-slice_bitcast_fusion.4), channel_id=1, source_target_pairs={{0,4},{4,0},{8,12},{12,8},{16,20},{20,16},{24,28},{28,24},{1,5},{5... | collective-permute-start | bytes 1327112 | tf_op jit(solution)/shard_map/ppermute | solution.py:38
  269.5 10.6 %collective-permute-start.34 = (bf16[48,2304]{1,0:T(8,128)(2,1)S(1)}, bf16[48,2304]{1,0:T(8,128)(2,1)S(1)}, u32[]{:S(2)}, u32[]{:S(2)}) collective-permute-start(bf16[48,2304]{1,0:T(8,128)(2,1)S(1)} %dynamic-slice_add_fusion.2), channel_id=1, source_target_pairs={{0,16},{4,20},{8,24},{12,28},{16,0},{20,4},{24,8},{28,12},{1,17},{... | collective-permute-start | bytes 663560 | tf_op jit(solution)/shard_map/ppermute | solution.py:38
  274.8 26.8 %collective-permute-start.39 = (bf16[144,768]{1,0:T(8,128)(2,1)S(1)}, bf16[144,768]{1,0:T(8,128)(2,1)S(1)}, u32[]{:S(2)}, u32[]{:S(2)}) collective-permute-start(bf16[144,768]{1,0:T(8,128)(2,1)S(1)} %add.176), channel_id=1, source_target_pairs={{0,4},{4,0},{8,12},{12,8},{16,20},{20,16},{24,28},{28,24},{1,5},{5... | collective-permute-start | bytes 663560 | tf_op jit(solution)/shard_map/ppermute | solution.py:38
  280.2 8.2 %collective-permute-start.35 = (bf16[48,2304]{1,0:T(8,128)(2,1)S(1)}, bf16[48,2304]{1,0:T(8,128)(2,1)S(1)}, u32[]{:S(2)}, u32[]{:S(2)}) collective-permute-start(bf16[48,2304]{1,0:T(8,128)(2,1)S(1)} %add.174), channel_id=1, source_target_pairs={{0,8},{4,12},{8,0},{12,4},{16,24},{20,28},{24,16},{28,20},{1,9},{5... | collective-permute-start | bytes 663560 | tf_op jit(solution)/shard_map/ppermute | solution.py:38
  280.5 10.3 %collective-permute-start.25 = (bf16[48,2304]{1,0:T(8,128)(2,1)S(1)}, bf16[48,2304]{1,0:T(8,128)(2,1)S(1)}, u32[]{:S(2)}, u32[]{:S(2)}) collective-permute-start(bf16[48,2304]{1,0:T(8,128)(2,1)S(1)} %constant_dynamic-slice_fusion.2), channel_id=1, source_target_pairs={{0,8},{4,12},{8,0},{12,4},{16,24},{20,28},{24,16},{28,20},{1,9},{5... | collective-permute-start | bytes 663560 | tf_op jit(solution)/shard_map/ppermute | solution.py:38
  290.9 10.6 %collective-permute-start.26 = (bf16[48,2304]{1,0:T(8,128)(2,1)S(1)}, bf16[48,2304]{1,0:T(8,128)(2,1)S(1)}, u32[]{:S(2)}, u32[]{:S(2)}) collective-permute-start(bf16[48,2304]{1,0:T(8,128)(2,1)S(1)} %dynamic-slice_add_fusion.3), channel_id=1, source_target_pairs={{0,16},{4,20},{8,24},{12,28},{16,0},{20,4},{24,8},{28,12},{1,17},{... | collective-permute-start | bytes 663560 | tf_op jit(solution)/shard_map/ppermute | solution.py:38
  291.2 17.0 %collective-permute-start.36 = (bf16[96,2304]{1,0:T(8,128)(2,1)S(1)}, bf16[96,2304]{1,0:T(8,128)(2,1)S(1)}, u32[]{:S(2)}, u32[]{:S(2)}) collective-permute-start(bf16[96,2304]{1,0:T(8,128)(2,1)S(1)} %pad_maximum_fusion.5), channel_id=1, source_target_pairs={{0,4},{4,0},{8,12},{12,8},{16,20},{20,16},{24,28},{28,24},{1,5},{5... | collective-permute-start | bytes 1327112 | tf_op jit(solution)/shard_map/ppermute | solution.py:38
  301.5 6.6 %collective-permute-start.27 = (bf16[48,2304]{1,0:T(8,128)(2,1)S(1)}, bf16[48,2304]{1,0:T(8,128)(2,1)S(1)}, u32[]{:S(2)}, u32[]{:S(2)}) collective-permute-start(bf16[48,2304]{1,0:T(8,128)(2,1)S(1)} %add.170), channel_id=1, source_target_pairs={{0,8},{4,12},{8,0},{12,4},{16,24},{20,28},{24,16},{28,20},{1,9},{5... | collective-permute-start | bytes 663560 | tf_op jit(solution)/shard_map/ppermute | solution.py:38
  308.1 10.4 %collective-permute-start.28 = (bf16[96,2304]{1,0:T(8,128)(2,1)S(1)}, bf16[96,2304]{1,0:T(8,128)(2,1)S(1)}, u32[]{:S(2)}, u32[]{:S(2)}) collective-permute-start(bf16[96,2304]{1,0:T(8,128)(2,1)S(1)} %pad_maximum_fusion.4), channel_id=1, source_target_pairs={{0,4},{4,0},{8,12},{12,8},{16,20},{20,16},{24,28},{28,24},{1,5},{5... | collective-permute-start | bytes 1327112 | tf_op jit(solution)/shard_map/ppermute | solution.py:38
  (12 other events, 37.7 us)
Sparse Core Ops, SparseCore 0:
  9.6 33.4 all-gather.3
  44.6 23.8 all-gather.5
  70.1 20.7 all-gather.7

commit v4 on v3

--- a/solution.py
+++ b/solution.py
@@ -64,7 +64,7 @@
 
 def sum_step(total, axis, bit, halved):
     rows = total.shape[0]
-    if bit == bits_of(axis)[-1] or rows % 32:
+    if bit == bits_of(axis)[-1] or rows % 16:
         return total + swap(total, axis, bit), halved
     side = ((lax.axis_index(axis) & bit) > 0).astype(jnp.int32)
     kept = lax.dynamic_slice_in_dim(total, side * (rows // 2), rows // 2, 0)
@@ -95,6 +95,19 @@
 def term_of(grad):
     owners = lax.axis_size("wshard")
     return grad.astype(jnp.bfloat16).reshape(owners, grad.shape[0] // owners, grad.shape[1])
+
+
+def folded(term, columns):
+    times = columns // term.shape[2]
+    rows = term.shape[1] // times
+    parts = [term[:, j * rows : (j + 1) * rows] for j in range(times)]
+    return jnp.concatenate(parts, axis=2)
+
+
+def unfolded(total, columns):
+    return jnp.concatenate(
+        [total[:, j : j + columns] for j in range(0, total.shape[1], columns)], axis=0
+    )
 
 
 def total_of(term):
@@ -420,11 +433,11 @@
         ],
         4 * tokens * width * (width + 3 * wide),
     )
-    terms = [
-        term_of(mm(normed2, grad_lifted, TN)),
-        term_of(mm(hidden, upstream, TN)),
-        term_of(mm(attended, grad_mid_low, TN)),
-    ]
+    term_in = term_of(mm(normed2, grad_lifted, TN))
+    term_down = folded(term_of(mm(hidden, upstream, TN)), 2 * wide)
+    term_out = folded(term_of(mm(attended, grad_mid_low, TN)), 2 * wide)
+    in_rows, down_rows = term_in.shape[1], term_down.shape[1]
+    terms = [jnp.concatenate([term_in, term_down, term_out], axis=1)]
     grad_att, *terms = lax.optimization_barrier((grad_att, *terms))
     part = width // 2
     query_grads, key_grads, value_grads = [], [], []
@@ -477,6 +490,9 @@
     sums = [
         summed(term, "seq", 1, halved).astype(f32) for term, (_, halved) in zip(terms, begun)
     ]
+    sum_in = sums[0][:in_rows]
+    sum_down = unfolded(sums[0][in_rows : in_rows + down_rows], width)
+    sum_out = unfolded(sums[0][in_rows + down_rows :], width)
     grad_w_qkv = mm(normed, grad_projected, TN)
     output, input_grad = output[None], input_grad[None]
     owners = lax.axis_size("wshard")
@@ -490,10 +506,10 @@
         input_grad,
         gains[0],
         total_of(term_of(grad_w_qkv)),
-        sums[2],
+        sum_out,
         gains[1],
-        sums[0],
-        sums[1],
+        sum_in,
+        sum_down,
     )
 
 

time: 327 us -> 319 us (0.976)
  starting transfers between devices: 50.8 us -> 38.3 us
  local copies, waits for them, and re-layouts: 17.5 us -> 23.4 us
  other arithmetic: 24.4 us -> 20.5 us
    ppermute x36 -> x23, starting transfers between devices: 40.8 us -> 27.9 us  [swap(): lax.ppermute(shard, axis, [(i, i ^ bit) for i in range(lax.axis_size(axis...]
    unnamed x39 -> x47, local copies, waits for them, and re-layouts: 5.32 us -> 11.2 us
    ppermute x36 -> x23, waiting for transfers between devices: 73.9 us -> 77.3 us  [swap(): lax.ppermute(shard, axis, [(i, i ^ bit) for i in range(lax.axis_size(axis...]
  transfers between devices with their start and end apart: 43 -> 30, of which waited for: 20 -> 18; matrix products, arithmetic and copies ran while one was open for 10% -> 8% of each run, Pallas kernels for 23% -> 23%
where the time goes in v4:
time: 319 us; the launch traced here: 318 us
  waiting for transfers between devices  105 us (33%)
  Pallas kernels  100 us (31%)
  starting transfers between devices  38.3 us (12%)
  local copies, waits for them, and re-layouts  23.4 us (7%)
  other arithmetic  20.5 us (6%)
  matrix products  15.9 us (5%)
  between operations  14.4 us (5%)
    pallas_call x6, Pallas kernels, run(): pl.pallas_call(body, grid=(steps,), in_specs=[spec(a, r) for a, r in ins]...  100 us
    ppermute x23, waiting for transfers between devices, swap(): lax.ppermute(shard, axis, [(i, i ^ bit) for i in range(lax.axis_size(axis...  77.3 us
    ppermute x23, starting transfers between devices, swap(): lax.ppermute(shard, axis, [(i, i ^ bit) for i in range(lax.axis_size(axis...  27.9 us
    all_gather x1, waiting for transfers between devices, local(): weight_qkv = lax.all_gather(w_qkv, 'wshard', axis=0, tiled=True)  25.7 us
    dot_general x4, matrix products, mm(): return lax.dot_general(a, b, dims, preferred_element_type=jnp.float32)  15.9 us
    unnamed x47, local copies, waits for them, and re-layouts  11.2 us
  transfers between devices with their start and end apart: 30, of which 18 were waited for; matrix products, arithmetic and copies ran while one was open for 8% of the time, Pallas kernels for 23%

profile of v4, /device:TPU:0, one launch (start us, length us, event | category | flops | bytes accessed | tf_op | source)
XLA Modules:
  0.0 318.3 jit_solution(7691982547334424219)
XLA Ops:
  10.0 3.0 collective-permute-start
  13.1 1.9 multiply_sine_fusion
  17.4 25.7 %all-gather.4.cloned.1.call-done.w_ref = bf16[768,2304]{1,0:T(8,128)(2,1)} async-done(((bf16[192,2304]{1,0:T(8,128)(2,1)}), bf16[768,2304]{1,0:T(8,128)(2,1)}) %all-gather.4.cloned.1.call-update) | async-done | bytes 3538960 | tf_op jit(solution)/shard_map/all_gather | solution.py:382
  43.4 8.9 %shard_map.152 = (bf16[1024,768]{1,0:T(8,128)(2,1)}, bf16[1024,768]{1,0:T(8,128)(2,1)}, bf16[1024,1536]{1,0:T(8,128)(2,1)}) custom-call(bf16[1024,768]{1,0:T(8,128)(2,1)} %bitcast.113, f32[1,768]{1,0:T(1,128)S(1)} %get-tuple-element.120.gain_ref, bf16[768,2304]{1,0:T(8,128)(2,1)} %all-gather.4.cloned.1.call-done.w_ref, ...), custom_call_target="tpu_custom_call" | custom-call | flops 10871635968 | bytes 12979200 | tf_op jit(solution)/shard_map/pallas_call | solution.py:357
  53.3 3.6 %collective-permute-start.2 = (bf16[64,1536]{1,0:T(8,128)(2,1)S(1)}, bf16[64,1536]{1,0:T(8,128)(2,1)S(1)}, u32[]{:S(2)}, u32[]{:S(2)}) collective-permute-start(bf16[64,1536]{1,0:T(8,128)(2,1)S(1)} %get-tuple-element.79), channel_id=1, source_target_pairs={{0,4},{4,8},{8,12},{12,16},{16,20},{20,24},{24,28},{1,5},{5,9},{9,... | collective-permute-start | bytes 589832 | tf_op jit(solution)/shard_map/ppermute | solution.py:25
  61.3 9.9 %collective-permute-done.4 = bf16[1,192,2304]{2,1,0:T(8,128)(2,1)S(1)} collective-permute-done((bf16[1,192,2304]{2,1,0:T(8,128)(2,1)S(1)}, bf16[1,192,2304]{2,1,0:T(8,128)(2,1)S(1)}, u32[]{:S(2)}, u32[]{:S(2)}) %collective-permute-start.4) | collective-permute-done | bytes 884768 | tf_op jit(solution)/shard_map/ppermute | solution.py:38
  71.6 1.6 copy-done.7
  73.4 1.8 copy-done.12
  75.3 14.1 %shard_map.153 = (bf16[1024,768]{1,0:T(8,128)(2,1)}, f32[1024,128]{1,0:T(8,128)S(1)}) custom-call(s32[4]{0:T(128)S(1)} %pad_add_fusion.meta_ref, bf16[1024,768]{1,0:T(8,128)(2,1)} %get-tuple-element.43.q_ref, bf16[1152,1536]{1,0:T(8,128)(2,1)} %copy-done.12), custom_call_target="tpu_custom_call" | custom-call | flops 15099494400 | bytes 7208976 | tf_op jit(solution)/shard_map/pallas_call | solution.py:357
  89.9 2.0 copy.21
  93.2 25.6 %shard_map.154 = (bf16[1024,768]{1,0:T(8,128)(2,1)}, bf16[1024,768]{1,0:T(8,128)(2,1)}, bf16[1024,1152]{1,0:T(8,128)(2,1)}, bf16[1024,2304]{1,0:T(8,128)(2,1)}, ...) custom-call(bf16[1024,768]{1,0:T(8,128)(2,1)} %bitcast.114, ...), custom_call_target="tpu_custom_call" | custom-call | flops 13287555072 | bytes 27727872 | tf_op jit(solution)/shard_map/pallas_call | solution.py:357
  118.8 3.9 %convolution_convert_fusion.2 = bf16[1152,768]{1,0:T(8,128)(2,1)S(1)} fusion(bf16[1024,1152]{1,0:T(8,128)(2,1)} %get-tuple-element.51, bf16[1,1024,768]{2,1,0:T(8,128)(2,1)S(1)} %copy-done.14), kind=kOutput, calls=%fused_computation.4 | convolution fusion | flops 1812824064 | bytes 5701632 | tf_op jit(solution)/shard_map/dot_general | solution.py:132
  125.9 4.2 %convolution_convert_fusion.1 = bf16[768,2304]{1,0:T(8,128)(2,1)S(1)} fusion(bf16[1024,768]{1,0:T(8,128)(2,1)S(1)} %copy-done.18, bf16[1024,2304]{1,0:T(8,128)(2,1)S(1)} %bitcast.119), kind=kOutput, calls=%fused_computation.2 | convolution fusion | flops 3625648128 | bytes 9830400 | tf_op jit(solution)/shard_map/dot_general | solution.py:132
  130.8 2.1 dynamic-slice_bitcast_fusion
  132.9 1.6 copy-done.3
  134.5 19.6 %shard_map.155 = (bf16[1024,384]{1,0:T(8,128)(2,1)}, f32[1152,384]{1,0:T(8,128)}, f32[1152,384]{1,0:T(8,128)}) custom-call(s32[4]{0:T(128)S(1)} %pad_add_fusion.meta_ref, bf16[1024,768]{1,0:T(8,128)(2,1)} %get-tuple-element.43.q_ref, bf16[1024,768]{1,0:T(8,128)(2,1)} %get-tuple-element.58.go_ref, bf16[1152,1536]{1,0:T(8,128)(2,1)} %copy-done.12, ...), custom_call_target="tpu_custom_call" | custom-call | flops 20132659200 | bytes 16646160 | tf_op jit(solution)/shard_map/pallas_call | solution.py:357
  154.0 1.7 convert.26
  156.2 2.2 bitcast_add_fusion
  158.4 1.7 copy-done.5
  160.4 19.4 %shard_map.156 = (bf16[1024,384]{1,0:T(8,128)(2,1)}, f32[1152,384]{1,0:T(8,128)}, f32[1152,384]{1,0:T(8,128)}) custom-call(s32[4]{0:T(128)S(1)} %pad_add_fusion.meta_ref, bf16[1024,768]{1,0:T(8,128)(2,1)} %get-tuple-element.43.q_ref, bf16[1024,768]{1,0:T(8,128)(2,1)} %get-tuple-element.58.go_ref, bf16[1152,1536]{1,0:T(8,128)(2,1)} %copy-done.12, ...), custom_call_target="tpu_custom_call" | custom-call | flops 20132659200 | bytes 16646160 | tf_op jit(solution)/shard_map/pallas_call | solution.py:357
  179.8 1.7 convert.27
  182.0 3.9 %collective-permute-start.8 = (bf16[64,1536]{1,0:T(8,128)(2,1)S(1)}, bf16[64,1536]{1,0:T(8,128)(2,1)S(1)}, u32[]{:S(2)}, u32[]{:S(2)}) collective-permute-start(bf16[64,1536]{1,0:T(8,128)(2,1)S(1)} %pad_maximum_fusion.9), channel_id=1, source_target_pairs={{0,4},{4,8},{8,12},{12,16},{16,20},{20,24},{24,28},{1,5},{5,9},{9,... | collective-permute-start | bytes 589832 | tf_op jit(solution)/shard_map/ppermute | solution.py:34
  187.4 10.7 %collective-permute-done.9 = bf16[1,352,2304]{2,1,0:T(8,128)(2,1)S(1)} collective-permute-done((bf16[1,352,2304]{2,1,0:T(8,128)(2,1)S(1)}, bf16[1,352,2304]{2,1,0:T(8,128)(2,1)S(1)}, u32[]{:S(2)}, u32[]{:S(2)}) %collective-permute-start.9) | collective-permute-done | bytes 1622048 | tf_op jit(solution)/shard_map/ppermute | solution.py:38
  198.4 1.5 collective-permute-start.15
  199.9 12.8 %shard_map.157 = (bf16[1024,2304]{1,0:T(8,128)(2,1)}, bf16[1024,768]{1,0:T(8,128)(2,1)}, f32[1,768]{1,0:T(1,128)S(1)}) custom-call(bf16[1024,768]{1,0:T(8,128)(2,1)} %bitcast.115, f32[1,768]{1,0:T(1,128)S(1)} %get-tuple-element.120.gain_ref, bf16[768,2304]{1,0:T(8,128)(2,1)} %all-gather.4.cloned.1.call-done.w_ref, ...), custom_call_target="tpu_custom_call" | custom-call | flops 10871635968 | bytes 25171968 | tf_op jit(solution)/shard_map/pallas_call | solution.py:357
  212.7 5.5 %collective-permute-done.15 = bf16[176,2304]{1,0:T(8,128)(2,1)S(1)} collective-permute-done((bf16[176,2304]{1,0:T(8,128)(2,1)S(1)}, bf16[176,2304]{1,0:T(8,128)(2,1)S(1)}, u32[]{:S(2)}, u32[]{:S(2)}) %collective-permute-start.15) | collective-permute-done | bytes 811040 | tf_op jit(solution)/shard_map/ppermute | solution.py:38
  218.4 6.5 %convolution_convert_fusion = bf16[768,2304]{1,0:T(8,128)(2,1)S(1)} fusion(bf16[1024,768]{1,0:T(8,128)(2,1)S(1)} %copy-done.17, bf16[1024,2304]{1,0:T(8,128)(2,1)} %get-tuple-element.74), kind=kOutput, calls=%fused_computation.1 | convolution fusion | flops 3625648128 | bytes 9830400 | tf_op jit(solution)/shard_map/dot_general | solution.py:132
  228.0 2.9 collective-permute-done.10
  231.4 1.5 collective-permute-start.23
  232.9 2.2 bitcast_add_fusion.1
  236.1 1.6 collective-permute-start.17
  237.7 4.9 %collective-permute-done.23 = bf16[88,2304]{1,0:T(8,128)(2,1)S(1)} collective-permute-done((bf16[88,2304]{1,0:T(8,128)(2,1)S(1)}, bf16[88,2304]{1,0:T(8,128)(2,1)S(1)}, u32[]{:S(2)}, u32[]{:S(2)}) %collective-permute-start.23) | collective-permute-done | bytes 405536 | tf_op jit(solution)/shard_map/ppermute | solution.py:38
  242.7 2.4 collective-permute-start.24
  245.2 1.5 collective-permute-start.12
  246.7 2.1 collective-permute-done.12
  250.3 2.8 collective-permute-done.13
  253.2 2.5 collective-permute-start.14
  255.6 7.2 %collective-permute-done.14 = f32[2,192]{1,0:T(2,128)S(1)} collective-permute-done((f32[2,192]{1,0:T(2,128)S(1)}, f32[2,192]{1,0:T(2,128)S(1)}, u32[]{:S(2)}, u32[]{:S(2)}) %collective-permute-start.14) | collective-permute-done | bytes 1568 | tf_op jit(solution)/shard_map/ppermute | solution.py:38
  264.8 1.5 collective-permute-start.18
  266.4 7.0 %collective-permute-done.25 = bf16[88,2304]{1,0:T(8,128)(2,1)S(1)} collective-permute-done((bf16[88,2304]{1,0:T(8,128)(2,1)S(1)}, bf16[88,2304]{1,0:T(8,128)(2,1)S(1)}, u32[]{:S(2)}, u32[]{:S(2)}) %collective-permute-start.25) | collective-permute-done | bytes 405536 | tf_op jit(solution)/shard_map/ppermute | solution.py:38
  273.5 1.5 collective-permute-start.26
  275.0 3.0 collective-permute-done.18
  278.7 5.3 %collective-permute-done.19 = bf16[48,2304]{1,0:T(8,128)(2,1)S(1)} collective-permute-done((bf16[48,2304]{1,0:T(8,128)(2,1)S(1)}, bf16[48,2304]{1,0:T(8,128)(2,1)S(1)}, u32[]{:S(2)}, u32[]{:S(2)}) %collective-permute-start.19) | collective-permute-done | bytes 221216 | tf_op jit(solution)/shard_map/ppermute | solution.py:38
  284.2 5.1 %collective-permute-start.20 = (bf16[48,2304]{1,0:T(8,128)(2,1)S(1)}, bf16[48,2304]{1,0:T(8,128)(2,1)S(1)}, u32[]{:S(2)}, u32[]{:S(2)}) collective-permute-start(bf16[48,2304]{1,0:T(8,128)(2,1)S(1)} %dynamic-slice_add_fusion.3), channel_id=1, source_target_pairs={{0,16},{4,20},{8,24},{12,28},{16,0},{20,4},{24,8},{28,12},{1,17},{... | collective-permute-start | bytes 663560 | tf_op jit(solution)/shard_map/ppermute | solution.py:38
  289.3 4.8 %collective-permute-done.26 = bf16[176,2304]{1,0:T(8,128)(2,1)S(1)} collective-permute-done((bf16[176,2304]{1,0:T(8,128)(2,1)S(1)}, bf16[176,2304]{1,0:T(8,128)(2,1)S(1)}, u32[]{:S(2)}, u32[]{:S(2)}) %collective-permute-start.26) | collective-permute-done | bytes 811040 | tf_op jit(solution)/shard_map/ppermute | solution.py:38
  295.3 5.4 %collective-permute-done.21 = bf16[48,2304]{1,0:T(8,128)(2,1)S(1)} collective-permute-done((bf16[48,2304]{1,0:T(8,128)(2,1)S(1)}, bf16[48,2304]{1,0:T(8,128)(2,1)S(1)}, u32[]{:S(2)}, u32[]{:S(2)}) %collective-permute-start.21) | collective-permute-done | bytes 221216 | tf_op jit(solution)/shard_map/ppermute | solution.py:38
  300.8 1.5 collective-permute-start.22
  305.6 4.7 %collective-permute-done.22 = bf16[96,2304]{1,0:T(8,128)(2,1)S(1)} collective-permute-done((bf16[96,2304]{1,0:T(8,128)(2,1)S(1)}, bf16[96,2304]{1,0:T(8,128)(2,1)S(1)}, u32[]{:S(2)}, u32[]{:S(2)}) %collective-permute-start.22) | collective-permute-done | bytes 442400 | tf_op jit(solution)/shard_map/ppermute | solution.py:38
  (153 shorter events, 35.2 us)
Async XLA Ops:
  7.2 35.9 %all-gather.4.cloned.1.call-start = ((), (), s32[]{:S(2)}) async-start(), calls=%async_computation | async-start | bytes 4423680 | tf_op jit(solution)/shard_map/all_gather | solution.py:382
  7.9 84.0 %all-gather.6.cloned.1.call-start = ((), (), s32[]{:S(2)}) async-start(), calls=%async_computation.1 | async-start | bytes 1474560 | tf_op jit(solution)/shard_map/all_gather | solution.py:383
  8.7 83.2 %all-gather.8.cloned.1.call-start = ((), (), s32[]{:S(2)}) async-start(), calls=%async_computation.2 | async-start | bytes 2211840 | tf_op jit(solution)/shard_map/all_gather | solution.py:386
  10.0 5.9 %collective-permute-start = (bf16[1,192,2]{1,2,0:T(2,128)(2,1)S(1)}, bf16[1,192,2]{1,2,0:T(2,128)(2,1)S(1)}, u32[]{:S(2)}, u32[]{:S(2)}) collective-permute-start(bf16[1,192,2]{1,2,0:T(2,128)(2,1)S(1)} %maximum_bitcast_fusion.2), channel_id=1, source_target_pairs={{0,2},{1,3},{2,0},{3,1},{4,6},{5,7},{6,4},{7,5},{8,10},{9,11},{10,... | collective-permute-start | bytes 2312 | tf_op jit(solution)/shard_map/ppermute | solution.py:38
  15.0 28.0 %copy-start.11 = (bf16[192,2304]{1,0:T(8,128)(2,1)S(1)}, bf16[192,2304]{1,0:T(8,128)(2,1)}, u32[]{:S(2)}) copy-start(bf16[192,2304]{1,0:T(8,128)(2,1)} %param.14) | copy-start | bytes 2654212
  15.9 36.3 %copy-start = (f32[1024,128]{1,0:T(8,128)}, f32[1024,128]{1,0:T(8,128)S(1)}, u32[]{:S(2)}) copy-start(f32[1024,128]{1,0:T(8,128)S(1)} %get-tuple-element.108.high_ref) | copy-start | bytes 1572868
  16.0 1.2 collective-permute-start.1
  43.1 28.1 %collective-permute-start.4 = (bf16[1,192,2304]{2,1,0:T(8,128)(2,1)S(1)}, bf16[1,192,2304]{2,1,0:T(8,128)(2,1)S(1)}, u32[]{:S(2)}, u32[]{:S(2)}) collective-permute-start(bf16[1,192,2304]{2,1,0:T(8,128)(2,1)S(1)} %bitcast.107), channel_id=1, source_target_pairs={{0,2},{1,3},{2,0},{3,1},{4,6},{5,7},{6,4},{7,5},{8,10},{9,11},{10,... | collective-permute-start | bytes 2654216 | tf_op jit(solution)/shard_map/ppermute | solution.py:38
  43.4 13.6 %copy-start.13 = (s32[1,2]{1,0:T(1,128)S(1)}, s32[1,2]{1,0:T(1,128)}, u32[]{:S(2)}) copy-start(s32[1,2]{1,0:T(1,128)} %param.16) | copy-start | bytes 28
  53.3 7.9 %collective-permute-start.2 = (bf16[64,1536]{1,0:T(8,128)(2,1)S(1)}, bf16[64,1536]{1,0:T(8,128)(2,1)S(1)}, u32[]{:S(2)}, u32[]{:S(2)}) collective-permute-start(bf16[64,1536]{1,0:T(8,128)(2,1)S(1)} %get-tuple-element.79), channel_id=1, source_target_pairs={{0,4},{4,8},{8,12},{12,16},{16,20},{20,24},{24,28},{1,5},{5,9},{9,... | collective-permute-start | bytes 589832 | tf_op jit(solution)/shard_map/ppermute | solution.py:25
  58.9 14.5 %collective-permute-start.3 = (bf16[64,1536]{1,0:T(8,128)(2,1)S(1)}, bf16[64,1536]{1,0:T(8,128)(2,1)S(1)}, u32[]{:S(2)}, u32[]{:S(2)}) collective-permute-start(bf16[64,1536]{1,0:T(8,128)(2,1)S(1)} %get-tuple-element.78), channel_id=1, source_target_pairs={{4,0},{8,4},{12,8},{16,12},{20,16},{24,20},{28,24},{5,1},{9,5},{13... | collective-permute-start | bytes 589832 | tf_op jit(solution)/shard_map/ppermute | solution.py:26
  71.3 1.9 copy-start.7
  71.5 17.8 %collective-permute-start.5 = (bf16[2,192,2304]{2,1,0:T(8,128)(2,1)S(1)}, bf16[2,192,2304]{2,1,0:T(8,128)(2,1)S(1)}, u32[]{:S(2)}, u32[]{:S(2)}) collective-permute-start(bf16[2,192,2304]{2,1,0:T(8,128)(2,1)S(1)} %maximum_bitcast_fusion), channel_id=1, source_target_pairs={{0,1},{1,0},{2,3},{3,2},{4,5},{5,4},{6,7},{7,6},{8,9},{9,8},{10,11... | collective-permute-start | bytes 5308424 | tf_op jit(solution)/shard_map/ppermute | solution.py:38
  73.4 1.8 copy-start.12
  93.2 25.6 %copy-start.14 = (bf16[1,1024,768]{2,1,0:T(8,128)(2,1)S(1)}, bf16[1,1024,768]{2,1,0:T(8,128)(2,1)}, u32[]{:S(2)}) copy-start(bf16[1,1024,768]{2,1,0:T(8,128)(2,1)} %param.17) | copy-start | bytes 4718596
  118.7 4.0 %copy-start.15 = (bf16[1024,768]{1,0:T(8,128)(2,1)S(1)}, bf16[1024,768]{1,0:T(8,128)(2,1)}, u32[]{:S(2)}) copy-start(bf16[1024,768]{1,0:T(8,128)(2,1)} %get-tuple-element.45.att_ref) | copy-start | bytes 4718596
  118.8 4.0 %copy-start.16 = (bf16[1024,768]{1,0:T(8,128)(2,1)S(1)}, bf16[1024,768]{1,0:T(8,128)(2,1)}, u32[]{:S(2)}) copy-start(bf16[1024,768]{1,0:T(8,128)(2,1)} %get-tuple-element.52) | copy-start | bytes 4718596
  122.6 2.2 slice-start
  122.8 2.2 slice-start.1
  130.8 3.7 %copy-start.3 = (bf16[4,352,2304]{2,1,0:T(8,128)(2,1)}, bf16[4,352,2304]{2,1,0:T(8,128)(2,1)S(1)}, u32[]{:S(2)}) copy-start(bf16[4,352,2304]{2,1,0:T(8,128)(2,1)S(1)} %maximum_maximum_fusion) | copy-start | bytes 19464196
  134.5 21.7 %collective-permute-start.6 = (bf16[2,352,2304]{2,1,0:T(8,128)(2,1)}, bf16[2,352,2304]{2,1,0:T(8,128)(2,1)}, u32[]{:S(2)}, u32[]{:S(2)}) collective-permute-start(bf16[2,352,2304]{2,1,0:T(8,128)(2,1)} %dynamic-slice_bitcast_fusion), channel_id=1, source_target_pairs={{0,1},{1,0},{2,3},{3,2},{4,5},{5,4},{6,7},{7,6},{8,9},{9,8},{10,11... | collective-permute-start | bytes 9732104 | tf_op jit(solution)/shard_map/ppermute | solution.py:38
  134.5 21.7 %copy-start.4 = (bf16[4,352,2304]{2,1,0:T(8,128)(2,1)S(1)}, bf16[4,352,2304]{2,1,0:T(8,128)(2,1)}, u32[]{:S(2)}) copy-start(bf16[4,352,2304]{2,1,0:T(8,128)(2,1)} %copy-done.3) | copy-start | bytes 19464196
  154.0 2.0 copy-start.9
  160.2 37.9 %collective-permute-start.9 = (bf16[1,352,2304]{2,1,0:T(8,128)(2,1)S(1)}, bf16[1,352,2304]{2,1,0:T(8,128)(2,1)S(1)}, u32[]{:S(2)}, u32[]{:S(2)}) collective-permute-start(bf16[1,352,2304]{2,1,0:T(8,128)(2,1)S(1)} %constant_dynamic-slice_fusion.8), channel_id=1, source_target_pairs={{0,2},{1,3},{2,0},{3,1},{4,6},{5,7},{6,4},{7,5},{8,10},{9,11},{10,... | collective-permute-start | bytes 4866056 | tf_op jit(solution)/shard_map/ppermute | solution.py:38
  179.8 2.0 copy-start.10
  181.8 16.3 %copy-start.6 = (bf16[2,352,2304]{2,1,0:T(8,128)(2,1)S(1)}, bf16[2,352,2304]{2,1,0:T(8,128)(2,1)}, u32[]{:S(2)}) copy-start(bf16[2,352,2304]{2,1,0:T(8,128)(2,1)} %copy-done.5) | copy-start | bytes 9732100
  182.0 16.3 %collective-permute-start.8 = (bf16[64,1536]{1,0:T(8,128)(2,1)S(1)}, bf16[64,1536]{1,0:T(8,128)(2,1)S(1)}, u32[]{:S(2)}, u32[]{:S(2)}) collective-permute-start(bf16[64,1536]{1,0:T(8,128)(2,1)S(1)} %pad_maximum_fusion.9), channel_id=1, source_target_pairs={{0,4},{4,8},{8,12},{12,16},{16,20},{20,24},{24,28},{1,5},{5,9},{9,... | collective-permute-start | bytes 589832 | tf_op jit(solution)/shard_map/ppermute | solution.py:34
  186.0 14.0 %copy-start.1 = (f32[1024,128]{1,0:T(8,128)S(1)}, f32[1024,128]{1,0:T(8,128)}, u32[]{:S(2)}) copy-start(f32[1024,128]{1,0:T(8,128)} %copy-done) | copy-start | bytes 1572868
  186.0 12.4 %collective-permute-start.7 = (bf16[64,1536]{1,0:T(8,128)(2,1)S(1)}, bf16[64,1536]{1,0:T(8,128)(2,1)S(1)}, u32[]{:S(2)}, u32[]{:S(2)}) collective-permute-start(bf16[64,1536]{1,0:T(8,128)(2,1)S(1)} %pad_maximum_fusion.8), channel_id=1, source_target_pairs={{4,0},{8,4},{12,8},{16,12},{20,16},{24,20},{28,24},{5,1},{9,5},{13... | collective-permute-start | bytes 589832 | tf_op jit(solution)/shard_map/ppermute | solution.py:34
  198.4 19.8 %collective-permute-start.15 = (bf16[176,2304]{1,0:T(8,128)(2,1)S(1)}, bf16[176,2304]{1,0:T(8,128)(2,1)S(1)}, u32[]{:S(2)}, u32[]{:S(2)}) collective-permute-start(bf16[176,2304]{1,0:T(8,128)(2,1)S(1)} %constant_dynamic-slice_fusion.3), channel_id=1, source_target_pairs={{0,4},{4,0},{8,12},{12,8},{16,20},{20,16},{24,28},{28,24},{1,5},{5... | collective-permute-start | bytes 2433032 | tf_op jit(solution)/shard_map/ppermute | solution.py:38
  212.7 5.7 %copy-start.17 = (bf16[1024,768]{1,0:T(8,128)(2,1)S(1)}, bf16[1024,768]{1,0:T(8,128)(2,1)}, u32[]{:S(2)}) copy-start(bf16[1024,768]{1,0:T(8,128)(2,1)} %get-tuple-element.71) | copy-start | bytes 4718596
  224.9 2.3 copy-start.8
  227.2 5.7 %collective-permute-start.16 = (bf16[2,192,2304]{2,1,0:T(8,128)(2,1)}, bf16[2,192,2304]{2,1,0:T(8,128)(2,1)}, u32[]{:S(2)}, u32[]{:S(2)}) collective-permute-start(bf16[2,192,2304]{2,1,0:T(8,128)(2,1)} %dynamic-slice_bitcast_fusion.1), channel_id=1, source_target_pairs={{0,1},{1,0},{2,3},{3,2},{4,5},{5,4},{6,7},{7,6},{8,9},{9,8},{10,11... | collective-permute-start | bytes 5308424 | tf_op jit(solution)/shard_map/ppermute | solution.py:38
  227.4 3.5 %collective-permute-start.10 = (f32[2,2,192]{2,0,1:T(2,128)S(1)}, f32[2,2,192]{2,0,1:T(2,128)S(1)}, u32[]{:S(2)}, u32[]{:S(2)}) collective-permute-start(f32[2,2,192]{2,0,1:T(2,128)S(1)} %bitcast.108), channel_id=1, source_target_pairs={{0,1},{1,0},{2,3},{3,2},{4,5},{5,4},{6,7},{7,6},{8,9},{9,8},{10,11... | collective-permute-start | bytes 9224 | tf_op jit(solution)/shard_map/ppermute | solution.py:38
  230.9 14.3 %collective-permute-start.11 = (f32[1,2,192]{2,0,1:T(1,128)S(1)}, f32[1,2,192]{2,0,1:T(1,128)S(1)}, u32[]{:S(2)}, u32[]{:S(2)}) collective-permute-start(f32[1,2,192]{2,0,1:T(1,128)S(1)} %constant_dynamic-slice_fusion.4), channel_id=1, source_target_pairs={{0,2},{1,3},{2,0},{3,1},{4,6},{5,7},{6,4},{7,5},{8,10},{9,11},{10,... | collective-permute-start | bytes 4616 | tf_op jit(solution)/shard_map/ppermute | solution.py:38
  231.4 11.2 %collective-permute-start.23 = (bf16[88,2304]{1,0:T(8,128)(2,1)S(1)}, bf16[88,2304]{1,0:T(8,128)(2,1)S(1)}, u32[]{:S(2)}, u32[]{:S(2)}) collective-permute-start(bf16[88,2304]{1,0:T(8,128)(2,1)S(1)} %constant_dynamic-slice_fusion), channel_id=1, source_target_pairs={{0,8},{4,12},{8,0},{12,4},{16,24},{20,28},{24,16},{28,20},{1,9},{5... | collective-permute-start | bytes 1216520 | tf_op jit(solution)/shard_map/ppermute | solution.py:38
  236.1 27.4 %collective-permute-start.17 = (bf16[1,192,2304]{2,1,0:T(8,128)(2,1)}, bf16[1,192,2304]{2,1,0:T(8,128)(2,1)}, u32[]{:S(2)}, u32[]{:S(2)}) collective-permute-start(bf16[1,192,2304]{2,1,0:T(8,128)(2,1)} %constant_dynamic-slice_fusion.2), channel_id=1, source_target_pairs={{0,2},{1,3},{2,0},{3,1},{4,6},{5,7},{6,4},{7,5},{8,10},{9,11},{10,... | collective-permute-start | bytes 2654216 | tf_op jit(solution)/shard_map/ppermute | solution.py:38
  242.7 20.1 %collective-permute-start.24 = (bf16[88,2304]{1,0:T(8,128)(2,1)S(1)}, bf16[88,2304]{1,0:T(8,128)(2,1)S(1)}, u32[]{:S(2)}, u32[]{:S(2)}) collective-permute-start(bf16[88,2304]{1,0:T(8,128)(2,1)S(1)} %dynamic-slice_add_fusion.2), channel_id=1, source_target_pairs={{0,16},{4,20},{8,24},{12,28},{16,0},{20,4},{24,8},{28,12},{1,17},{... | collective-permute-start | bytes 1216520 | tf_op jit(solution)/shard_map/ppermute | solution.py:38
  245.2 3.7 %collective-permute-start.12 = (f32[2,192]{1,0:T(2,128)S(1)}, f32[2,192]{1,0:T(2,128)S(1)}, u32[]{:S(2)}, u32[]{:S(2)}) collective-permute-start(f32[2,192]{1,0:T(2,128)S(1)} %bitcast.109), channel_id=1, source_target_pairs={{0,4},{4,0},{8,12},{12,8},{16,20},{20,16},{24,28},{28,24},{1,5},{5... | collective-permute-start | bytes 4616 | tf_op jit(solution)/shard_map/ppermute | solution.py:38
  248.9 4.3 %collective-permute-start.13 = (f32[2,192]{1,0:T(2,128)S(1)}, f32[2,192]{1,0:T(2,128)S(1)}, u32[]{:S(2)}, u32[]{:S(2)}) collective-permute-start(f32[2,192]{1,0:T(2,128)S(1)} %fusion.9), channel_id=1, source_target_pairs={{0,8},{4,12},{8,0},{12,4},{16,24},{20,28},{24,16},{28,20},{1,9},{5... | collective-permute-start | bytes 4616 | tf_op jit(solution)/shard_map/ppermute | solution.py:38
  253.2 9.7 %collective-permute-start.14 = (f32[2,192]{1,0:T(2,128)S(1)}, f32[2,192]{1,0:T(2,128)S(1)}, u32[]{:S(2)}, u32[]{:S(2)}) collective-permute-start(f32[2,192]{1,0:T(2,128)S(1)} %add.110), channel_id=1, source_target_pairs={{0,16},{4,20},{8,24},{12,28},{16,0},{20,4},{24,8},{28,12},{1,17},{... | collective-permute-start | bytes 4616 | tf_op jit(solution)/shard_map/ppermute | solution.py:38
  263.0 10.4 %collective-permute-start.25 = (bf16[88,2304]{1,0:T(8,128)(2,1)S(1)}, bf16[88,2304]{1,0:T(8,128)(2,1)S(1)}, u32[]{:S(2)}, u32[]{:S(2)}) collective-permute-start(bf16[88,2304]{1,0:T(8,128)(2,1)S(1)} %add.123), channel_id=1, source_target_pairs={{0,8},{4,12},{8,0},{12,4},{16,24},{20,28},{24,16},{28,20},{1,9},{5... | collective-permute-start | bytes 1216520 | tf_op jit(solution)/shard_map/ppermute | solution.py:38
  264.8 13.1 %collective-permute-start.18 = (bf16[96,2304]{1,0:T(8,128)(2,1)S(1)}, bf16[96,2304]{1,0:T(8,128)(2,1)S(1)}, u32[]{:S(2)}, u32[]{:S(2)}) collective-permute-start(bf16[96,2304]{1,0:T(8,128)(2,1)S(1)} %dynamic-slice_bitcast_fusion.2), channel_id=1, source_target_pairs={{0,4},{4,0},{8,12},{12,8},{16,20},{20,16},{24,28},{28,24},{1,5},{5... | collective-permute-start | bytes 1327112 | tf_op jit(solution)/shard_map/ppermute | solution.py:38
  273.5 20.6 %collective-permute-start.26 = (bf16[176,2304]{1,0:T(8,128)(2,1)S(1)}, bf16[176,2304]{1,0:T(8,128)(2,1)S(1)}, u32[]{:S(2)}, u32[]{:S(2)}) collective-permute-start(bf16[176,2304]{1,0:T(8,128)(2,1)S(1)} %pad_maximum_fusion.2), channel_id=1, source_target_pairs={{0,4},{4,0},{8,12},{12,8},{16,20},{20,16},{24,28},{28,24},{1,5},{5... | collective-permute-start | bytes 2433032 | tf_op jit(solution)/shard_map/ppermute | solution.py:38
  278.1 6.0 %collective-permute-start.19 = (bf16[48,2304]{1,0:T(8,128)(2,1)S(1)}, bf16[48,2304]{1,0:T(8,128)(2,1)S(1)}, u32[]{:S(2)}, u32[]{:S(2)}) collective-permute-start(bf16[48,2304]{1,0:T(8,128)(2,1)S(1)} %constant_dynamic-slice_fusion.1), channel_id=1, source_target_pairs={{0,8},{4,12},{8,0},{12,4},{16,24},{20,28},{24,16},{28,20},{1,9},{5... | collective-permute-start | bytes 663560 | tf_op jit(solution)/shard_map/ppermute | solution.py:38
  284.2 10.5 %collective-permute-start.20 = (bf16[48,2304]{1,0:T(8,128)(2,1)S(1)}, bf16[48,2304]{1,0:T(8,128)(2,1)S(1)}, u32[]{:S(2)}, u32[]{:S(2)}) collective-permute-start(bf16[48,2304]{1,0:T(8,128)(2,1)S(1)} %dynamic-slice_add_fusion.3), channel_id=1, source_target_pairs={{0,16},{4,20},{8,24},{12,28},{16,0},{20,4},{24,8},{28,12},{1,17},{... | collective-permute-start | bytes 663560 | tf_op jit(solution)/shard_map/ppermute | solution.py:38
  294.7 6.0 %collective-permute-start.21 = (bf16[48,2304]{1,0:T(8,128)(2,1)S(1)}, bf16[48,2304]{1,0:T(8,128)(2,1)S(1)}, u32[]{:S(2)}, u32[]{:S(2)}) collective-permute-start(bf16[48,2304]{1,0:T(8,128)(2,1)S(1)} %add.120), channel_id=1, source_target_pairs={{0,8},{4,12},{8,0},{12,4},{16,24},{20,28},{24,16},{28,20},{1,9},{5... | collective-permute-start | bytes 663560 | tf_op jit(solution)/shard_map/ppermute | solution.py:38
  300.8 9.5 %collective-permute-start.22 = (bf16[96,2304]{1,0:T(8,128)(2,1)S(1)}, bf16[96,2304]{1,0:T(8,128)(2,1)S(1)}, u32[]{:S(2)}, u32[]{:S(2)}) collective-permute-start(bf16[96,2304]{1,0:T(8,128)(2,1)S(1)} %pad_maximum_fusion.7), channel_id=1, source_target_pairs={{0,4},{4,0},{8,12},{12,8},{16,20},{20,16},{24,28},{28,24},{1,5},{5... | collective-permute-start | bytes 1327112 | tf_op jit(solution)/shard_map/ppermute | solution.py:38
  (3 other events, 4.6 us)
Sparse Core Ops, SparseCore 0:
  9.6 33.4 all-gather.3
  44.6 23.8 all-gather.5
  70.1 20.7 all-gather.7
